TPU v7x, 128 devices: a whole 4x4x4 slice. The times are simulated.
128 devices in a mesh: ij: 8 (over z_hi, x), vir: 16 (over y, z_lo, core).
Axes of the slice: x: 4, y: 4, z: 4 (z_hi: 2, z_lo: 2; z = z_hi * 2 + z_lo), core: 2. Of those that a mesh axis runs over, the one named last changes fastest.
Arguments:
- amplitudes: float32 [16384, 32768], P('ij', 'vir'), may hold values from -6 to 6
- integrals: float32 [256, 128, 256], P(('vir', 'ij')), may hold values from -0.03125 to 0.03125
- block_mask: int32 [256, 2], P(('vir', 'ij')), may hold values 0 or 1
- partner: int32 [16384], P(('ij', 'vir')), may hold values from 0 to 16383, as said below
- occ_pair: float32 [16384], P(('ij', 'vir')), may hold values from -4 to -1
- vir_pair: float32 [256], replicated, may hold values from 0.5 to 6
Outputs:
- update: float32 [16384, 256], P(('ij', 'vir'))
Inputs may be any that keep to these rules, and one draw needn't show every extreme that they name: partner is an involution without fixed points: partner[partner[k]] = k and partner[k] != k.
All inputs are finite; a program needn't handle non-finite values. No bound on the sum of `block_mask` on one device may be relied on, other than what follows from the above.
Results may differ from a plain program's by a relative error of at most 0.000078.
Values sent between devices are 32-bit elements; how exact they have to be, the bound alone decides.
No kernel may reach another device: no remote copies, remote signals or barrier semaphores. Data moves between devices by JAX's collectives and lax.ppermute only.
A program may use at most 128 MiB of HBM per device.

v0:
```python
import jax
import jax.numpy as jnp
from jax import lax
from jax.sharding import PartitionSpec as P


def on_device(amplitudes, integrals, block_mask, partner, occ_pair, vir_pair):
    tile_size = integrals.shape[1]
    ab_width = integrals.shape[2]
    tile_slots = ab_width // tile_size
    rows_out = partner.shape[0]
    tile_block = lax.all_gather(integrals, "ij", axis=0, tiled=True)
    block_count = tile_block.shape[0]
    scaled = (
        tile_block.reshape(block_count, tile_size, tile_slots, tile_size)
        * lax.all_gather(block_mask, "ij", axis=0, tiled=True).astype(jnp.float32)[:, None, :, None]
    )
    masked_rows = scaled.reshape(block_count * tile_size, ab_width)
    partial_sum = jnp.dot(
        amplitudes, masked_rows, precision=lax.Precision.HIGHEST, preferred_element_type=jnp.float32
    )
    summed = lax.psum(partial_sum, "vir")
    ladder = lax.dynamic_slice_in_dim(summed, lax.axis_index("vir") * rows_out, rows_out, 0)
    all_rows = lax.all_gather(ladder, ("ij", "vir"), axis=0, tiled=True)
    mirrored = jnp.take(all_rows, partner, axis=0)
    denominator = vir_pair[None, :] - occ_pair[:, None]
    return (ladder - mirrored) / denominator


def solution(mesh):
    in_specs = (
        P("ij", "vir"),
        P(("vir", "ij"), None, None),
        P(("vir", "ij"), None),
        P(("ij", "vir")),
        P(("ij", "vir")),
        P(),
    )
    out_specs = P(("ij", "vir"), None)
    return jax.shard_map(
        on_device, mesh=mesh, in_specs=in_specs, out_specs=out_specs, check_vma=False
    )
```

profile of v0, /device:TPU:0, one launch (start us, length us, event | category | flops | bytes accessed | tf_op | source)
XLA Modules:
  0.0 506.3 jit_solution(16190914200815966905)
XLA Ops:
  6.5 0.0 all-gather.4.cloned.1.call-start
  6.5 0.7 all-gather.4.cloned.1.call-update
  7.3 0.0 all-reduce.2.cloned.1.call-start
  7.3 24.5 %all-gather = s32[8,2,2]{2,1,0:T(2,128)S(1)} all-gather(s32[1,2,2]{2,1,0:T(2,128)} %bitcast.14), channel_id=1, replica_groups=mesh['ij'=8,'vir'=16] {'ij'}, dimensions={0}, use_global_device_ids=true | all-gather | bytes 144 | tf_op jit(solution)/shard_map/all_gather | solution.py:16
  31.8 0.1 copy.22
  31.9 0.1 copy.28
  32.0 35.2 %all-gather.4.cloned.1.call-done = f32[16,128,256]{2,1,0:T(8,128)} async-done(((f32[2,128,256]{2,1,0:T(8,128)}), f32[16,128,256]{2,1,0:T(8,128)}) %all-gather.4.cloned.1.call-update) | async-done | bytes 2097168 | tf_op jit(solution)/shard_map/all_gather | solution.py:12
  67.2 0.0 copy-start
  67.2 0.6 mul.14
  67.8 1.0 copy-done
  68.8 31.0 %convolution_bitcast_fusion = f32[2048,256]{0,1:T(8,128)} fusion(f32[2048,2048]{1,0:T(8,128)} %param.6, f32[2048,256]{1,0:T(8,128)S(1)} %bitcast.12, f32[256,8,2,128]{3,2,1,0:T(2,128)S(1)} %bitcast.11), kind=kOutput, calls=%fused_computation.1 | convolution fusion | flops 12885426176 | bytes 23068672 | tf_op jit(solution)/shard_map/dot_general | solution.py:19
  99.8 0.0 copy-start.3
  99.8 0.0 all-reduce.2.cloned.1.call-update
  99.8 0.0 all-gather.6.cloned.1.call-start
  99.9 122.6 %all-reduce.2.cloned.1.call-done = f32[2048,256]{0,1:T(8,128)} async-done(((f32[2048,256]{0,1:T(8,128)}), f32[2048,256]{0,1:T(8,128)}) %all-reduce.2.cloned.1.call-update) | async-done | bytes 2097168 | tf_op jit(solution)/shard_map/psum | solution.py:22
  222.5 1.6 constant_dynamic-slice_fusion
  224.0 0.0 all-gather.6.cloned.1.call-update
  224.1 0.0 copy-done.3
  224.1 0.0 copy-start.1
  224.1 0.0 copy-start.2
  224.1 249.7 %all-gather.6.cloned.1.call-done = f32[16384,256]{0,1:T(8,128)} async-done(((f32[128,256]{0,1:T(8,128)}), f32[16384,256]{0,1:T(8,128)}) %all-gather.6.cloned.1.call-update) | async-done | bytes 16777232 | tf_op jit(solution)/shard_map/all_gather | solution.py:24
  473.9 17.5 %copy.25 = f32[16384,256]{1,0:T(8,128)} copy(f32[16384,256]{0,1:T(8,128)} %all-gather.6.cloned.1.call-done) | data formatting | bytes 33554432 | tf_op jit(solution)/shard_map/all_gather | solution.py:24
  491.3 6.5 %gather_fusion = f32[128,256]{1,0:T(8,128)S(1)} fusion(f32[16384,256]{1,0:T(8,128)} %copy.25, s32[1024]{0:T(1024)S(1)} %pad_clamp_fusion), kind=kCustom, calls=%fused_computation | custom fusion | bytes 262656 | tf_op jit(solution)/shard_map/jit(_take)/gather | solution.py:25
  497.9 0.1 copy.26
  498.0 0.0 copy-done.1
  498.0 0.0 copy-done.2
  498.0 1.0 subtract_divide_fusion
  499.0 0.8 copy.27
  (4 shorter events, 0.0 us)
Async XLA Ops:
  6.5 60.6 %all-gather.4.cloned.1.call-start = ((), (), s32[]{:S(2)}) async-start(), calls=%async_computation | async-start | bytes 2359296 | tf_op jit(solution)/shard_map/all_gather | solution.py:12
  7.3 215.2 %all-reduce.2.cloned.1.call-start = ((), (), s32[]{:S(2)}) async-start(), calls=%async_computation.1 | async-start | bytes 4194304 | tf_op jit(solution)/shard_map/psum | solution.py:22
  67.2 1.6 copy-start
  99.8 124.3 %copy-start.3 = (s32[128]{0:T(128)S(1)}, s32[128]{0:T(128)}, u32[]{:S(2)}) copy-start(s32[128]{0:T(128)} %param.9) | copy-start | bytes 1540
  99.8 374.1 %all-gather.6.cloned.1.call-start = ((), (), s32[]{:S(2)}) async-start(), calls=%async_computation.2 | async-start | bytes 16908288 | tf_op jit(solution)/shard_map/all_gather | solution.py:24
  224.1 273.8 %copy-start.1 = (f32[256]{0:T(256)S(1)}, f32[256]{0:T(256)}, u32[]{:S(2)}) copy-start(f32[256]{0:T(256)} %param.11) | copy-start | bytes 3076
  224.1 273.8 %copy-start.2 = (f32[128]{0:T(128)S(1)}, f32[128]{0:T(128)}, u32[]{:S(2)}) copy-start(f32[128]{0:T(128)} %param.10) | copy-start | bytes 1540
Sparse Core Ops, SparseCore 0:
  9.7 57.4 all-gather.3
  100.0 122.4 all-reduce.1
  224.2 249.6 all-gather.5
where the time goes:
time: 508 us; the launch traced here: 506 us
  waiting for transfers between devices  408 us (80%)
  matrix products  31 us (6%)
  local copies, waits for them, and re-layouts  28.2 us (6%)
  blocking collectives  24.5 us (5%)
  between operations  13.2 us (3%)
    all_gather x1, waiting for transfers between devices, on_device(): all_rows = lax.all_gather(ladder, ('ij', 'vir'), axis=0, tiled=True)  250 us
    psum x1, waiting for transfers between devices, on_device(): summed = lax.psum(partial_sum, 'vir')  123 us
    all_gather x1, waiting for transfers between devices, on_device(): tile_block = lax.all_gather(integrals, 'ij', axis=0, tiled=True)  35.2 us
    dot_general x1, matrix products, on_device(): jnp.dot(amplitudes, masked_rows, precision=lax.Precision.HIGHEST, preferr...  31 us
    all_gather x1, blocking collectives, on_device(): lax.all_gather(block_mask, 'ij', axis=0, tiled=True).astype(jnp.float32)  24.5 us
    all_gather x1, local copies, waits for them, and re-layouts, on_device(): all_rows = lax.all_gather(ladder, ('ij', 'vir'), axis=0, tiled=True)  17.5 us
  transfers between devices with their start and end apart: 3, of which 3 were waited for; matrix products, arithmetic and copies ran while one was open for 0% of the time, Pallas kernels for 0%

commit v1 on v0

v1 whole, which is shorter than its diff:
```python
import functools

import jax
import jax.numpy as jnp
from jax import lax
from jax.experimental import pallas as pl
from jax.experimental.pallas import tpu as pltpu
from jax.sharding import Mesh
from jax.sharding import PartitionSpec as P

SLOTS = 8
STRIDE = SLOTS + 1


def split_bf16(values):
    high = values.astype(jnp.bfloat16)
    low = (values - high.astype(jnp.float32)).astype(jnp.bfloat16)
    return high, low


def product_kernel(parts, first, *refs):
    _, *refs = refs
    pieces = sum(parts)
    lefts = refs[: len(parts)]
    rights = refs[len(parts) : len(parts) + pieces]
    total_in = None if first else refs[len(parts) + pieces]
    total_out = refs[-1]
    shape = total_out.shape
    rows = shape[1] * shape[2]
    total = None if first else total_in[...].reshape(rows, shape[3])
    at = 0
    for left, count in zip(lefts, parts):
        right = [rights[at + n][...] for n in range(count)]
        at += count
        right = right[0] if count == 1 else jnp.concatenate(right, axis=0)
        right_high, right_low = split_bf16(right)
        left_high, left_low = split_bf16(left[...].reshape(rows, right.shape[0]))
        dot = functools.partial(jnp.dot, preferred_element_type=jnp.float32)
        term = dot(left_high, right_low) + dot(left_low, right_high) + dot(left_high, right_high)
        total = term if total is None else total + term
    total_out[...] = total.reshape(shape)


def add_product(amps, places, groups, total, halves=(0, 1)):
    blocks, _, tile, _ = amps.shape
    width = groups[0][0].shape[-1]
    deep = sum(block.shape[0] for block in groups[0])
    run = 4
    parts = tuple(len(group) for group in groups)
    first = total is None
    half_count = len(halves)
    base = halves[0]

    def left_map(n):
        return lambda h, b, at: (b, at[h + base], 0, at[2 + n])

    in_specs = [pl.BlockSpec((run, None, tile, deep), left_map(n)) for n in range(len(groups))]
    operands = [amps] * len(groups)
    for group in groups:
        for block in group:
            in_specs.append(pl.BlockSpec(block.shape, lambda h, b, at: (0, 0)))
            operands.append(block)
    total_spec = pl.BlockSpec((1, run, tile, width), lambda h, b, at: (h, b, 0, 0))
    shape = (half_count, blocks, tile, width)
    aliases = {}
    if not first:
        in_specs.append(pl.BlockSpec((1, run, tile, width), lambda h, b, at: (h + base, b, 0, 0)))
        operands.append(total)
        if half_count == 2:
            aliases = {len(operands): 0}
    rows = half_count * blocks * tile
    return pl.pallas_call(
        functools.partial(product_kernel, parts, first),
        grid_spec=pltpu.PrefetchScalarGridSpec(
            num_scalar_prefetch=1,
            grid=(half_count, blocks // run),
            in_specs=in_specs,
            out_specs=total_spec,
        ),
        out_shape=jax.ShapeDtypeStruct(shape, jnp.float32),
        input_output_aliases=aliases,
        cost_estimate=pl.CostEstimate(
            flops=6 * rows * deep * width * len(groups),
            bytes_accessed=4 * rows * (deep * len(groups) + width),
            transcendentals=0,
        ),
        compiler_params=pltpu.CompilerParams(vmem_limit_bytes=40 * 2**20),
    )(places, *operands)


def pack_rows(own, place, out):
    half = own.shape[1] // 2
    for k in range(own.shape[0]):
        to = place[k]
        out[to, 0:1, :] = own[k : k + 1, :half]
        out[to, 1:2, :] = own[k : k + 1, half:]


def pack_kernel(place, most, partials, own, out):
    own[...] = jnp.sum(partials[...], axis=0)
    pack_rows(own, place, out)
    mark = jnp.broadcast_to(most[...], (2, most.shape[1]))

    def note(d, _):
        out[d * STRIDE + SLOTS] = mark
        return 0

    lax.fori_loop(0, out.shape[0] // STRIDE, note, 0, unroll=16)


def repack_kernel(place, own, out):
    pack_rows(own, place, out)


def unpack_kernel(place, got, own, scale, out, most, held):
    half = own.shape[1] // 2
    for k in range(own.shape[0]):
        at = place[k]
        held[k : k + 1, :half] = got[at, 0:1, :]
        held[k : k + 1, half:] = got[at, 1:2, :]
    worst = jnp.zeros(most.shape, jnp.float32)
    for d in range(got.shape[0] // STRIDE):
        worst = jnp.maximum(worst, got[d * STRIDE + SLOTS])
    most[...] = worst
    out[...] = (own[...] - held[...]) / scale[...]


def mend_kernel(place, got, own, scale, before, out):
    half = own.shape[1] // 2
    for k in range(own.shape[0]):
        at = place[k]
        row = slice(k, k + 1)
        for part, lanes in enumerate((slice(0, half), slice(half, 2 * half))):
            fresh = (own[row, lanes] - got[jnp.maximum(at, 0), part : part + 1, :]) / scale[row, lanes]
            out[row, lanes] = jnp.where(at >= 0, fresh, before[row, lanes])


SMEM = pl.BlockSpec(memory_space=pltpu.SMEM)
VMEM = pl.BlockSpec(memory_space=pltpu.VMEM)


def on_device(amplitudes, integrals, block_mask, partner, occ_pair, vir_pair):
    tiles, tile, width = integrals.shape
    slots = width // tile
    row_count = partner.shape[0]
    z_size, x_size, y_size, zl_size, core_size = (lax.axis_size(a) for a in ("zh", "x", "y", "zl", "c"))
    device_count = z_size * x_size * y_size * zl_size * core_size
    zh, x, core = lax.axis_index("zh"), lax.axis_index("x"), lax.axis_index("c")

    mask = jnp.repeat(block_mask.astype(jnp.float32), tile, axis=1)
    mine = (integrals * mask[:, None, :]).reshape(tiles * tile, width)
    cut = tiles * tile // 2

    def shift(block, by):
        return lax.ppermute(block, "x", [(n, (n + by) % x_size) for n in range(x_size)])

    up1 = shift(mine, 1)
    down1 = shift(mine, -1)
    across = lax.ppermute(mine, "zh", [(0, 1), (1, 0)])
    up2 = shift(up1[:cut], 1)
    down2 = shift(down1[cut:], -1)
    across_up1 = shift(across, 1)
    across_down1 = shift(across, -1)
    across_up2 = shift(across_up1[:cut], 1)
    across_down2 = shift(across_down1[cut:], -1)

    here, there = zh * x_size, (1 - zh) * x_size
    left, right, far = (x + x_size - 1) % x_size, (x + 1) % x_size, (x + 2) % x_size
    amps = amplitudes.reshape(y_size * zl_size, core_size, row_count, amplitudes.shape[1])

    def places(*columns):
        return jnp.stack([1 - core, core, *columns]).astype(jnp.int32)

    total = add_product(amps, places(here + x), [[mine]], None)
    total = add_product(
        amps,
        places(here + left, here + right, there + x),
        [[up1], [down1], [across]],
        total,
    )
    total = add_product(
        amps,
        places(here + far, there + left, there + right),
        [[up2, down2], [across_up1], [across_down1]],
        total,
    )
    last = [[across_up2, across_down2]]
    outgoing = add_product(amps, places(there + far), last, total, (0,))
    incoming = lax.ppermute(outgoing, "c", [(0, 1), (1, 0)])
    kept = add_product(amps, places(there + far), last, total, (1,))
    chip_sum = (kept + incoming)[0]
    partials = lax.all_to_all(chip_sum, ("y", "zl"), 0, 0, tiled=True)

    to = partner // row_count
    same = to[:, None] == to[None, :]
    index = jnp.arange(row_count, dtype=jnp.int32)
    send_rank = jnp.sum(same & (index[None, :] < index[:, None]), axis=1, dtype=jnp.int32)
    take_rank = jnp.sum(same & (partner[None, :] < partner[:, None]), axis=1, dtype=jnp.int32)
    longest = jnp.max(send_rank) + 1
    most = jnp.broadcast_to(longest.astype(jnp.float32), (1, width // 2))
    scale = vir_pair[None, :] - occ_pair[:, None]

    def send_place(turn):
        inside = send_rank // SLOTS == turn
        return to * STRIDE + jnp.where(inside, send_rank % SLOTS, SLOTS)

    packed = jax.ShapeDtypeStruct((device_count * STRIDE, 2, width // 2), jnp.float32)
    rows = jax.ShapeDtypeStruct((row_count, width), jnp.float32)
    everyone = ("zh", "x", "y", "zl", "c")
    own, outbox = pl.pallas_call(
        pack_kernel,
        in_specs=[SMEM, VMEM, VMEM],
        out_specs=[VMEM, VMEM],
        out_shape=[rows, packed],
    )(send_place(0), most, partials)
    inbox = lax.all_to_all(outbox, everyone, 0, 0, tiled=True)
    update, worst = pl.pallas_call(
        unpack_kernel,
        in_specs=[SMEM, VMEM, VMEM, VMEM],
        out_specs=[VMEM, VMEM],
        out_shape=[rows, jax.ShapeDtypeStruct((2, width // 2), jnp.float32)],
        scratch_shapes=[pltpu.VMEM((row_count, width), jnp.float32)],
    )(to * STRIDE + take_rank % SLOTS, inbox, own, scale)

    turns = (worst[0, 0].astype(jnp.int32) + SLOTS - 1) // SLOTS

    def more(state):
        return state[0] < turns

    def again(state):
        turn, before = state
        outbox = pl.pallas_call(
            repack_kernel, in_specs=[SMEM, VMEM], out_specs=VMEM, out_shape=packed
        )(send_place(turn), own)
        inbox = lax.all_to_all(outbox, everyone, 0, 0, tiled=True)
        place = jnp.where(take_rank // SLOTS == turn, to * STRIDE + take_rank % SLOTS, -1)
        after = pl.pallas_call(
            mend_kernel, in_specs=[SMEM, VMEM, VMEM, VMEM, VMEM], out_specs=VMEM, out_shape=rows
        )(place, inbox, own, scale, before)
        return turn + 1, after

    return lax.while_loop(more, again, (jnp.int32(1), update))[1]


def solution(mesh):
    fine = Mesh(mesh.devices.reshape(2, 4, 4, 2, 2), ("zh", "x", "y", "zl", "c"))
    ij, vir = ("zh", "x"), ("y", "zl", "c")
    in_specs = (
        P(ij, vir),
        P(vir + ij, None, None),
        P(vir + ij, None),
        P(ij + vir),
        P(ij + vir),
        P(),
    )
    return jax.shard_map(
        on_device, mesh=fine, in_specs=in_specs, out_specs=P(ij + vir, None), check_vma=False
    )
```

time: 508 us -> 102 us (0.20)
  waiting for transfers between devices: 408 us -> 37.6 us
  matrix products: 31 us -> 0 us
  starting transfers between devices: 0.08 us -> 28 us
  Pallas kernels: 0 us -> 25.4 us
  blocking collectives: 24.5 us -> 0 us
  local copies, waits for them, and re-layouts: 28.2 us -> 4.13 us
  between operations: 13.2 us -> 1.57 us
    all_gather x2 -> x0, waiting for transfers between devices: 285 us -> none  [the longest x1 250 us: on_device(): all_rows = lax.all_gather(ladder, ('ij', 'vir'), axis=0, tiled=True)]
    psum x1 -> x0, waiting for transfers between devices: 123 us -> none  [on_device(): summed = lax.psum(partial_sum, 'vir')]
    all_to_all x0 -> x2, waiting for transfers between devices: none -> 34.4 us  [the longest x1 19.6 us: on_device(): inbox = lax.all_to_all(outbox, everyone, 0, 0, tiled=True)]
    dot_general x1 -> x0, matrix products: 31 us -> none  [on_device(): jnp.dot(amplitudes, masked_rows, precision=lax.Precision.HIGHEST, preferr...]
    pallas_call x0 -> x7, Pallas kernels: none -> 25.4 us  [the longest x5 20.8 us: add_product(): pl.pallas_call(functools.partial(product_kernel, parts, first), grid_spec...]
    all_gather x1 -> x0, blocking collectives: 24.5 us -> none  [on_device(): lax.all_gather(block_mask, 'ij', axis=0, tiled=True).astype(jnp.float32)]
    all_gather x2 -> x0, local copies, waits for them, and re-layouts: 17.5 us -> none  [the longest x1 17.5 us: on_device(): all_rows = lax.all_gather(ladder, ('ij', 'vir'), axis=0, tiled=True)]
    ppermute x0 -> x10, starting transfers between devices: none -> 17.3 us  [the longest x8 13.2 us: shift(): lax.ppermute(block, 'x', [(n, (n + by) % x_size) for n in range(x_size)])]
  transfers between devices with their start and end apart: 3 -> 12, of which waited for: 3 -> 4; matrix products, arithmetic and copies ran while one was open for 0% -> 2% of each run, Pallas kernels for 0% -> 18%
where the time goes in v1:
time: 102 us
  waiting for transfers between devices  37.6 us (37%)
  starting transfers between devices  28 us (27%)
  Pallas kernels  25.4 us (25%)
  other arithmetic  5.03 us (5%)
  local copies, waits for them, and re-layouts  4.13 us (4%)
  between operations  1.57 us (2%)
    pallas_call x5, Pallas kernels, add_product(): pl.pallas_call(functools.partial(product_kernel, parts, first), grid_spec...  20.8 us
    all_to_all x1, waiting for transfers between devices, on_device(): inbox = lax.all_to_all(outbox, everyone, 0, 0, tiled=True)  19.6 us
    all_to_all x1, waiting for transfers between devices, on_device(): partials = lax.all_to_all(chip_sum, ('y', 'zl'), 0, 0, tiled=True)  14.8 us
    ppermute x8, starting transfers between devices, shift(): lax.ppermute(block, 'x', [(n, (n + by) % x_size) for n in range(x_size)])  13.2 us
    all_to_all x1, starting transfers between devices, on_device(): inbox = lax.all_to_all(outbox, everyone, 0, 0, tiled=True)  5.51 us
    all_to_all x1, starting transfers between devices, on_device(): partials = lax.all_to_all(chip_sum, ('y', 'zl'), 0, 0, tiled=True)  5.19 us
    ppermute x1, starting transfers between devices, on_device(): across = lax.ppermute(mine, 'zh', [(0, 1), (1, 0)])  4.04 us
    ppermute x1, waiting for transfers between devices, on_device(): across = lax.ppermute(mine, 'zh', [(0, 1), (1, 0)])  3.02 us
  transfers between devices with their start and end apart: 12, of which 4 were waited for; matrix products, arithmetic and copies ran while one was open for 2% of the time, Pallas kernels for 18%

profile of v1, /device:TPU:0, one launch (start us, length us, event | category | flops | bytes accessed | tf_op | source)
XLA Modules:
  0.0 101.8 jit_solution(11718486832653090645)
XLA Ops:
  0.0 0.7 convert_element_type.19
  0.7 0.1 broadcast_bitcast_fusion
  0.8 1.0 broadcast_multiply_fusion
  1.7 4.0 %collective-permute-start = (f32[256,256]{1,0:T(8,128)S(1)}, f32[256,256]{1,0:T(8,128)}, u32[]{:S(2)}, u32[]{:S(2)}) collective-permute-start(f32[256,256]{1,0:T(8,128)S(1)} %bitcast.20), channel_id=1, source_target_pairs={{0,64},{64,0},{1,65},{65,1},{2,66},{66,2},{3,67},{67,3},{4,68},{68... | collective-permute-start | bytes 786440 | tf_op jit(solution)/shard_map/ppermute | solution.py:159
  5.8 1.5 %collective-permute-start.5 = (f32[256,256]{1,0:T(8,128)S(1)}, f32[256,256]{1,0:T(8,128)S(1)}, u32[]{:S(2)}, u32[]{:S(2)}) collective-permute-start(f32[256,256]{1,0:T(8,128)S(1)} %bitcast.21), channel_id=1, source_target_pairs={{0,16},{16,32},{32,48},{48,0},{1,17},{17,33},{33,49},{49,1},{2,18}... | collective-permute-start | bytes 786440 | tf_op jit(solution)/shard_map/ppermute | solution.py:155
  7.3 1.7 %collective-permute-start.7 = (f32[256,256]{1,0:T(8,128)S(1)}, f32[256,256]{1,0:T(8,128)S(1)}, u32[]{:S(2)}, u32[]{:S(2)}) collective-permute-start(f32[256,256]{1,0:T(8,128)S(1)} %bitcast.22), channel_id=1, source_target_pairs={{0,48},{16,0},{32,16},{48,32},{1,49},{17,1},{33,17},{49,33},{2,50}... | collective-permute-start | bytes 786440 | tf_op jit(solution)/shard_map/ppermute | solution.py:155
  9.0 0.1 pad_add_fusion.2.refs_0_
  9.1 0.1 pad_add_fusion.refs_0_
  9.2 3.0 %collective-permute-done.refs_6_ = f32[256,256]{1,0:T(8,128)} collective-permute-done((f32[256,256]{1,0:T(8,128)S(1)}, f32[256,256]{1,0:T(8,128)}, u32[]{:S(2)}, u32[]{:S(2)}) %collective-permute-start) | collective-permute-done | bytes 262176 | tf_op jit(solution)/shard_map/ppermute | solution.py:159
  12.2 1.5 %collective-permute-start.1 = (f32[256,256]{1,0:T(8,128)}, f32[256,256]{1,0:T(8,128)S(1)}, u32[]{:S(2)}, u32[]{:S(2)}) collective-permute-start(f32[256,256]{1,0:T(8,128)} %collective-permute-done.refs_6_), channel_id=1, source_target_pairs={{0,16},{16,32},{32,48},{48,0},{1,17},{17,33},{33,49},{49,1},{2,18}... | collective-permute-start | bytes 786440 | tf_op jit(solution)/shard_map/ppermute | solution.py:155
  13.7 1.7 %collective-permute-start.3 = (f32[256,256]{1,0:T(8,128)}, f32[256,256]{1,0:T(8,128)S(1)}, u32[]{:S(2)}, u32[]{:S(2)}) collective-permute-start(f32[256,256]{1,0:T(8,128)} %collective-permute-done.refs_6_), channel_id=1, source_target_pairs={{0,48},{16,0},{32,16},{48,32},{1,49},{17,1},{33,17},{49,33},{2,50}... | collective-permute-start | bytes 786440 | tf_op jit(solution)/shard_map/ppermute | solution.py:155
  15.4 3.9 %shard_map.64.refs_7_ = f32[2,8,128,256]{3,2,1,0:T(8,128)S(1)} custom-call(s32[3]{0:T(128)S(1)} %pad_add_fusion.2.refs_0_, f32[8,2,128,2048]{3,2,1,0:T(8,128)} %bitcast.24, f32[256,256]{1,0:T(8,128)S(1)} %bitcast.23), custom_call_target="tpu_custom_call" | custom-call | flops 805306368 | bytes 4194304 | tf_op jit(solution)/shard_map/pallas_call | solution.py:72
  19.4 0.1 stack.63.refs_0_
  19.5 0.1 stack.59.refs_0_
  19.5 0.0 collective-permute-done.5.refs_4_
  19.6 0.4 collective-permute-start.6
  19.9 0.0 collective-permute-done.7.refs_5_
  19.9 3.0 %collective-permute-start.8 = (f32[128,256]{1,0:T(8,128)S(1)}, f32[128,256]{1,0:T(8,128)S(1)}, u32[]{:S(2)}, u32[]{:S(2)}) collective-permute-start(f32[128,256]{1,0:T(8,128)S(1)} %slice.23), channel_id=1, source_target_pairs={{0,48},{16,0},{32,16},{48,32},{1,49},{17,1},{33,17},{49,33},{2,50}... | collective-permute-start | bytes 393224 | tf_op jit(solution)/shard_map/ppermute | solution.py:155
  22.9 6.1 %shard_map.65.refs_8_ = f32[2,8,128,256]{3,2,1,0:T(8,128)S(1)} custom-call(s32[5]{0:T(128)S(1)} %stack.63.refs_0_, f32[8,2,128,2048]{3,2,1,0:T(8,128)} %bitcast.25, f32[8,2,128,2048]{3,2,1,0:T(8,128)} %bitcast.26, f32[8,2,128,2048]{3,2,1,0:T(8,128)} %bitcast.27, f32[256,256]{1,0:T(8,128)S(1)} %collective-permute-done.5.refs_4_, ...), custom_call_target="tpu_custom_call", output_to_operand_aliasing={{}: (7, {})} | custom-call | flops 2415919104 | bytes 8388608 | tf_op jit(solution)/shard_map/pallas_call | solution.py:72
  29.0 0.0 collective-permute-done.1.refs_6_
  29.1 0.1 collective-permute-start.2
  29.1 0.0 collective-permute-done.3.refs_7_
  29.2 3.3 %collective-permute-start.4 = (f32[128,256]{1,0:T(8,128)S(1)}, f32[128,256]{1,0:T(8,128)S(1)}, u32[]{:S(2)}, u32[]{:S(2)}) collective-permute-start(f32[128,256]{1,0:T(8,128)S(1)} %slice.21), channel_id=1, source_target_pairs={{0,48},{16,0},{32,16},{48,32},{1,49},{17,1},{33,17},{49,33},{2,50}... | collective-permute-start | bytes 393224 | tf_op jit(solution)/shard_map/ppermute | solution.py:155
  32.5 6.0 %shard_map.66.refs_4_ = f32[2,8,128,256]{3,2,1,0:T(8,128)S(1)} custom-call(s32[5]{0:T(128)S(1)} %stack.59.refs_0_, f32[8,2,128,2048]{3,2,1,0:T(8,128)} %bitcast.28, f32[8,2,128,2048]{3,2,1,0:T(8,128)} %bitcast.29, f32[8,2,128,2048]{3,2,1,0:T(8,128)} %bitcast.30, f32[128,256]{1,0:T(8,128)S(1)} %collective-permute-done.6.refs_4_, ...), custom_call_target="tpu_custom_call", output_to_operand_aliasing={{}: (8, {})} | custom-call | flops 2415919104 | bytes 8388608 | tf_op jit(solution)/shard_map/pallas_call | solution.py:72
  38.5 0.0 collective-permute-done.4.refs_3_
  38.5 2.4 %shard_map.68 = f32[1,8,128,256]{3,2,1,0:T(8,128)S(1)} custom-call(s32[3]{0:T(128)S(1)} %pad_add_fusion.refs_0_, f32[8,2,128,2048]{3,2,1,0:T(8,128)} %bitcast.31, f32[128,256]{1,0:T(8,128)S(1)} %collective-permute-done.2.refs_2_, f32[128,256]{1,0:T(8,128)S(1)} %collective-permute-done.4.refs_3_, f32[2,8,128,256]{3,2,1,0:T(8,128)S(1)} %shard_map.66.refs_4_), custom_call_target="tpu_custom_call" | custom-call | flops 402653184 | bytes 2097152 | tf_op jit(solution)/shard_map/pallas_call | solution.py:72
  40.9 0.1 collective-permute-start.9
  41.0 2.4 %shard_map.67 = f32[1,8,128,256]{3,2,1,0:T(8,128)S(1)} custom-call(s32[3]{0:T(128)S(1)} %pad_add_fusion.refs_0_, f32[8,2,128,2048]{3,2,1,0:T(8,128)} %bitcast.32, f32[128,256]{1,0:T(8,128)S(1)} %collective-permute-done.2.refs_2_, f32[128,256]{1,0:T(8,128)S(1)} %collective-permute-done.4.refs_3_, f32[2,8,128,256]{3,2,1,0:T(8,128)S(1)} %shard_map.66.refs_4_), custom_call_target="tpu_custom_call" | custom-call | flops 402653184 | bytes 2097152 | tf_op jit(solution)/shard_map/pallas_call | solution.py:72
  43.5 0.0 copy-start.6
  43.5 0.2 collective-permute-done.9
  43.7 1.1 %add_bitcast_fusion = f32[8,128,256]{2,1,0:T(8,128)} fusion(f32[1,8,128,256]{3,2,1,0:T(8,128)S(1)} %shard_map.67, f32[1,8,128,256]{3,2,1,0:T(8,128)S(1)} %collective-permute-done.9), kind=kLoop, calls=%fused_computation.16 | loop fusion | flops 262144 | bytes 3145728 | tf_op jit(solution)/shard_map/squeeze | solution.py:191
  44.8 5.2 %all-to-all-start.1 = ((f32[8,128,256]{2,1,0:T(8,128)}), f32[8,128,256]{2,1,0:T(8,128)S(1)}, u32[]{:S(2)}, u32[]{:S(2)}) async-start(f32[8,128,256]{2,1,0:T(8,128)} %add_bitcast_fusion), calls=%async_computation.1 | async-start | bytes 2097152 | tf_op jit(solution)/shard_map/all_to_all | solution.py:192
  50.0 0.0 copy-start.4
  50.0 0.0 copy-start.5
  50.0 0.2 convert_reduce_fusion
  50.2 1.2 %fusion.7 = (s32[128]{0:T(128)S(1)}, s32[]{:T(128)}, s32[128]{0:T(128)}, s32[128]{0:T(128)}, s32[128]{0:T(128)S(1)}, /*index=5*/s32[128]{0:T(128)S(1)}, s32[128]{0:T(128)S(1)}) fusion(s32[128]{0:T(128)S(1)} %get-tuple-element.426, s32[128]{0:T(128)S(1)} %get-tuple-element.422, s32[128]{0:T(128)S(1)} %copy-done.6), kind=kLoop, calls=%fused_computation.45 | loop fusion | flops 6655 | bytes 4612 | tf_op jit(solution)/shard_map/jit(floor_divide)/rem | solution.py:204
  52.1 14.8 %all-to-all-done.1.partials = f32[8,128,256]{2,1,0:T(8,128)S(1)} async-done(((f32[8,128,256]{2,1,0:T(8,128)}), f32[8,128,256]{2,1,0:T(8,128)S(1)}, u32[]{:S(2)}, u32[]{:S(2)}) %all-to-all-start.1) | async-done | bytes 1048608 | tf_op jit(solution)/shard_map/all_to_all | solution.py:192
  66.8 0.5 broadcast_in_dim.10.most
  67.4 0.4 copy-done.2
  67.8 2.5 %shard_map.69 = (f32[128,256]{1,0:T(8,128)S(1)}, f32[1152,2,128]{2,1,0:T(2,128)}) custom-call(s32[128]{0:T(128)} %get-tuple-element.329.place, f32[1,128]{1,0:T(1,128)} %broadcast_in_dim.10.most, f32[8,128,256]{2,1,0:T(8,128)} %copy-done.2), custom_call_target="tpu_custom_call" | custom-call | tf_op jit(solution)/shard_map/pallas_call | solution.py:210
  70.3 5.5 %all-to-all-start.2 = ((f32[1152,2,128]{2,1,0:T(2,128)}), f32[1152,2,128]{2,1,0:T(2,128)S(1)}, u32[]{:S(2)}, u32[]{:S(2)}) async-start(f32[1152,2,128]{2,1,0:T(2,128)} %get-tuple-element.261), calls=%async_computation.2 | async-start | bytes 2359296 | tf_op jit(solution)/shard_map/all_to_all | solution.py:216
  75.8 0.7 broadcast_subtract_fusion.1.scale
  76.6 19.6 %all-to-all-done.2.got = f32[1152,2,128]{2,1,0:T(2,128)S(1)} async-done(((f32[1152,2,128]{2,1,0:T(2,128)}), f32[1152,2,128]{2,1,0:T(2,128)S(1)}, u32[]{:S(2)}, u32[]{:S(2)}) %all-to-all-start.2) | async-done | bytes 1179680 | tf_op jit(solution)/shard_map/all_to_all | solution.py:216
  96.2 1.0 %copy-done.1 = f32[1152,2,128]{2,1,0:T(2,128)} copy-done((f32[1152,2,128]{2,1,0:T(2,128)}, f32[1152,2,128]{2,1,0:T(2,128)S(1)}, u32[]{:S(2)}) %copy-start.1) | copy-done | bytes 1179672
  97.2 2.0 %shard_map.70 = (f32[128,256]{1,0:T(8,128)S(1)}, f32[2,128]{1,0:T(2,128)}) custom-call(s32[128]{0:T(128)} %get-tuple-element.330.place, f32[1152,2,128]{2,1,0:T(2,128)} %copy-done.1, f32[128,256]{1,0:T(8,128)S(1)} %get-tuple-element.428.own, f32[128,256]{1,0:T(8,128)} %broadcast_subtract_fusion.1.scale), custom_call_target="tpu_custom_call" | custom-call | tf_op jit(solution)/shard_map/pallas_call | solution.py:217
  99.2 1.2 %slice.19 = f32[1,1]{1,0:T(1,128)} slice(f32[2,128]{1,0:T(2,128)} %get-tuple-element.264), slice={[0:1], [0:1]} | slice | bytes 8 | tf_op jit(solution)/shard_map/slice | solution.py:225
  101.1 0.0 copy-start.3
  101.1 0.6 copy-done.3
  (15 shorter events, 0.1 us)
Async XLA Ops:
  1.7 10.5 %collective-permute-start = (f32[256,256]{1,0:T(8,128)S(1)}, f32[256,256]{1,0:T(8,128)}, u32[]{:S(2)}, u32[]{:S(2)}) collective-permute-start(f32[256,256]{1,0:T(8,128)S(1)} %bitcast.20), channel_id=1, source_target_pairs={{0,64},{64,0},{1,65},{65,1},{2,66},{66,2},{3,67},{67,3},{4,68},{68... | collective-permute-start | bytes 786440 | tf_op jit(solution)/shard_map/ppermute | solution.py:159
  5.8 13.8 %collective-permute-start.5 = (f32[256,256]{1,0:T(8,128)S(1)}, f32[256,256]{1,0:T(8,128)S(1)}, u32[]{:S(2)}, u32[]{:S(2)}) collective-permute-start(f32[256,256]{1,0:T(8,128)S(1)} %bitcast.21), channel_id=1, source_target_pairs={{0,16},{16,32},{32,48},{48,0},{1,17},{17,33},{33,49},{49,1},{2,18}... | collective-permute-start | bytes 786440 | tf_op jit(solution)/shard_map/ppermute | solution.py:155
  7.3 12.7 %collective-permute-start.7 = (f32[256,256]{1,0:T(8,128)S(1)}, f32[256,256]{1,0:T(8,128)S(1)}, u32[]{:S(2)}, u32[]{:S(2)}) collective-permute-start(f32[256,256]{1,0:T(8,128)S(1)} %bitcast.22), channel_id=1, source_target_pairs={{0,48},{16,0},{32,16},{48,32},{1,49},{17,1},{33,17},{49,33},{2,50}... | collective-permute-start | bytes 786440 | tf_op jit(solution)/shard_map/ppermute | solution.py:155
  12.2 16.8 %collective-permute-start.1 = (f32[256,256]{1,0:T(8,128)}, f32[256,256]{1,0:T(8,128)S(1)}, u32[]{:S(2)}, u32[]{:S(2)}) collective-permute-start(f32[256,256]{1,0:T(8,128)} %collective-permute-done.refs_6_), channel_id=1, source_target_pairs={{0,16},{16,32},{32,48},{48,0},{1,17},{17,33},{33,49},{49,1},{2,18}... | collective-permute-start | bytes 786440 | tf_op jit(solution)/shard_map/ppermute | solution.py:155
  13.7 15.5 %collective-permute-start.3 = (f32[256,256]{1,0:T(8,128)}, f32[256,256]{1,0:T(8,128)S(1)}, u32[]{:S(2)}, u32[]{:S(2)}) collective-permute-start(f32[256,256]{1,0:T(8,128)} %collective-permute-done.refs_6_), channel_id=1, source_target_pairs={{0,48},{16,0},{32,16},{48,32},{1,49},{17,1},{33,17},{49,33},{2,50}... | collective-permute-start | bytes 786440 | tf_op jit(solution)/shard_map/ppermute | solution.py:155
  19.6 12.9 %collective-permute-start.6 = (f32[128,256]{1,0:T(8,128)S(1)}, f32[128,256]{1,0:T(8,128)S(1)}, u32[]{:S(2)}, u32[]{:S(2)}) collective-permute-start(f32[128,256]{1,0:T(8,128)S(1)} %slice.22), channel_id=1, source_target_pairs={{0,16},{16,32},{32,48},{48,0},{1,17},{17,33},{33,49},{49,1},{2,18}... | collective-permute-start | bytes 393224 | tf_op jit(solution)/shard_map/ppermute | solution.py:155
  19.9 12.5 %collective-permute-start.8 = (f32[128,256]{1,0:T(8,128)S(1)}, f32[128,256]{1,0:T(8,128)S(1)}, u32[]{:S(2)}, u32[]{:S(2)}) collective-permute-start(f32[128,256]{1,0:T(8,128)S(1)} %slice.23), channel_id=1, source_target_pairs={{0,48},{16,0},{32,16},{48,32},{1,49},{17,1},{33,17},{49,33},{2,50}... | collective-permute-start | bytes 393224 | tf_op jit(solution)/shard_map/ppermute | solution.py:155
  29.1 9.5 %collective-permute-start.2 = (f32[128,256]{1,0:T(8,128)S(1)}, f32[128,256]{1,0:T(8,128)S(1)}, u32[]{:S(2)}, u32[]{:S(2)}) collective-permute-start(f32[128,256]{1,0:T(8,128)S(1)} %slice.20), channel_id=1, source_target_pairs={{0,16},{16,32},{32,48},{48,0},{1,17},{17,33},{33,49},{49,1},{2,18}... | collective-permute-start | bytes 393224 | tf_op jit(solution)/shard_map/ppermute | solution.py:155
  29.2 9.4 %collective-permute-start.4 = (f32[128,256]{1,0:T(8,128)S(1)}, f32[128,256]{1,0:T(8,128)S(1)}, u32[]{:S(2)}, u32[]{:S(2)}) collective-permute-start(f32[128,256]{1,0:T(8,128)S(1)} %slice.21), channel_id=1, source_target_pairs={{0,48},{16,0},{32,16},{48,32},{1,49},{17,1},{33,17},{49,33},{2,50}... | collective-permute-start | bytes 393224 | tf_op jit(solution)/shard_map/ppermute | solution.py:155
  40.9 2.7 %collective-permute-start.9 = (f32[1,8,128,256]{3,2,1,0:T(8,128)S(1)}, f32[1,8,128,256]{3,2,1,0:T(8,128)S(1)}, u32[]{:S(2)}, u32[]{:S(2)}) collective-permute-start(f32[1,8,128,256]{3,2,1,0:T(8,128)S(1)} %shard_map.68), channel_id=1, source_target_pairs={{0,1},{1,0},{2,3},{3,2},{4,5},{5,4},{6,7},{7,6},{8,9},{9,8},{10,11... | collective-permute-start | bytes 3145736 | tf_op jit(solution)/shard_map/ppermute | solution.py:189
  43.5 6.6 %copy-start.6 = (s32[128]{0:T(128)S(1)}, s32[128]{0:T(128)}, u32[]{:S(2)}) copy-start(s32[128]{0:T(128)} %param.11) | copy-start | bytes 1540
  44.8 22.0 %all-to-all-start.1 = ((f32[8,128,256]{2,1,0:T(8,128)}), f32[8,128,256]{2,1,0:T(8,128)S(1)}, u32[]{:S(2)}, u32[]{:S(2)}) async-start(f32[8,128,256]{2,1,0:T(8,128)} %add_bitcast_fusion), calls=%async_computation.1 | async-start | bytes 2097152 | tf_op jit(solution)/shard_map/all_to_all | solution.py:192
  50.0 25.8 %copy-start.4 = (f32[256]{0:T(256)S(1)}, f32[256]{0:T(256)}, u32[]{:S(2)}) copy-start(f32[256]{0:T(256)} %param.13) | copy-start | bytes 3076
  50.0 25.8 %copy-start.5 = (f32[128]{0:T(128)S(1)}, f32[128]{0:T(128)}, u32[]{:S(2)}) copy-start(f32[128]{0:T(128)} %param.12) | copy-start | bytes 1540
  66.8 1.0 copy-start.2
  70.3 25.9 %all-to-all-start.2 = ((f32[1152,2,128]{2,1,0:T(2,128)}), f32[1152,2,128]{2,1,0:T(2,128)S(1)}, u32[]{:S(2)}, u32[]{:S(2)}) async-start(f32[1152,2,128]{2,1,0:T(2,128)} %get-tuple-element.261), calls=%async_computation.2 | async-start | bytes 2359296 | tf_op jit(solution)/shard_map/all_to_all | solution.py:216
  96.2 1.0 %copy-start.1 = (f32[1152,2,128]{2,1,0:T(2,128)}, f32[1152,2,128]{2,1,0:T(2,128)S(1)}, u32[]{:S(2)}) copy-start(f32[1152,2,128]{2,1,0:T(2,128)S(1)} %all-to-all-done.2.got) | copy-start | bytes 3538948
  101.1 0.7 copy-start.3

commit v2 on v0

v2 whole, which is shorter than its diff:
```python
import functools

import jax
import jax.numpy as jnp
from jax import lax
from jax.experimental import pallas as pl
from jax.experimental.pallas import tpu as pltpu
from jax.sharding import Mesh
from jax.sharding import PartitionSpec as P

SLOTS = 12
STRIDE = SLOTS + 1
STEP = 4
SMEM = pl.BlockSpec(memory_space=pltpu.SMEM)
VMEM = pl.BlockSpec(memory_space=pltpu.VMEM)
HBM = pl.BlockSpec(memory_space=pltpu.HBM)
SMALL = pltpu.CompilerParams(vmem_limit_bytes=12 * 2**20)


def in_vmem(array):
    return pltpu.with_memory_space_constraint(array, pltpu.VMEM)


def in_hbm(array):
    return pltpu.with_memory_space_constraint(array, pltpu.HBM)


def split_bf16(values):
    high = values.astype(jnp.bfloat16)
    low = (values - high.astype(jnp.float32)).astype(jnp.bfloat16)
    return high, low


def product_kernel(halves, count, at, places, left, *refs):
    blocks = refs[:count]
    totals, out = refs[count:]
    deep, width = blocks[0].shape
    runs, tile = left.shape[0] // STEP, left.shape[2]
    right = []
    for block in blocks:
        high, low = split_bf16(block[...])
        right += [low, high, high]
    right = jnp.concatenate(right, axis=0)
    for spot, half in enumerate(halves):
        for run in range(runs):
            rows = slice(run * STEP, (run + 1) * STEP)
            strips = []
            for n in range(count):
                columns = pl.ds(pl.multiple_of(places[at + n] * deep, deep), deep)
                strip = left[rows, places[half], :, columns].reshape(STEP * tile, deep)
                high, low = split_bf16(strip)
                strips += [high, low, high]
            term = jnp.dot(jnp.concatenate(strips, axis=1), right, preferred_element_type=jnp.float32)
            term = term.reshape(STEP, tile, width)
            out[spot, rows] = term + totals[half, rows]


def add_product(amps, places, at, blocks, totals, halves=(0, 1)):
    runs, _, tile, _ = amps.shape
    deep, width = blocks[0].shape
    operands = [places, amps, *(in_vmem(block) for block in blocks), totals]
    rows = len(halves) * runs * tile
    return pl.pallas_call(
        functools.partial(product_kernel, halves, len(blocks), at),
        in_specs=[SMEM] + [VMEM] * (len(operands) - 1),
        out_specs=VMEM,
        out_shape=pltpu.VMEM((len(halves), runs, tile, width), jnp.float32),
        input_output_aliases={len(operands) - 1: 0} if len(halves) == 2 else {},
        cost_estimate=pl.CostEstimate(
            flops=6 * rows * deep * width * len(blocks), bytes_accessed=4 * rows * width, transcendentals=0
        ),
        compiler_params=SMALL,
    )(*operands)


def load_kernel(places, block, far, near, out, arrived):
    deep, width = block.shape
    tile = far.shape[2]
    step = far.shape[0] // arrived.shape[0]
    copies = []
    for n in range(arrived.shape[0]):
        part = pl.ds(n * step, step)
        copies.append(pltpu.make_async_copy(far.at[part], near.at[part], arrived.at[n]))
        copies[-1].start()
    high, low = split_bf16(block[...])
    right = jnp.concatenate([low, high, high], axis=0)
    columns = pl.ds(pl.multiple_of(places[2] * deep, deep), deep)
    for n, copy in enumerate(copies):
        copy.wait()
        rows = slice(n * step, (n + 1) * step)
        strip = jnp.concatenate(
            [near[rows, places[half], :, columns].reshape(step * tile, deep) for half in range(2)]
        )
        high, low = split_bf16(strip)
        term = jnp.dot(
            jnp.concatenate([high, low, high], axis=1), right, preferred_element_type=jnp.float32
        ).reshape(2, step, tile, width)
        out[:, rows] = term


def load_and_start(amps, places, block):
    runs, cores, tile, _ = amps.shape
    deep, width = block.shape
    rows = runs * cores * tile
    return pl.pallas_call(
        load_kernel,
        in_specs=[SMEM, VMEM, HBM],
        out_specs=[VMEM, VMEM],
        out_shape=[
            pltpu.VMEM(amps.shape, jnp.float32),
            pltpu.VMEM((cores, runs, tile, width), jnp.float32),
        ],
        scratch_shapes=[pltpu.SemaphoreType.DMA((4,))],
        cost_estimate=pl.CostEstimate(
            flops=6 * rows * deep * width, bytes_accessed=4 * amps.size, transcendentals=0
        ),
        compiler_params=SMALL,
    )(places, in_vmem(block), in_hbm(amps))


def mask_kernel(mask, block, out, flags, held, arrived):
    copies = [
        pltpu.make_async_copy(mask, flags, arrived.at[0]),
        pltpu.make_async_copy(block, held, arrived.at[1]),
    ]
    for copy in copies:
        copy.start()
    for copy in copies:
        copy.wait()
    tiles, tile, width = block.shape
    for t in range(tiles):
        for a in range(mask.shape[1]):
            lanes = slice(a * tile, (a + 1) * tile)
            out[t * tile : (t + 1) * tile, lanes] = held[t, :, lanes] * flags[t, a].astype(jnp.float32)


def sum_kernel(partials, out):
    out[...] = jnp.sum(partials[...], axis=0)


def pack_kernel(place, most, own, other, out):
    rows = own.shape[0]
    half = own.shape[1] // 2
    for part, source in enumerate((own, other)):
        for k in range(rows):
            to = place[part * rows + k]
            out[to, 0:1, :] = source[k : k + 1, :half]
            out[to, 1:2, :] = source[k : k + 1, half:]
    mark = jnp.full((2, half), most[0].astype(jnp.float32))
    for d in range(out.shape[0] // STRIDE):
        out[d * STRIDE + SLOTS] = mark


def unpack_kernel(place, got, own, scale, out, turns, held):
    half = own.shape[1] // 2
    for k in range(own.shape[0]):
        at = place[k]
        held[k : k + 1, :half] = got[at, 0:1, :]
        held[k : k + 1, half:] = got[at, 1:2, :]
    worst = jnp.zeros((2, half), jnp.float32)
    for d in range(got.shape[0] // STRIDE):
        worst = jnp.maximum(worst, got[d * STRIDE + SLOTS])
    turns[0] = (jnp.max(worst).astype(jnp.int32) + SLOTS - 1) // SLOTS
    out[...] = (own[...] - held[...]) / scale[...]


def mend_kernel(place, got, own, scale, before, out):
    half = own.shape[1] // 2
    for k in range(own.shape[0]):
        at = place[k]
        row = slice(k, k + 1)
        for part, lanes in enumerate((slice(0, half), slice(half, 2 * half))):
            fresh = (own[row, lanes] - got[jnp.maximum(at, 0), part : part + 1, :]) / scale[row, lanes]
            out[row, lanes] = jnp.where(at >= 0, fresh, before[row, lanes])


def on_device(amplitudes, integrals, block_mask, partner, occ_pair, vir_pair):
    tiles, tile, width = integrals.shape
    row_count = partner.shape[0]
    z_size, x_size, y_size, zl_size, core_size = (lax.axis_size(a) for a in ("zh", "x", "y", "zl", "c"))
    device_count = z_size * x_size * y_size * zl_size * core_size
    zh, x, core = lax.axis_index("zh"), lax.axis_index("x"), lax.axis_index("c")

    mine = pl.pallas_call(
        mask_kernel,
        in_specs=[HBM, HBM],
        out_specs=VMEM,
        out_shape=pltpu.VMEM((tiles * tile, width), jnp.float32),
        scratch_shapes=[
            pltpu.SMEM(block_mask.shape, jnp.int32),
            pltpu.VMEM(integrals.shape, jnp.float32),
            pltpu.SemaphoreType.DMA((2,)),
        ],
        compiler_params=SMALL,
    )(in_hbm(block_mask), in_hbm(integrals))

    def shift(block, by):
        return lax.ppermute(block, "x", [(n, (n + by) % x_size) for n in range(x_size)])

    across = lax.ppermute(mine, "zh", [(0, 1), (1, 0)])
    up1 = shift(mine, 1)
    down1 = shift(mine, -1)
    across_down1 = shift(across, -1)
    up2 = shift(up1, 1)
    across_up1 = shift(across, 1)
    across_far = shift(across_down1, -1)

    def swap(array):
        return lax.ppermute(array, "c", [(0, 1), (1, 0)])

    here, there = zh * x_size, (1 - zh) * x_size
    left, right, far = (x + x_size - 1) % x_size, (x + 1) % x_size, (x + 2) % x_size
    amps = amplitudes.reshape(y_size * zl_size, core_size, row_count, amplitudes.shape[1])

    where = [1 - core, core, here + x, there + x, here + left, here + right, there + right]
    where += [here + far, there + left, there + far]
    slot = jnp.arange(len(where), dtype=jnp.int32)
    places = jnp.zeros((len(where),), jnp.int32)
    for n, place in enumerate(where):
        places = jnp.where(slot == n, place.astype(jnp.int32), places)

    amps, total = load_and_start(amps, places, mine)
    total = add_product(amps, places, 3, [across, up1, down1], total)
    total = add_product(amps, places, 6, [across_down1, up2, across_up1], total)
    outgoing = add_product(amps, places, 9, [across_far], total, (0,))
    incoming = swap(outgoing)
    kept = add_product(amps, places, 9, [across_far], total, (1,))
    chip_sum = (kept + incoming)[0]
    partials = lax.all_to_all(chip_sum, ("y", "zl"), 0, 0, tiled=True)

    rows = pltpu.VMEM((row_count, width), jnp.float32)
    own = pl.pallas_call(
        sum_kernel, in_specs=[VMEM], out_specs=VMEM, out_shape=rows, compiler_params=SMALL
    )(in_vmem(partials))
    other = swap(own)

    wanted = jnp.concatenate([partner, swap(partner)])
    to = wanted // row_count
    row = jnp.arange(row_count, dtype=jnp.int32)
    index = jnp.concatenate([core * row_count + row, (1 - core) * row_count + row])
    earlier = (to[:, None] == to[None, :]) & (index[None, :] < index[:, None])
    send_rank = jnp.sum(earlier, axis=1, dtype=jnp.int32)
    most = (jnp.max(send_rank) + 1).reshape(1)
    chip = partner // (row_count * core_size)
    before = (chip[:, None] == chip[None, :]) & (partner[None, :] < partner[:, None])
    take_rank = jnp.sum(before, axis=1, dtype=jnp.int32)
    scale = vir_pair[None, :] - occ_pair[:, None]

    def send_place(turn):
        inside = (send_rank // SLOTS == turn) & (to % core_size == core)
        return to // core_size * STRIDE + jnp.where(inside, send_rank % SLOTS, SLOTS)

    packed = pltpu.VMEM((device_count // core_size * STRIDE, 2, width // 2), jnp.float32)
    chips = ("zh", "x", "y", "zl")

    def exchange(turn):
        outbox = pl.pallas_call(
            pack_kernel,
            in_specs=[SMEM, SMEM, VMEM, VMEM],
            out_specs=VMEM,
            out_shape=packed,
            compiler_params=SMALL,
        )(send_place(turn), most, own, other)
        return in_vmem(lax.all_to_all(outbox, chips, 0, 0, tiled=True))

    update, turns = pl.pallas_call(
        unpack_kernel,
        in_specs=[SMEM, VMEM, VMEM, VMEM],
        out_specs=[VMEM, SMEM],
        out_shape=[rows, pltpu.SMEM((1,), jnp.int32)],
        scratch_shapes=[pltpu.VMEM((row_count, width), jnp.float32)],
        compiler_params=SMALL,
    )(chip * STRIDE + take_rank % SLOTS, exchange(0), own, scale)

    def more(state):
        return state[0] < turns[0]

    def again(state):
        turn, so_far = state
        place = jnp.where(take_rank // SLOTS == turn, chip * STRIDE + take_rank % SLOTS, -1)
        after = pl.pallas_call(
            mend_kernel,
            in_specs=[SMEM, VMEM, VMEM, VMEM, VMEM],
            out_specs=VMEM,
            out_shape=rows,
            compiler_params=SMALL,
        )(place, exchange(turn), own, scale, so_far)
        return turn + 1, after

    return lax.while_loop(more, again, (jnp.int32(1), update))[1]


def solution(mesh):
    fine = Mesh(mesh.devices.reshape(2, 4, 4, 2, 2), ("zh", "x", "y", "zl", "c"))
    ij, vir = ("zh", "x"), ("y", "zl", "c")
    in_specs = (
        P(ij, vir),
        P(vir + ij, None, None),
        P(vir + ij, None),
        P(ij + vir),
        P(ij + vir),
        P(),
    )
    return jax.shard_map(
        on_device, mesh=fine, in_specs=in_specs, out_specs=P(ij + vir, None), check_vma=False
    )
```

time: 508 us -> 88 us (0.17)
  waiting for transfers between devices: 408 us -> 38.1 us
  matrix products: 31 us -> 0 us
  local copies, waits for them, and re-layouts: 28.2 us -> 0.69 us
  starting transfers between devices: 0.08 us -> 26.2 us
  blocking collectives: 24.5 us -> 0 us
  Pallas kernels: 0 us -> 19.5 us
  between operations: 13.2 us -> 0.88 us
    all_gather x2 -> x0, waiting for transfers between devices: 285 us -> none  [the longest x1 250 us: on_device(): all_rows = lax.all_gather(ladder, ('ij', 'vir'), axis=0, tiled=True)]
    psum x1 -> x0, waiting for transfers between devices: 123 us -> none  [on_device(): summed = lax.psum(partial_sum, 'vir')]
    dot_general x1 -> x0, matrix products: 31 us -> none  [on_device(): jnp.dot(amplitudes, masked_rows, precision=lax.Precision.HIGHEST, preferr...]
    all_to_all x0 -> x2, waiting for transfers between devices: none -> 30.7 us  [the longest x1 15.7 us: exchange(): return in_vmem(lax.all_to_all(outbox, chips, 0, 0, tiled=True))]
    all_gather x1 -> x0, blocking collectives: 24.5 us -> none  [on_device(): lax.all_gather(block_mask, 'ij', axis=0, tiled=True).astype(jnp.float32)]
    pallas_call x0 -> x9, Pallas kernels: none -> 19.5 us  [the longest x4 9.02 us: add_product(): pl.pallas_call(functools.partial(product_kernel, halves, len(blocks), at)...]
    all_gather x2 -> x0, local copies, waits for them, and re-layouts: 17.5 us -> none  [the longest x1 17.5 us: on_device(): all_rows = lax.all_gather(ladder, ('ij', 'vir'), axis=0, tiled=True)]
    ppermute x0 -> x10, starting transfers between devices: none -> 13.9 us  [the longest x6 9.65 us: shift(): lax.ppermute(block, 'x', [(n, (n + by) % x_size) for n in range(x_size)])]
  transfers between devices with their start and end apart: 3 -> 12, of which waited for: 3 -> 5; matrix products, arithmetic and copies ran while one was open for 0% -> 1% of each run, Pallas kernels for 0% -> 17%
where the time goes in v2:
time: 88 us; the launch traced here: 87.8 us
  waiting for transfers between devices  38.1 us (43%)
  starting transfers between devices  26.2 us (30%)
  Pallas kernels  19.5 us (22%)
  other arithmetic  2.29 us (3%)
  between operations  0.88 us (1%)
    all_to_all x1, waiting for transfers between devices, exchange(): return in_vmem(lax.all_to_all(outbox, chips, 0, 0, tiled=True))  15.7 us
    all_to_all x1, waiting for transfers between devices, on_device(): partials = lax.all_to_all(chip_sum, ('y', 'zl'), 0, 0, tiled=True)  15 us
    ppermute x6, starting transfers between devices, shift(): lax.ppermute(block, 'x', [(n, (n + by) % x_size) for n in range(x_size)])  9.65 us
    pallas_call x4, Pallas kernels, add_product(): pl.pallas_call(functools.partial(product_kernel, halves, len(blocks), at)...  9.02 us
    all_to_all x1, starting transfers between devices, exchange(): return in_vmem(lax.all_to_all(outbox, chips, 0, 0, tiled=True))  7.09 us
    pallas_call x1, Pallas kernels, load_and_start(): pl.pallas_call(load_kernel, in_specs=[SMEM, VMEM, HBM], out_specs=[VMEM,...  6.98 us
    all_to_all x1, starting transfers between devices, on_device(): partials = lax.all_to_all(chip_sum, ('y', 'zl'), 0, 0, tiled=True)  5.19 us
    ppermute x1, waiting for transfers between devices, on_device(): across = lax.ppermute(mine, 'zh', [(0, 1), (1, 0)])  4.81 us
  transfers between devices with their start and end apart: 12, of which 5 were waited for; matrix products, arithmetic and copies ran while one was open for 1% of the time, Pallas kernels for 17%

profile of v2, /device:TPU:0, one launch (start us, length us, event | category | flops | bytes accessed | tf_op | source)
XLA Modules:
  0.0 87.8 jit_solution(2109954323986073531)
XLA Ops:
  0.0 1.0 %shard_map.64.block = f32[256,256]{1,0:T(8,128)S(1)} custom-call(s32[2,2]{1,0:T(2,128)} %mask.1, f32[2,128,256]{2,1,0:T(8,128)} %block.1), custom_call_target="tpu_custom_call" | custom-call | tf_op jit(solution)/shard_map/pallas_call | solution.py:184
  1.0 4.0 %collective-permute-start.1 = (f32[256,256]{1,0:T(8,128)S(1)}, f32[256,256]{1,0:T(8,128)S(1)}, u32[]{:S(2)}, u32[]{:S(2)}) collective-permute-start(f32[256,256]{1,0:T(8,128)S(1)} %shard_map.64.block), channel_id=1, source_target_pairs={{0,64},{64,0},{1,65},{65,1},{2,66},{66,2},{3,67},{67,3},{4,68},{68... | collective-permute-start | bytes 786440 | tf_op jit(solution)/shard_map/ppermute | solution.py:200
  5.0 1.5 %collective-permute-start.4 = (f32[256,256]{1,0:T(8,128)S(1)}, f32[256,256]{1,0:T(8,128)S(1)}, u32[]{:S(2)}, u32[]{:S(2)}) collective-permute-start(f32[256,256]{1,0:T(8,128)S(1)} %shard_map.64.block), channel_id=1, source_target_pairs={{0,16},{16,32},{32,48},{48,0},{1,17},{17,33},{33,49},{49,1},{2,18}... | collective-permute-start | bytes 786440 | tf_op jit(solution)/shard_map/ppermute | solution.py:198
  6.5 4.8 %collective-permute-done.1.refs_0_ = f32[256,256]{1,0:T(8,128)S(1)} collective-permute-done((f32[256,256]{1,0:T(8,128)S(1)}, f32[256,256]{1,0:T(8,128)S(1)}, u32[]{:S(2)}, u32[]{:S(2)}) %collective-permute-start.1) | collective-permute-done | bytes 262176 | tf_op jit(solution)/shard_map/ppermute | solution.py:200
  11.3 2.8 %collective-permute-start.2 = (f32[256,256]{1,0:T(8,128)S(1)}, f32[256,256]{1,0:T(8,128)S(1)}, u32[]{:S(2)}, u32[]{:S(2)}) collective-permute-start(f32[256,256]{1,0:T(8,128)S(1)} %collective-permute-done.1.refs_0_), channel_id=1, source_target_pairs={{0,48},{16,0},{32,16},{48,32},{1,49},{17,1},{33,17},{49,33},{2,50}... | collective-permute-start | bytes 786440 | tf_op jit(solution)/shard_map/ppermute | solution.py:198
  14.1 0.8 collective-permute-start.7
  14.9 1.3 %collective-permute-start.6 = (f32[256,256]{1,0:T(8,128)S(1)}, f32[256,256]{1,0:T(8,128)S(1)}, u32[]{:S(2)}, u32[]{:S(2)}) collective-permute-start(f32[256,256]{1,0:T(8,128)S(1)} %collective-permute-done.1.refs_0_), channel_id=1, source_target_pairs={{0,16},{16,32},{32,48},{48,0},{1,17},{17,33},{33,49},{49,1},{2,18}... | collective-permute-start | bytes 786440 | tf_op jit(solution)/shard_map/ppermute | solution.py:198
  16.2 0.0 collective-permute-done.4.refs_1_
  16.2 0.1 collective-permute-start.5
  16.3 7.0 %shard_map.65 = (f32[8,2,128,2048]{3,2,1,0:T(8,128)S(1)}, f32[2,8,128,256]{3,2,1,0:T(8,128)S(1)}) custom-call(s32[10]{0:T(128)S(1)} %compare_select_fusion.11.places, f32[256,256]{1,0:T(8,128)S(1)} %shard_map.64.block, f32[8,2,128,2048]{3,2,1,0:T(8,128)} %bitcast.6), custom_call_target="tpu_custom_call" | custom-call | flops 805306368 | bytes 16777216 | tf_op jit(solution)/shard_map/pallas_call | solution.py:105
  23.3 0.0 collective-permute-done.2.refs_0_
  23.3 3.2 %collective-permute-start.3 = (f32[256,256]{1,0:T(8,128)S(1)}, f32[256,256]{1,0:T(8,128)S(1)}, u32[]{:S(2)}, u32[]{:S(2)}) collective-permute-start(f32[256,256]{1,0:T(8,128)S(1)} %collective-permute-done.2.refs_0_), channel_id=1, source_target_pairs={{0,48},{16,0},{32,16},{48,32},{1,49},{17,1},{33,17},{49,33},{2,50}... | collective-permute-start | bytes 786440 | tf_op jit(solution)/shard_map/ppermute | solution.py:198
  26.5 0.0 collective-permute-done.7.refs_2_
  26.5 3.4 %shard_map.66.refs_3_ = f32[2,8,128,256]{3,2,1,0:T(8,128)S(1)} custom-call(s32[10]{0:T(128)S(1)} %compare_select_fusion.11.places, f32[8,2,128,2048]{3,2,1,0:T(8,128)S(1)} %get-tuple-element.343.left, f32[256,256]{1,0:T(8,128)S(1)} %collective-permute-done.1.refs_0_, f32[256,256]{1,0:T(8,128)S(1)} %collective-permute-done.4.refs_1_, ...), custom_call_target="tpu_custom_call", output_to_operand_aliasing={{}: (5, {})} | custom-call | flops 2415919104 | bytes 2097152 | tf_op jit(solution)/shard_map/pallas_call | solution.py:63
  29.9 0.0 collective-permute-done.6.refs_2_
  29.9 0.0 collective-permute-done.5.refs_1_
  29.9 3.4 %shard_map.67.refs_1_ = f32[2,8,128,256]{3,2,1,0:T(8,128)S(1)} custom-call(s32[10]{0:T(128)S(1)} %compare_select_fusion.11.places, f32[8,2,128,2048]{3,2,1,0:T(8,128)S(1)} %get-tuple-element.343.left, f32[256,256]{1,0:T(8,128)S(1)} %collective-permute-done.2.refs_0_, f32[256,256]{1,0:T(8,128)S(1)} %collective-permute-done.5.refs_1_, ...), custom_call_target="tpu_custom_call", output_to_operand_aliasing={{}: (5, {})} | custom-call | flops 2415919104 | bytes 2097152 | tf_op jit(solution)/shard_map/pallas_call | solution.py:63
  33.3 0.0 collective-permute-done.3.refs_0_
  33.3 1.1 %shard_map.69 = f32[1,8,128,256]{3,2,1,0:T(8,128)S(1)} custom-call(s32[10]{0:T(128)S(1)} %compare_select_fusion.11.places, f32[8,2,128,2048]{3,2,1,0:T(8,128)S(1)} %get-tuple-element.343.left, f32[256,256]{1,0:T(8,128)S(1)} %collective-permute-done.3.refs_0_, f32[2,8,128,256]{3,2,1,0:T(8,128)S(1)} %shard_map.67.refs_1_), custom_call_target="tpu_custom_call" | custom-call | flops 402653184 | bytes 1048576 | tf_op jit(solution)/shard_map/pallas_call | solution.py:63
  34.5 0.1 collective-permute-start.8
  34.6 1.1 %shard_map.68 = f32[1,8,128,256]{3,2,1,0:T(8,128)S(1)} custom-call(s32[10]{0:T(128)S(1)} %compare_select_fusion.11.places, f32[8,2,128,2048]{3,2,1,0:T(8,128)S(1)} %get-tuple-element.343.left, f32[256,256]{1,0:T(8,128)S(1)} %collective-permute-done.3.refs_0_, f32[2,8,128,256]{3,2,1,0:T(8,128)S(1)} %shard_map.67.refs_1_), custom_call_target="tpu_custom_call" | custom-call | flops 402653184 | bytes 1048576 | tf_op jit(solution)/shard_map/pallas_call | solution.py:63
  35.7 0.0 copy-start.2
  35.7 1.5 %collective-permute-done.8 = f32[1,8,128,256]{3,2,1,0:T(8,128)S(1)} collective-permute-done((f32[1,8,128,256]{3,2,1,0:T(8,128)S(1)}, f32[1,8,128,256]{3,2,1,0:T(8,128)S(1)}, u32[]{:S(2)}, u32[]{:S(2)}) %collective-permute-start.8) | collective-permute-done | bytes 1048608 | tf_op jit(solution)/shard_map/ppermute | solution.py:209
  37.2 1.1 %add_bitcast_fusion = f32[8,128,256]{2,1,0:T(8,128)} fusion(f32[1,8,128,256]{3,2,1,0:T(8,128)S(1)} %shard_map.68, f32[1,8,128,256]{3,2,1,0:T(8,128)S(1)} %collective-permute-done.8), kind=kLoop, calls=%fused_computation.15 | loop fusion | flops 262144 | bytes 3145728 | tf_op jit(solution)/shard_map/squeeze | solution.py:228
  38.3 5.2 %all-to-all-start.1 = ((f32[8,128,256]{2,1,0:T(8,128)}), f32[8,128,256]{2,1,0:T(8,128)S(1)}, u32[]{:S(2)}, u32[]{:S(2)}) async-start(f32[8,128,256]{2,1,0:T(8,128)} %add_bitcast_fusion), calls=%async_computation.1 | async-start | bytes 2097152 | tf_op jit(solution)/shard_map/all_to_all | solution.py:229
  43.5 0.0 copy-done.2
  43.5 0.0 copy-start
  43.5 0.0 copy-start.1
  43.5 0.1 collective-permute-start
  43.7 1.0 %collective-permute-done = s32[128]{0:T(128)S(1)} collective-permute-done((s32[128]{0:T(128)S(1)}, s32[128]{0:T(128)S(1)}, u32[]{:S(2)}, u32[]{:S(2)}) %collective-permute-start) | collective-permute-done | bytes 544 | tf_op jit(solution)/shard_map/ppermute | solution.py:209
  44.8 0.2 convert_reduce_fusion
  45.0 15.0 %all-to-all-done.1.partials = f32[8,128,256]{2,1,0:T(8,128)S(1)} async-done(((f32[8,128,256]{2,1,0:T(8,128)}), f32[8,128,256]{2,1,0:T(8,128)S(1)}, u32[]{:S(2)}, u32[]{:S(2)}) %all-to-all-start.1) | async-done | bytes 1048608 | tf_op jit(solution)/shard_map/all_to_all | solution.py:229
  60.0 0.1 shard_map.70.own
  60.1 0.1 collective-permute-start.9
  60.2 0.6 fusion.5
  61.5 0.0 collective-permute-done.9.other
  61.5 1.7 %shard_map.71 = f32[832,2,128]{2,1,0:T(2,128)} custom-call(s32[256]{0:T(256)S(1)} %get-tuple-element.425.place, s32[1]{0:T(128)} %bitcast.most, f32[128,256]{1,0:T(8,128)S(1)} %shard_map.70.own, f32[128,256]{1,0:T(8,128)S(1)} %collective-permute-done.9.other), custom_call_target="tpu_custom_call" | custom-call | tf_op jit(solution)/shard_map/pallas_call | solution.py:257
  63.2 7.1 %all-to-all-start.2 = ((f32[832,2,128]{2,1,0:T(2,128)}), f32[832,2,128]{2,1,0:T(2,128)S(1)}, u32[]{:S(2)}, u32[]{:S(2)}) async-start(f32[832,2,128]{2,1,0:T(2,128)} %shard_map.71), calls=%async_computation.2 | async-start | bytes 1703936 | tf_op jit(solution)/shard_map/all_to_all | solution.py:264
  70.3 0.2 convert_reduce_fusion.1
  70.5 0.0 copy-done
  70.5 0.0 copy-done.1
  70.5 0.1 broadcast_subtract_fusion.1.scale
  70.6 15.7 %all-to-all-done.2.got = f32[832,2,128]{2,1,0:T(2,128)S(1)} async-done(((f32[832,2,128]{2,1,0:T(2,128)}), f32[832,2,128]{2,1,0:T(2,128)S(1)}, u32[]{:S(2)}, u32[]{:S(2)}) %all-to-all-start.2) | async-done | bytes 852000 | tf_op jit(solution)/shard_map/all_to_all | solution.py:264
  86.3 0.7 shard_map.72
  87.1 0.7 copy.20
  (9 shorter events, 0.1 us)
Async XLA Ops:
  1.0 10.3 %collective-permute-start.1 = (f32[256,256]{1,0:T(8,128)S(1)}, f32[256,256]{1,0:T(8,128)S(1)}, u32[]{:S(2)}, u32[]{:S(2)}) collective-permute-start(f32[256,256]{1,0:T(8,128)S(1)} %shard_map.64.block), channel_id=1, source_target_pairs={{0,64},{64,0},{1,65},{65,1},{2,66},{66,2},{3,67},{67,3},{4,68},{68... | collective-permute-start | bytes 786440 | tf_op jit(solution)/shard_map/ppermute | solution.py:200
  5.0 11.2 %collective-permute-start.4 = (f32[256,256]{1,0:T(8,128)S(1)}, f32[256,256]{1,0:T(8,128)S(1)}, u32[]{:S(2)}, u32[]{:S(2)}) collective-permute-start(f32[256,256]{1,0:T(8,128)S(1)} %shard_map.64.block), channel_id=1, source_target_pairs={{0,16},{16,32},{32,48},{48,0},{1,17},{17,33},{33,49},{49,1},{2,18}... | collective-permute-start | bytes 786440 | tf_op jit(solution)/shard_map/ppermute | solution.py:198
  11.3 12.0 %collective-permute-start.2 = (f32[256,256]{1,0:T(8,128)S(1)}, f32[256,256]{1,0:T(8,128)S(1)}, u32[]{:S(2)}, u32[]{:S(2)}) collective-permute-start(f32[256,256]{1,0:T(8,128)S(1)} %collective-permute-done.1.refs_0_), channel_id=1, source_target_pairs={{0,48},{16,0},{32,16},{48,32},{1,49},{17,1},{33,17},{49,33},{2,50}... | collective-permute-start | bytes 786440 | tf_op jit(solution)/shard_map/ppermute | solution.py:198
  14.1 12.4 %collective-permute-start.7 = (f32[256,256]{1,0:T(8,128)S(1)}, f32[256,256]{1,0:T(8,128)S(1)}, u32[]{:S(2)}, u32[]{:S(2)}) collective-permute-start(f32[256,256]{1,0:T(8,128)S(1)} %shard_map.64.block), channel_id=1, source_target_pairs={{0,48},{16,0},{32,16},{48,32},{1,49},{17,1},{33,17},{49,33},{2,50}... | collective-permute-start | bytes 786440 | tf_op jit(solution)/shard_map/ppermute | solution.py:198
  14.9 15.0 %collective-permute-start.6 = (f32[256,256]{1,0:T(8,128)S(1)}, f32[256,256]{1,0:T(8,128)S(1)}, u32[]{:S(2)}, u32[]{:S(2)}) collective-permute-start(f32[256,256]{1,0:T(8,128)S(1)} %collective-permute-done.1.refs_0_), channel_id=1, source_target_pairs={{0,16},{16,32},{32,48},{48,0},{1,17},{17,33},{33,49},{49,1},{2,18}... | collective-permute-start | bytes 786440 | tf_op jit(solution)/shard_map/ppermute | solution.py:198
  16.2 13.7 %collective-permute-start.5 = (f32[256,256]{1,0:T(8,128)S(1)}, f32[256,256]{1,0:T(8,128)S(1)}, u32[]{:S(2)}, u32[]{:S(2)}) collective-permute-start(f32[256,256]{1,0:T(8,128)S(1)} %collective-permute-done.4.refs_1_), channel_id=1, source_target_pairs={{0,16},{16,32},{32,48},{48,0},{1,17},{17,33},{33,49},{49,1},{2,18}... | collective-permute-start | bytes 786440 | tf_op jit(solution)/shard_map/ppermute | solution.py:198
  23.3 10.0 %collective-permute-start.3 = (f32[256,256]{1,0:T(8,128)S(1)}, f32[256,256]{1,0:T(8,128)S(1)}, u32[]{:S(2)}, u32[]{:S(2)}) collective-permute-start(f32[256,256]{1,0:T(8,128)S(1)} %collective-permute-done.2.refs_0_), channel_id=1, source_target_pairs={{0,48},{16,0},{32,16},{48,32},{1,49},{17,1},{33,17},{49,33},{2,50}... | collective-permute-start | bytes 786440 | tf_op jit(solution)/shard_map/ppermute | solution.py:198
  34.5 2.7 %collective-permute-start.8 = (f32[1,8,128,256]{3,2,1,0:T(8,128)S(1)}, f32[1,8,128,256]{3,2,1,0:T(8,128)S(1)}, u32[]{:S(2)}, u32[]{:S(2)}) collective-permute-start(f32[1,8,128,256]{3,2,1,0:T(8,128)S(1)} %shard_map.69), channel_id=1, source_target_pairs={{0,1},{1,0},{2,3},{3,2},{4,5},{5,4},{6,7},{7,6},{8,9},{9,8},{10,11... | collective-permute-start | bytes 3145736 | tf_op jit(solution)/shard_map/ppermute | solution.py:209
  35.7 7.8 %copy-start.2 = (s32[128]{0:T(128)S(1)}, s32[128]{0:T(128)}, u32[]{:S(2)}) copy-start(s32[128]{0:T(128)} %param.11) | copy-start | bytes 1540
  38.3 21.7 %all-to-all-start.1 = ((f32[8,128,256]{2,1,0:T(8,128)}), f32[8,128,256]{2,1,0:T(8,128)S(1)}, u32[]{:S(2)}, u32[]{:S(2)}) async-start(f32[8,128,256]{2,1,0:T(8,128)} %add_bitcast_fusion), calls=%async_computation.1 | async-start | bytes 2097152 | tf_op jit(solution)/shard_map/all_to_all | solution.py:229
  43.5 27.0 %copy-start = (f32[256]{0:T(256)S(1)}, f32[256]{0:T(256)}, u32[]{:S(2)}) copy-start(f32[256]{0:T(256)} %param.13) | copy-start | bytes 3076
  43.5 27.0 %copy-start.1 = (f32[128]{0:T(128)S(1)}, f32[128]{0:T(128)}, u32[]{:S(2)}) copy-start(f32[128]{0:T(128)} %param.12) | copy-start | bytes 1540
  43.5 1.2 %collective-permute-start = (s32[128]{0:T(128)S(1)}, s32[128]{0:T(128)S(1)}, u32[]{:S(2)}, u32[]{:S(2)}) collective-permute-start(s32[128]{0:T(128)S(1)} %copy-done.2), channel_id=1, source_target_pairs={{0,1},{1,0},{2,3},{3,2},{4,5},{5,4},{6,7},{7,6},{8,9},{9,8},{10,11... | collective-permute-start | bytes 1544 | tf_op jit(solution)/shard_map/ppermute | solution.py:209
  60.1 1.4 %collective-permute-start.9 = (f32[128,256]{1,0:T(8,128)S(1)}, f32[128,256]{1,0:T(8,128)S(1)}, u32[]{:S(2)}, u32[]{:S(2)}) collective-permute-start(f32[128,256]{1,0:T(8,128)S(1)} %shard_map.70.own), channel_id=1, source_target_pairs={{0,1},{1,0},{2,3},{3,2},{4,5},{5,4},{6,7},{7,6},{8,9},{9,8},{10,11... | collective-permute-start | bytes 393224 | tf_op jit(solution)/shard_map/ppermute | solution.py:209
  63.2 23.1 %all-to-all-start.2 = ((f32[832,2,128]{2,1,0:T(2,128)}), f32[832,2,128]{2,1,0:T(2,128)S(1)}, u32[]{:S(2)}, u32[]{:S(2)}) async-start(f32[832,2,128]{2,1,0:T(2,128)} %shard_map.71), calls=%async_computation.2 | async-start | bytes 1703936 | tf_op jit(solution)/shard_map/all_to_all | solution.py:264

commit v3 on v2

--- a/solution.py
+++ b/solution.py
@@ -10,7 +10,6 @@
 
 SLOTS = 12
 STRIDE = SLOTS + 1
-STEP = 4
 SMEM = pl.BlockSpec(memory_space=pltpu.SMEM)
 VMEM = pl.BlockSpec(memory_space=pltpu.VMEM)
 HBM = pl.BlockSpec(memory_space=pltpu.HBM)
@@ -31,91 +30,101 @@
     return high, low
 
 
-def product_kernel(halves, count, at, places, left, *refs):
-    blocks = refs[:count]
-    totals, out = refs[count:]
-    deep, width = blocks[0].shape
-    runs, tile = left.shape[0] // STEP, left.shape[2]
-    right = []
-    for block in blocks:
-        high, low = split_bf16(block[...])
-        right += [low, high, high]
-    right = jnp.concatenate(right, axis=0)
-    for spot, half in enumerate(halves):
-        for run in range(runs):
-            rows = slice(run * STEP, (run + 1) * STEP)
-            strips = []
-            for n in range(count):
-                columns = pl.ds(pl.multiple_of(places[at + n] * deep, deep), deep)
-                strip = left[rows, places[half], :, columns].reshape(STEP * tile, deep)
-                high, low = split_bf16(strip)
-                strips += [high, low, high]
-            term = jnp.dot(jnp.concatenate(strips, axis=1), right, preferred_element_type=jnp.float32)
-            term = term.reshape(STEP, tile, width)
-            out[spot, rows] = term + totals[half, rows]
-
-
-def add_product(amps, places, at, blocks, totals, halves=(0, 1)):
-    runs, _, tile, _ = amps.shape
-    deep, width = blocks[0].shape
-    operands = [places, amps, *(in_vmem(block) for block in blocks), totals]
-    rows = len(halves) * runs * tile
-    return pl.pallas_call(
-        functools.partial(product_kernel, halves, len(blocks), at),
-        in_specs=[SMEM] + [VMEM] * (len(operands) - 1),
-        out_specs=VMEM,
-        out_shape=pltpu.VMEM((len(halves), runs, tile, width), jnp.float32),
-        input_output_aliases={len(operands) - 1: 0} if len(halves) == 2 else {},
-        cost_estimate=pl.CostEstimate(
-            flops=6 * rows * deep * width * len(blocks), bytes_accessed=4 * rows * width, transcendentals=0
-        ),
-        compiler_params=SMALL,
-    )(*operands)
-
-
-def load_kernel(places, block, far, near, out, arrived):
-    deep, width = block.shape
-    tile = far.shape[2]
+def halves_of(block):
+    high, low = split_bf16(block)
+    return [low, high, high]
+
+
+def strips_of(rows, width):
+    high, low = split_bf16(rows.reshape(-1, width))
+    return [high, low, high]
+
+
+def product(strips, right):
+    return jnp.dot(jnp.concatenate(strips, axis=1), right, preferred_element_type=jnp.float32)
+
+
+def columns_of(place, deep):
+    return pl.ds(pl.multiple_of(place * deep, deep), deep)
+
+
+def bring(far, near, side, arrived):
     step = far.shape[0] // arrived.shape[0]
+    wide = near.shape[3]
     copies = []
     for n in range(arrived.shape[0]):
         part = pl.ds(n * step, step)
-        copies.append(pltpu.make_async_copy(far.at[part], near.at[part], arrived.at[n]))
+        source = far.at[part, :, :, columns_of(side, wide)]
+        copies.append(pltpu.make_async_copy(source, near.at[part], arrived.at[n]))
         copies[-1].start()
-    high, low = split_bf16(block[...])
-    right = jnp.concatenate([low, high, high], axis=0)
-    columns = pl.ds(pl.multiple_of(places[2] * deep, deep), deep)
+    return step, copies
+
+
+def both_cores(near, places, rows, column, deep):
+    columns = columns_of(column, deep)
+    return jnp.concatenate(
+        [near[rows, places[half], :, columns].reshape(-1, deep) for half in range(2)]
+    )
+
+
+def first_kernel(places, block, far, near, out, arrived):
+    deep, width = block.shape
+    step, copies = bring(far, near, places[2], arrived)
+    right = jnp.concatenate(halves_of(block[...]), axis=0)
     for n, copy in enumerate(copies):
         copy.wait()
         rows = slice(n * step, (n + 1) * step)
-        strip = jnp.concatenate(
-            [near[rows, places[half], :, columns].reshape(step * tile, deep) for half in range(2)]
-        )
-        high, low = split_bf16(strip)
-        term = jnp.dot(
-            jnp.concatenate([high, low, high], axis=1), right, preferred_element_type=jnp.float32
-        ).reshape(2, step, tile, width)
-        out[:, rows] = term
-
-
-def load_and_start(amps, places, block):
-    runs, cores, tile, _ = amps.shape
-    deep, width = block.shape
-    rows = runs * cores * tile
+        strips = strips_of(both_cores(near, places, rows, places[4], deep), deep)
+        out[:, rows] = product(strips, right).reshape(2, step, -1, width)
+
+
+def second_kernel(places, here, left, right, across, totals, far, near, out, arrived):
+    deep, width = across.shape
+    step, copies = bring(far, near, places[3], arrived)
+    sides = jnp.concatenate(halves_of(left[...]) + halves_of(right[...]), axis=0)
+    for n in range(len(copies)):
+        rows = slice(n * step, (n + 1) * step)
+        strips = []
+        for column in (places[5], places[6]):
+            strips += strips_of(both_cores(here, places, rows, column, deep), deep)
+        out[:, rows] = totals[:, rows] + product(strips, sides).reshape(2, step, -1, width)
+    beyond = jnp.concatenate(halves_of(across[...]), axis=0)
+    for n, copy in enumerate(copies):
+        copy.wait()
+        rows = slice(n * step, (n + 1) * step)
+        strips = strips_of(both_cores(near, places, rows, places[4], deep), deep)
+        out[:, rows] += product(strips, beyond).reshape(2, step, -1, width)
+
+
+def last_kernel(half, places, here, there, far, across_left, across_right, across_far, totals, out):
+    deep, width = far.shape
+    blocks = (
+        (here, places[7], far),
+        (there, places[5], across_left),
+        (there, places[6], across_right),
+        (there, places[7], across_far),
+    )
+    right = jnp.concatenate(sum((halves_of(block[...]) for _, _, block in blocks), []), axis=0)
+    step = 4
+    for n in range(here.shape[0] // step):
+        rows = slice(n * step, (n + 1) * step)
+        strips = []
+        for near, column, _ in blocks:
+            strips += strips_of(near[rows, places[half], :, columns_of(column, deep)], deep)
+        out[rows] = totals[half, rows] + product(strips, right).reshape(step, -1, width)
+
+
+def call(kernel, operands, specs, results, scratch=(), aliases={}, flops=0):
     return pl.pallas_call(
-        load_kernel,
-        in_specs=[SMEM, VMEM, HBM],
-        out_specs=[VMEM, VMEM],
-        out_shape=[
-            pltpu.VMEM(amps.shape, jnp.float32),
-            pltpu.VMEM((cores, runs, tile, width), jnp.float32),
-        ],
-        scratch_shapes=[pltpu.SemaphoreType.DMA((4,))],
-        cost_estimate=pl.CostEstimate(
-            flops=6 * rows * deep * width, bytes_accessed=4 * amps.size, transcendentals=0
-        ),
+        kernel,
+        in_specs=specs,
+        out_specs=[VMEM] * len(results),
+        out_shape=[pltpu.VMEM(shape, jnp.float32) for shape in results],
+        scratch_shapes=scratch,
+        input_output_aliases=aliases,
+        cost_estimate=pl.CostEstimate(flops=flops, bytes_accessed=2**20, transcendentals=0),
         compiler_params=SMALL,
-    )(places, in_vmem(block), in_hbm(amps))
+    )(*operands)
 
 
 def mask_kernel(mask, block, out, flags, held, arrived):
@@ -134,6 +143,10 @@
             out[t * tile : (t + 1) * tile, lanes] = held[t, :, lanes] * flags[t, a].astype(jnp.float32)
 
 
+def add_kernel(left, right, out):
+    out[...] = left[...] + right[...]
+
+
 def sum_kernel(partials, out):
     out[...] = jnp.sum(partials[...], axis=0)
 
@@ -197,35 +210,66 @@
     def shift(block, by):
         return lax.ppermute(block, "x", [(n, (n + by) % x_size) for n in range(x_size)])
 
-    across = lax.ppermute(mine, "zh", [(0, 1), (1, 0)])
-    up1 = shift(mine, 1)
-    down1 = shift(mine, -1)
-    across_down1 = shift(across, -1)
-    up2 = shift(up1, 1)
-    across_up1 = shift(across, 1)
-    across_far = shift(across_down1, -1)
+    def cross(block):
+        return lax.ppermute(block, "zh", [(0, 1), (1, 0)])
 
     def swap(array):
         return lax.ppermute(array, "c", [(0, 1), (1, 0)])
 
-    here, there = zh * x_size, (1 - zh) * x_size
-    left, right, far = (x + x_size - 1) % x_size, (x + 1) % x_size, (x + 2) % x_size
     amps = amplitudes.reshape(y_size * zl_size, core_size, row_count, amplitudes.shape[1])
 
-    where = [1 - core, core, here + x, there + x, here + left, here + right, there + right]
-    where += [here + far, there + left, there + far]
+    left, right, opposite = (x + x_size - 1) % x_size, (x + 1) % x_size, (x + 2) % x_size
+    where = [1 - core, core, zh, 1 - zh, x, left, right, opposite]
     slot = jnp.arange(len(where), dtype=jnp.int32)
     places = jnp.zeros((len(where),), jnp.int32)
     for n, place in enumerate(where):
         places = jnp.where(slot == n, place.astype(jnp.int32), places)
 
-    amps, total = load_and_start(amps, places, mine)
-    total = add_product(amps, places, 3, [across, up1, down1], total)
-    total = add_product(amps, places, 6, [across_down1, up2, across_up1], total)
-    outgoing = add_product(amps, places, 9, [across_far], total, (0,))
-    incoming = swap(outgoing)
-    kept = add_product(amps, places, 9, [across_far], total, (1,))
-    chip_sum = (kept + incoming)[0]
+    chunks = y_size * zl_size
+    wide = amplitudes.shape[1] // z_size
+    side = (chunks, core_size, row_count, wide)
+    sums = (core_size, chunks, row_count, width)
+    loads = [pltpu.SemaphoreType.DMA((4,))]
+    work = 6 * core_size * chunks * row_count * width * tiles * tile
+
+    across, up1, down1 = cross(mine), shift(mine, 1), shift(mine, -1)
+    around = [(n, (1 - n // x_size) * x_size + (n + 2) % x_size) for n in range(2 * x_size)]
+    across_far = lax.ppermute(mine, ("zh", "x"), around)
+    here, total = call(
+        first_kernel,
+        [places, mine, in_hbm(amps)],
+        [SMEM, VMEM, HBM],
+        [side, sums],
+        loads,
+        flops=work,
+    )
+    across, up1, total = lax.optimization_barrier((across, up1, total))
+    across_down1 = shift(across, -1)
+    up2 = shift(up1, 1)
+    across_up1 = cross(up1)
+    there, total = call(
+        second_kernel,
+        [places, here, in_vmem(up1), in_vmem(down1), in_vmem(across), total, in_hbm(amps)],
+        [SMEM, VMEM, VMEM, VMEM, VMEM, VMEM, HBM],
+        [side, sums],
+        loads,
+        {5: 1},
+        3 * work,
+    )
+    blocks = [in_vmem(block) for block in (up2, across_up1, across_down1, across_far)]
+
+    def finish(half):
+        (out,) = call(
+            functools.partial(last_kernel, half),
+            [places, here, there, *blocks, total],
+            [SMEM] + [VMEM] * 7,
+            [sums[1:]],
+            flops=2 * work,
+        )
+        return out
+
+    incoming = swap(finish(0))
+    (chip_sum,) = call(add_kernel, [finish(1), in_vmem(incoming)], [VMEM, VMEM], [sums[1:]])
     partials = lax.all_to_all(chip_sum, ("y", "zl"), 0, 0, tiled=True)
 
     rows = pltpu.VMEM((row_count, width), jnp.float32)

time: 88 us -> 82.4 us (0.936)
  waiting for transfers between devices: 38.1 us -> 32.7 us
  other arithmetic: 2.29 us -> 1.17 us
    ppermute x1 -> x3, waiting for transfers between devices: 4.81 us -> 0.01 us  [the longest x2 0.01 us: cross(): return lax.ppermute(block, 'zh', [(0, 1), (1, 0)])]
    ppermute x1 -> x3, starting transfers between devices: 4.04 us -> 7.97 us  [the longest x2 6.63 us: cross(): return lax.ppermute(block, 'zh', [(0, 1), (1, 0)])]
    ppermute x6 -> x4, starting transfers between devices: 9.65 us -> 7.15 us  [shift(): lax.ppermute(block, 'x', [(n, (n + by) % x_size) for n in range(x_size)])]
    ppermute x3, waiting for transfers between devices: 2.58 us -> 1.3 us  [swap(): return lax.ppermute(array, 'c', [(0, 1), (1, 0)])]
    squeeze x1 -> x0, other arithmetic: 1.12 us -> none  [on_device(): chip_sum = (kept + incoming)[0]]
  transfers between devices with their start and end apart: 12 -> 12, of which waited for: 5 -> 5; matrix products, arithmetic and copies ran while one was open for 1% -> 1% of each run, Pallas kernels for 17% -> 16%
where the time goes in v3:
time: 82.4 us; the launch traced here: 82.1 us
  waiting for transfers between devices  32.7 us (40%)
  starting transfers between devices  27 us (33%)
  Pallas kernels  19.7 us (24%)
  other arithmetic  1.17 us (1%)
  between operations  0.87 us (1%)
    pallas_call x5, Pallas kernels, call(): pl.pallas_call(kernel, in_specs=specs, out_specs=[VMEM] * len(results), o...  16.2 us
    all_to_all x1, waiting for transfers between devices, exchange(): return in_vmem(lax.all_to_all(outbox, chips, 0, 0, tiled=True))  15.7 us
    all_to_all x1, waiting for transfers between devices, on_device(): partials = lax.all_to_all(chip_sum, ('y', 'zl'), 0, 0, tiled=True)  15.4 us
    ppermute x4, starting transfers between devices, shift(): lax.ppermute(block, 'x', [(n, (n + by) % x_size) for n in range(x_size)])  7.15 us
    all_to_all x1, starting transfers between devices, exchange(): return in_vmem(lax.all_to_all(outbox, chips, 0, 0, tiled=True))  6.68 us
    ppermute x2, starting transfers between devices, cross(): return lax.ppermute(block, 'zh', [(0, 1), (1, 0)])  6.63 us
    all_to_all x1, starting transfers between devices, on_device(): partials = lax.all_to_all(chip_sum, ('y', 'zl'), 0, 0, tiled=True)  4.92 us
    pallas_call x1, Pallas kernels, exchange(): pl.pallas_call(pack_kernel, in_specs=[SMEM, SMEM, VMEM, VMEM], out_specs=...  1.71 us
  transfers between devices with their start and end apart: 12, of which 5 were waited for; matrix products, arithmetic and copies ran while one was open for 1% of the time, Pallas kernels for 16%

profile of v3, /device:TPU:0, one launch (start us, length us, event | category | flops | bytes accessed | tf_op | source)
XLA Modules:
  0.0 82.1 jit_solution(8402861284845464336)
XLA Ops:
  0.0 1.0 %shard_map.64.block = f32[256,256]{1,0:T(8,128)S(1)} custom-call(s32[2,2]{1,0:T(2,128)} %mask.1, f32[2,128,256]{2,1,0:T(8,128)} %block.1), custom_call_target="tpu_custom_call" | custom-call | tf_op jit(solution)/shard_map/pallas_call | solution.py:197
  1.0 4.0 %collective-permute-start.1 = (f32[256,256]{1,0:T(8,128)S(1)}, f32[256,256]{1,0:T(8,128)S(1)}, u32[]{:S(2)}, u32[]{:S(2)}) collective-permute-start(f32[256,256]{1,0:T(8,128)S(1)} %shard_map.64.block), channel_id=1, source_target_pairs={{0,64},{64,0},{1,65},{65,1},{2,66},{66,2},{3,67},{67,3},{4,68},{68... | collective-permute-start | bytes 786440 | tf_op jit(solution)/shard_map/ppermute | solution.py:214
  5.0 1.5 %collective-permute-start.2 = (f32[256,256]{1,0:T(8,128)S(1)}, f32[256,256]{1,0:T(8,128)S(1)}, u32[]{:S(2)}, u32[]{:S(2)}) collective-permute-start(f32[256,256]{1,0:T(8,128)S(1)} %shard_map.64.block), channel_id=1, source_target_pairs={{0,16},{16,32},{32,48},{48,0},{1,17},{17,33},{33,49},{49,1},{2,18}... | collective-permute-start | bytes 786440 | tf_op jit(solution)/shard_map/ppermute | solution.py:211
  6.5 1.7 %collective-permute-start.3 = (f32[256,256]{1,0:T(8,128)S(1)}, f32[256,256]{1,0:T(8,128)S(1)}, u32[]{:S(2)}, u32[]{:S(2)}) collective-permute-start(f32[256,256]{1,0:T(8,128)S(1)} %shard_map.64.block), channel_id=1, source_target_pairs={{0,48},{16,0},{32,16},{48,32},{1,49},{17,1},{33,17},{49,33},{2,50}... | collective-permute-start | bytes 786440 | tf_op jit(solution)/shard_map/ppermute | solution.py:211
  8.3 1.3 %collective-permute-start.7 = (f32[256,256]{1,0:T(8,128)S(1)}, f32[256,256]{1,0:T(8,128)S(1)}, u32[]{:S(2)}, u32[]{:S(2)}) collective-permute-start(f32[256,256]{1,0:T(8,128)S(1)} %shard_map.64.block), channel_id=1, source_target_pairs={{0,96},{16,112},{32,64},{48,80},{64,32},{80,48},{96,0},{112,16},{1... | collective-permute-start | bytes 786440 | tf_op jit(solution)/shard_map/ppermute | solution.py:237
  9.6 4.6 %shard_map.65 = (f32[8,2,128,1024]{3,2,1,0:T(8,128)S(1)}, f32[2,8,128,256]{3,2,1,0:T(8,128)S(1)}) custom-call(s32[8]{0:T(128)S(1)} %compare_select_fusion.9.places, f32[256,256]{1,0:T(8,128)S(1)} %shard_map.64.block, f32[8,2,128,2048]{3,2,1,0:T(8,128)} %bitcast.4), custom_call_target="tpu_custom_call" | custom-call | flops 805306368 | bytes 1048576 | tf_op jit(solution)/shard_map/pallas_call | solution.py:118
  14.2 0.0 collective-permute-done.1.across
  14.2 0.3 collective-permute-done.2.left
  14.5 1.3 %collective-permute-start.4 = (f32[256,256]{1,0:T(8,128)S(1)}, f32[256,256]{1,0:T(8,128)S(1)}, u32[]{:S(2)}, u32[]{:S(2)}) collective-permute-start(f32[256,256]{1,0:T(8,128)S(1)} %collective-permute-done.2.left), channel_id=1, source_target_pairs={{0,16},{16,32},{32,48},{48,0},{1,17},{17,33},{33,49},{49,1},{2,18}... | collective-permute-start | bytes 786440 | tf_op jit(solution)/shard_map/ppermute | solution.py:211
  15.8 2.6 %collective-permute-start.5 = (f32[256,256]{1,0:T(8,128)S(1)}, f32[256,256]{1,0:T(8,128)S(1)}, u32[]{:S(2)}, u32[]{:S(2)}) collective-permute-start(f32[256,256]{1,0:T(8,128)S(1)} %collective-permute-done.2.left), channel_id=1, source_target_pairs={{0,64},{64,0},{1,65},{65,1},{2,66},{66,2},{3,67},{67,3},{4,68},{68... | collective-permute-start | bytes 786440 | tf_op jit(solution)/shard_map/ppermute | solution.py:214
  18.4 2.6 %collective-permute-start.6 = (f32[256,256]{1,0:T(8,128)S(1)}, f32[256,256]{1,0:T(8,128)S(1)}, u32[]{:S(2)}, u32[]{:S(2)}) collective-permute-start(f32[256,256]{1,0:T(8,128)S(1)} %collective-permute-done.1.across), channel_id=1, source_target_pairs={{0,48},{16,0},{32,16},{48,32},{1,49},{17,1},{33,17},{49,33},{2,50}... | collective-permute-start | bytes 786440 | tf_op jit(solution)/shard_map/ppermute | solution.py:211
  21.0 0.0 collective-permute-done.3.right
  21.0 5.7 %shard_map.66 = (f32[8,2,128,1024]{3,2,1,0:T(8,128)S(1)}, f32[2,8,128,256]{3,2,1,0:T(8,128)S(1)}) custom-call(s32[8]{0:T(128)S(1)} %compare_select_fusion.9.places, f32[8,2,128,1024]{3,2,1,0:T(8,128)S(1)} %get-tuple-element.348.here, f32[256,256]{1,0:T(8,128)S(1)} %collective-permute-done.2.left, ...), custom_call_target="tpu_custom_call", output_to_operand_aliasing={{1}: (5, {})} | custom-call | flops 2415919104 | bytes 1048576 | tf_op jit(solution)/shard_map/pallas_call | solution.py:118
  26.8 0.0 collective-permute-done.7.across_far
  26.8 0.0 collective-permute-done.4.far
  26.8 0.0 collective-permute-done.5.across_left
  26.8 0.0 collective-permute-done.6.across_right
  26.8 2.4 %shard_map.68 = f32[8,128,256]{2,1,0:T(8,128)S(1)} custom-call(s32[8]{0:T(128)S(1)} %compare_select_fusion.9.places, f32[8,2,128,1024]{3,2,1,0:T(8,128)S(1)} %get-tuple-element.348.here, f32[8,2,128,1024]{3,2,1,0:T(8,128)S(1)} %get-tuple-element.353.there, f32[256,256]{1,0:T(8,128)S(1)} %collective-permute-done.4.far, ...), custom_call_target="tpu_custom_call" | custom-call | flops 1610612736 | bytes 1048576 | tf_op jit(solution)/shard_map/pallas_call | solution.py:118
  29.2 0.0 copy-start.2
  29.2 0.1 collective-permute-start.8
  29.3 2.4 %shard_map.67.left = f32[8,128,256]{2,1,0:T(8,128)S(1)} custom-call(s32[8]{0:T(128)S(1)} %compare_select_fusion.9.places, f32[8,2,128,1024]{3,2,1,0:T(8,128)S(1)} %get-tuple-element.348.here, f32[8,2,128,1024]{3,2,1,0:T(8,128)S(1)} %get-tuple-element.353.there, f32[256,256]{1,0:T(8,128)S(1)} %collective-permute-done.4.far, ...), custom_call_target="tpu_custom_call" | custom-call | flops 1610612736 | bytes 1048576 | tf_op jit(solution)/shard_map/pallas_call | solution.py:118
  31.7 0.0 copy-start
  31.7 0.0 copy-start.1
  31.8 0.2 collective-permute-done.8.right
  32.0 1.1 %shard_map.69 = f32[8,128,256]{2,1,0:T(8,128)} custom-call(f32[8,128,256]{2,1,0:T(8,128)S(1)} %shard_map.67.left, f32[8,128,256]{2,1,0:T(8,128)S(1)} %collective-permute-done.8.right), custom_call_target="tpu_custom_call" | custom-call | bytes 1048576 | tf_op jit(solution)/shard_map/pallas_call | solution.py:118
  33.0 4.9 %all-to-all-start.1 = ((f32[8,128,256]{2,1,0:T(8,128)}), f32[8,128,256]{2,1,0:T(8,128)S(1)}, u32[]{:S(2)}, u32[]{:S(2)}) async-start(f32[8,128,256]{2,1,0:T(8,128)} %shard_map.69), calls=%async_computation.1 | async-start | bytes 2097152 | tf_op jit(solution)/shard_map/all_to_all | solution.py:273
  38.0 0.0 copy-done.2
  38.0 0.1 collective-permute-start
  38.1 1.0 %collective-permute-done = s32[128]{0:T(128)S(1)} collective-permute-done((s32[128]{0:T(128)S(1)}, s32[128]{0:T(128)S(1)}, u32[]{:S(2)}, u32[]{:S(2)}) %collective-permute-start) | collective-permute-done | bytes 544 | tf_op jit(solution)/shard_map/ppermute | solution.py:217
  39.2 0.2 convert_reduce_fusion
  39.4 15.4 %all-to-all-done.1.partials = f32[8,128,256]{2,1,0:T(8,128)S(1)} async-done(((f32[8,128,256]{2,1,0:T(8,128)}), f32[8,128,256]{2,1,0:T(8,128)S(1)}, u32[]{:S(2)}, u32[]{:S(2)}) %all-to-all-start.1) | async-done | bytes 1048608 | tf_op jit(solution)/shard_map/all_to_all | solution.py:273
  54.8 0.1 shard_map.70.own
  54.9 0.1 collective-permute-start.9
  55.0 0.6 fusion.5
  56.3 0.0 collective-permute-done.9.other
  56.3 1.7 %shard_map.71 = f32[832,2,128]{2,1,0:T(2,128)} custom-call(s32[256]{0:T(256)S(1)} %get-tuple-element.435.place, s32[1]{0:T(128)} %bitcast.most, f32[128,256]{1,0:T(8,128)S(1)} %shard_map.70.own, f32[128,256]{1,0:T(8,128)S(1)} %collective-permute-done.9.other), custom_call_target="tpu_custom_call" | custom-call | tf_op jit(solution)/shard_map/pallas_call | solution.py:301
  58.0 6.7 %all-to-all-start.2 = ((f32[832,2,128]{2,1,0:T(2,128)}), f32[832,2,128]{2,1,0:T(2,128)S(1)}, u32[]{:S(2)}, u32[]{:S(2)}) async-start(f32[832,2,128]{2,1,0:T(2,128)} %shard_map.71), calls=%async_computation.2 | async-start | bytes 1703936 | tf_op jit(solution)/shard_map/all_to_all | solution.py:308
  64.7 0.2 convert_reduce_fusion.1
  64.9 0.0 copy-done
  64.9 0.0 copy-done.1
  64.9 0.1 broadcast_subtract_fusion.1.scale
  65.0 15.7 %all-to-all-done.2.got = f32[832,2,128]{2,1,0:T(2,128)S(1)} async-done(((f32[832,2,128]{2,1,0:T(2,128)}), f32[832,2,128]{2,1,0:T(2,128)S(1)}, u32[]{:S(2)}, u32[]{:S(2)}) %all-to-all-start.2) | async-done | bytes 852000 | tf_op jit(solution)/shard_map/all_to_all | solution.py:308
  80.7 0.7 shard_map.72
  81.5 0.7 copy.18
  (9 shorter events, 0.1 us)
Async XLA Ops:
  1.0 13.2 %collective-permute-start.1 = (f32[256,256]{1,0:T(8,128)S(1)}, f32[256,256]{1,0:T(8,128)S(1)}, u32[]{:S(2)}, u32[]{:S(2)}) collective-permute-start(f32[256,256]{1,0:T(8,128)S(1)} %shard_map.64.block), channel_id=1, source_target_pairs={{0,64},{64,0},{1,65},{65,1},{2,66},{66,2},{3,67},{67,3},{4,68},{68... | collective-permute-start | bytes 786440 | tf_op jit(solution)/shard_map/ppermute | solution.py:214
  5.0 9.5 %collective-permute-start.2 = (f32[256,256]{1,0:T(8,128)S(1)}, f32[256,256]{1,0:T(8,128)S(1)}, u32[]{:S(2)}, u32[]{:S(2)}) collective-permute-start(f32[256,256]{1,0:T(8,128)S(1)} %shard_map.64.block), channel_id=1, source_target_pairs={{0,16},{16,32},{32,48},{48,0},{1,17},{17,33},{33,49},{49,1},{2,18}... | collective-permute-start | bytes 786440 | tf_op jit(solution)/shard_map/ppermute | solution.py:211
  6.5 14.5 %collective-permute-start.3 = (f32[256,256]{1,0:T(8,128)S(1)}, f32[256,256]{1,0:T(8,128)S(1)}, u32[]{:S(2)}, u32[]{:S(2)}) collective-permute-start(f32[256,256]{1,0:T(8,128)S(1)} %shard_map.64.block), channel_id=1, source_target_pairs={{0,48},{16,0},{32,16},{48,32},{1,49},{17,1},{33,17},{49,33},{2,50}... | collective-permute-start | bytes 786440 | tf_op jit(solution)/shard_map/ppermute | solution.py:211
  8.3 18.5 %collective-permute-start.7 = (f32[256,256]{1,0:T(8,128)S(1)}, f32[256,256]{1,0:T(8,128)S(1)}, u32[]{:S(2)}, u32[]{:S(2)}) collective-permute-start(f32[256,256]{1,0:T(8,128)S(1)} %shard_map.64.block), channel_id=1, source_target_pairs={{0,96},{16,112},{32,64},{48,80},{64,32},{80,48},{96,0},{112,16},{1... | collective-permute-start | bytes 786440 | tf_op jit(solution)/shard_map/ppermute | solution.py:237
  14.5 12.3 %collective-permute-start.4 = (f32[256,256]{1,0:T(8,128)S(1)}, f32[256,256]{1,0:T(8,128)S(1)}, u32[]{:S(2)}, u32[]{:S(2)}) collective-permute-start(f32[256,256]{1,0:T(8,128)S(1)} %collective-permute-done.2.left), channel_id=1, source_target_pairs={{0,16},{16,32},{32,48},{48,0},{1,17},{17,33},{33,49},{49,1},{2,18}... | collective-permute-start | bytes 786440 | tf_op jit(solution)/shard_map/ppermute | solution.py:211
  15.8 11.0 %collective-permute-start.5 = (f32[256,256]{1,0:T(8,128)S(1)}, f32[256,256]{1,0:T(8,128)S(1)}, u32[]{:S(2)}, u32[]{:S(2)}) collective-permute-start(f32[256,256]{1,0:T(8,128)S(1)} %collective-permute-done.2.left), channel_id=1, source_target_pairs={{0,64},{64,0},{1,65},{65,1},{2,66},{66,2},{3,67},{67,3},{4,68},{68... | collective-permute-start | bytes 786440 | tf_op jit(solution)/shard_map/ppermute | solution.py:214
  18.4 8.4 %collective-permute-start.6 = (f32[256,256]{1,0:T(8,128)S(1)}, f32[256,256]{1,0:T(8,128)S(1)}, u32[]{:S(2)}, u32[]{:S(2)}) collective-permute-start(f32[256,256]{1,0:T(8,128)S(1)} %collective-permute-done.1.across), channel_id=1, source_target_pairs={{0,48},{16,0},{32,16},{48,32},{1,49},{17,1},{33,17},{49,33},{2,50}... | collective-permute-start | bytes 786440 | tf_op jit(solution)/shard_map/ppermute | solution.py:211
  29.2 8.8 %copy-start.2 = (s32[128]{0:T(128)S(1)}, s32[128]{0:T(128)}, u32[]{:S(2)}) copy-start(s32[128]{0:T(128)} %param.11) | copy-start | bytes 1540
  29.2 2.7 %collective-permute-start.8 = (f32[8,128,256]{2,1,0:T(8,128)S(1)}, f32[8,128,256]{2,1,0:T(8,128)S(1)}, u32[]{:S(2)}, u32[]{:S(2)}) collective-permute-start(f32[8,128,256]{2,1,0:T(8,128)S(1)} %shard_map.68), channel_id=1, source_target_pairs={{0,1},{1,0},{2,3},{3,2},{4,5},{5,4},{6,7},{7,6},{8,9},{9,8},{10,11... | collective-permute-start | bytes 3145736 | tf_op jit(solution)/shard_map/ppermute | solution.py:217
  31.7 33.2 %copy-start = (f32[256]{0:T(256)S(1)}, f32[256]{0:T(256)}, u32[]{:S(2)}) copy-start(f32[256]{0:T(256)} %param.13) | copy-start | bytes 3076
  31.7 33.2 %copy-start.1 = (f32[128]{0:T(128)S(1)}, f32[128]{0:T(128)}, u32[]{:S(2)}) copy-start(f32[128]{0:T(128)} %param.12) | copy-start | bytes 1540
  33.0 21.8 %all-to-all-start.1 = ((f32[8,128,256]{2,1,0:T(8,128)}), f32[8,128,256]{2,1,0:T(8,128)S(1)}, u32[]{:S(2)}, u32[]{:S(2)}) async-start(f32[8,128,256]{2,1,0:T(8,128)} %shard_map.69), calls=%async_computation.1 | async-start | bytes 2097152 | tf_op jit(solution)/shard_map/all_to_all | solution.py:273
  38.0 1.2 %collective-permute-start = (s32[128]{0:T(128)S(1)}, s32[128]{0:T(128)S(1)}, u32[]{:S(2)}, u32[]{:S(2)}) collective-permute-start(s32[128]{0:T(128)S(1)} %copy-done.2), channel_id=1, source_target_pairs={{0,1},{1,0},{2,3},{3,2},{4,5},{5,4},{6,7},{7,6},{8,9},{9,8},{10,11... | collective-permute-start | bytes 1544 | tf_op jit(solution)/shard_map/ppermute | solution.py:217
  54.9 1.4 %collective-permute-start.9 = (f32[128,256]{1,0:T(8,128)S(1)}, f32[128,256]{1,0:T(8,128)S(1)}, u32[]{:S(2)}, u32[]{:S(2)}) collective-permute-start(f32[128,256]{1,0:T(8,128)S(1)} %shard_map.70.own), channel_id=1, source_target_pairs={{0,1},{1,0},{2,3},{3,2},{4,5},{5,4},{6,7},{7,6},{8,9},{9,8},{10,11... | collective-permute-start | bytes 393224 | tf_op jit(solution)/shard_map/ppermute | solution.py:217
  58.0 22.7 %all-to-all-start.2 = ((f32[832,2,128]{2,1,0:T(2,128)}), f32[832,2,128]{2,1,0:T(2,128)S(1)}, u32[]{:S(2)}, u32[]{:S(2)}) async-start(f32[832,2,128]{2,1,0:T(2,128)} %shard_map.71), calls=%async_computation.2 | async-start | bytes 1703936 | tf_op jit(solution)/shard_map/all_to_all | solution.py:308

commit v4 on v3

--- a/solution.py
+++ b/solution.py
@@ -143,20 +143,22 @@
             out[t * tile : (t + 1) * tile, lanes] = held[t, :, lanes] * flags[t, a].astype(jnp.float32)
 
 
-def add_kernel(left, right, out):
-    out[...] = left[...] + right[...]
-
-
-def sum_kernel(partials, out):
-    out[...] = jnp.sum(partials[...], axis=0)
-
-
-def pack_kernel(place, most, own, other, out):
+def add_kernel(places, left, right, *outs):
+    for n, out in enumerate(outs):
+        out[...] = left[places[8 + n]] + right[places[8 + n]]
+
+
+def sum_kernel(*refs):
+    *parts, out = refs
+    out[...] = sum(part[...] for part in parts)
+
+
+def pack_kernel(own_place, other_place, most, own, other, out):
     rows = own.shape[0]
     half = own.shape[1] // 2
-    for part, source in enumerate((own, other)):
+    for place, source in ((own_place, own), (other_place, other)):
         for k in range(rows):
-            to = place[part * rows + k]
+            to = place[k]
             out[to, 0:1, :] = source[k : k + 1, :half]
             out[to, 1:2, :] = source[k : k + 1, half:]
     mark = jnp.full((2, half), most[0].astype(jnp.float32))
@@ -220,6 +222,9 @@
 
     left, right, opposite = (x + x_size - 1) % x_size, (x + 1) % x_size, (x + 2) % x_size
     where = [1 - core, core, zh, 1 - zh, x, left, right, opposite]
+    y, zl = lax.axis_index("y"), lax.axis_index("zl")
+    moves = [(2, 1), (2, 0), (1, 1), (3, 1), (1, 0), (3, 0), (0, 1), (0, 0)]
+    where += [(y + up) % y_size * zl_size + (zl + over) % zl_size for up, over in moves]
     slot = jnp.arange(len(where), dtype=jnp.int32)
     places = jnp.zeros((len(where),), jnp.int32)
     for n, place in enumerate(where):
@@ -269,30 +274,56 @@
         return out
 
     incoming = swap(finish(0))
-    (chip_sum,) = call(add_kernel, [finish(1), in_vmem(incoming)], [VMEM, VMEM], [sums[1:]])
-    partials = lax.all_to_all(chip_sum, ("y", "zl"), 0, 0, tiled=True)
+    parts = call(
+        add_kernel,
+        [places, finish(1), in_vmem(incoming)],
+        [SMEM, VMEM, VMEM],
+        [sums[2:]] * len(moves),
+    )
+
+    *parts, partner, core = lax.optimization_barrier((*parts, partner, core))
+
+    def send(part, move):
+        up, over = move
+        pairs = [
+            (a * zl_size + b, (a + up) % y_size * zl_size + (b + over) % zl_size)
+            for a in range(y_size)
+            for b in range(zl_size)
+        ]
+        return in_vmem(lax.ppermute(part, ("y", "zl"), pairs))
+
+    partials = [send(part, move) for part, move in zip(parts[:-1], moves)] + [parts[-1]]
 
     rows = pltpu.VMEM((row_count, width), jnp.float32)
     own = pl.pallas_call(
-        sum_kernel, in_specs=[VMEM], out_specs=VMEM, out_shape=rows, compiler_params=SMALL
-    )(in_vmem(partials))
+        sum_kernel,
+        in_specs=[VMEM] * len(partials),
+        out_specs=VMEM,
+        out_shape=rows,
+        compiler_params=SMALL,
+    )(*partials)
     other = swap(own)
 
-    wanted = jnp.concatenate([partner, swap(partner)])
-    to = wanted // row_count
+    sibling = swap(partner)
     row = jnp.arange(row_count, dtype=jnp.int32)
-    index = jnp.concatenate([core * row_count + row, (1 - core) * row_count + row])
-    earlier = (to[:, None] == to[None, :]) & (index[None, :] < index[:, None])
-    send_rank = jnp.sum(earlier, axis=1, dtype=jnp.int32)
-    most = (jnp.max(send_rank) + 1).reshape(1)
+
+    def rank(wanted, others, others_first):
+        to, beside = wanted // row_count, others // row_count
+        earlier = (to[:, None] == to[None, :]) & (row[None, :] < row[:, None])
+        also = (to[:, None] == beside[None, :]) & others_first
+        return jnp.sum(earlier.astype(jnp.int32) + also.astype(jnp.int32), axis=1)
+
+    ranks = (rank(partner, sibling, core == 1), rank(sibling, partner, core == 0))
+    most = (jnp.maximum(jnp.max(ranks[0]), jnp.max(ranks[1])) + 1).reshape(1)
     chip = partner // (row_count * core_size)
     before = (chip[:, None] == chip[None, :]) & (partner[None, :] < partner[:, None])
     take_rank = jnp.sum(before, axis=1, dtype=jnp.int32)
     scale = vir_pair[None, :] - occ_pair[:, None]
 
-    def send_place(turn):
-        inside = (send_rank // SLOTS == turn) & (to % core_size == core)
-        return to // core_size * STRIDE + jnp.where(inside, send_rank % SLOTS, SLOTS)
+    def send_place(wanted, rank, turn):
+        to = wanted // row_count
+        inside = (rank // SLOTS == turn) & (to % core_size == core)
+        return to // core_size * STRIDE + jnp.where(inside, rank % SLOTS, SLOTS)
 
     packed = pltpu.VMEM((device_count // core_size * STRIDE, 2, width // 2), jnp.float32)
     chips = ("zh", "x", "y", "zl")
@@ -300,11 +331,11 @@
     def exchange(turn):
         outbox = pl.pallas_call(
             pack_kernel,
-            in_specs=[SMEM, SMEM, VMEM, VMEM],
+            in_specs=[SMEM, SMEM, SMEM, VMEM, VMEM],
             out_specs=VMEM,
             out_shape=packed,
             compiler_params=SMALL,
-        )(send_place(turn), most, own, other)
+        )(send_place(partner, ranks[0], turn), send_place(sibling, ranks[1], turn), most, own, other)
         return in_vmem(lax.all_to_all(outbox, chips, 0, 0, tiled=True))
 
     update, turns = pl.pallas_call(

time: 82.4 us -> 81.2 us (0.985)
  waiting for transfers between devices: 32.7 us -> 21.9 us
  starting transfers between devices: 27 us -> 36.5 us
    all_to_all x1 -> x0, waiting for transfers between devices: 15.4 us -> none  [on_device(): partials = lax.all_to_all(chip_sum, ('y', 'zl'), 0, 0, tiled=True)]
    ppermute x0 -> x7, starting transfers between devices: none -> 12.7 us  [send(): return in_vmem(lax.ppermute(part, ('y', 'zl'), pairs))]
    ppermute x0 -> x7, waiting for transfers between devices: none -> 5.68 us  [send(): return in_vmem(lax.ppermute(part, ('y', 'zl'), pairs))]
    all_to_all x1 -> x0, starting transfers between devices: 4.92 us -> none  [on_device(): partials = lax.all_to_all(chip_sum, ('y', 'zl'), 0, 0, tiled=True)]
    all_to_all x1, starting transfers between devices: 6.68 us -> 8.11 us  [exchange(): return in_vmem(lax.all_to_all(outbox, chips, 0, 0, tiled=True))]
    ppermute x3, waiting for transfers between devices: 1.3 us -> 0.24 us  [swap(): return lax.ppermute(array, 'c', [(0, 1), (1, 0)])]
  transfers between devices with their start and end apart: 12 -> 18, of which waited for: 5 -> 8; matrix products, arithmetic and copies ran while one was open for 1% -> 1% of each run, Pallas kernels for 16% -> 16%
where the time goes in v4:
time: 81.2 us; the launch traced here: 81 us
  starting transfers between devices  36.5 us (45%)
  waiting for transfers between devices  21.9 us (27%)
  Pallas kernels  19.3 us (24%)
  between operations  1.43 us (2%)
  other arithmetic  1.12 us (1%)
    pallas_call x5, Pallas kernels, call(): pl.pallas_call(kernel, in_specs=specs, out_specs=[VMEM] * len(results), o...  15.8 us
    all_to_all x1, waiting for transfers between devices, exchange(): return in_vmem(lax.all_to_all(outbox, chips, 0, 0, tiled=True))  15.7 us
    ppermute x7, starting transfers between devices, send(): return in_vmem(lax.ppermute(part, ('y', 'zl'), pairs))  12.7 us
    all_to_all x1, starting transfers between devices, exchange(): return in_vmem(lax.all_to_all(outbox, chips, 0, 0, tiled=True))  8.11 us
    ppermute x4, starting transfers between devices, shift(): lax.ppermute(block, 'x', [(n, (n + by) % x_size) for n in range(x_size)])  7.15 us
    ppermute x2, starting transfers between devices, cross(): return lax.ppermute(block, 'zh', [(0, 1), (1, 0)])  6.64 us
    ppermute x7, waiting for transfers between devices, send(): return in_vmem(lax.ppermute(part, ('y', 'zl'), pairs))  5.68 us
    pallas_call x1, Pallas kernels, exchange(): pl.pallas_call(pack_kernel, in_specs=[SMEM, SMEM, SMEM, VMEM, VMEM], out_...  1.7 us
  transfers between devices with their start and end apart: 18, of which 8 were waited for; matrix products, arithmetic and copies ran while one was open for 1% of the time, Pallas kernels for 16%

profile of v4, /device:TPU:0, one launch (start us, length us, event | category | flops | bytes accessed | tf_op | source)
XLA Modules:
  0.0 81.0 jit_solution(6881327277075851314)
XLA Ops:
  0.0 1.0 %shard_map.64.block = f32[256,256]{1,0:T(8,128)S(1)} custom-call(s32[2,2]{1,0:T(2,128)} %mask.1, f32[2,128,256]{2,1,0:T(8,128)} %block.1), custom_call_target="tpu_custom_call" | custom-call | tf_op jit(solution)/shard_map/pallas_call | solution.py:199
  1.0 4.0 %collective-permute-start = (f32[256,256]{1,0:T(8,128)S(1)}, f32[256,256]{1,0:T(8,128)S(1)}, u32[]{:S(2)}, u32[]{:S(2)}) collective-permute-start(f32[256,256]{1,0:T(8,128)S(1)} %shard_map.64.block), channel_id=1, source_target_pairs={{0,64},{64,0},{1,65},{65,1},{2,66},{66,2},{3,67},{67,3},{4,68},{68... | collective-permute-start | bytes 786440 | tf_op jit(solution)/shard_map/ppermute | solution.py:216
  5.0 1.5 %collective-permute-start.1 = (f32[256,256]{1,0:T(8,128)S(1)}, f32[256,256]{1,0:T(8,128)S(1)}, u32[]{:S(2)}, u32[]{:S(2)}) collective-permute-start(f32[256,256]{1,0:T(8,128)S(1)} %shard_map.64.block), channel_id=1, source_target_pairs={{0,16},{16,32},{32,48},{48,0},{1,17},{17,33},{33,49},{49,1},{2,18}... | collective-permute-start | bytes 786440 | tf_op jit(solution)/shard_map/ppermute | solution.py:213
  6.5 1.7 %collective-permute-start.2 = (f32[256,256]{1,0:T(8,128)S(1)}, f32[256,256]{1,0:T(8,128)S(1)}, u32[]{:S(2)}, u32[]{:S(2)}) collective-permute-start(f32[256,256]{1,0:T(8,128)S(1)} %shard_map.64.block), channel_id=1, source_target_pairs={{0,48},{16,0},{32,16},{48,32},{1,49},{17,1},{33,17},{49,33},{2,50}... | collective-permute-start | bytes 786440 | tf_op jit(solution)/shard_map/ppermute | solution.py:213
  8.3 1.3 %collective-permute-start.6 = (f32[256,256]{1,0:T(8,128)S(1)}, f32[256,256]{1,0:T(8,128)S(1)}, u32[]{:S(2)}, u32[]{:S(2)}) collective-permute-start(f32[256,256]{1,0:T(8,128)S(1)} %shard_map.64.block), channel_id=1, source_target_pairs={{0,96},{16,112},{32,64},{48,80},{64,32},{80,48},{96,0},{112,16},{1... | collective-permute-start | bytes 786440 | tf_op jit(solution)/shard_map/ppermute | solution.py:242
  9.6 4.6 %shard_map.65 = (f32[8,2,128,1024]{3,2,1,0:T(8,128)S(1)}, f32[2,8,128,256]{3,2,1,0:T(8,128)S(1)}) custom-call(s32[16]{0:T(128)S(1)} %compare_select_fusion.28.places, f32[256,256]{1,0:T(8,128)S(1)} %shard_map.64.block, f32[8,2,128,2048]{3,2,1,0:T(8,128)} %bitcast.4), custom_call_target="tpu_custom_call" | custom-call | flops 805306368 | bytes 1048576 | tf_op jit(solution)/shard_map/pallas_call | solution.py:118
  14.2 0.0 collective-permute-done.across
  14.2 0.2 collective-permute-done.1.left
  14.5 1.3 %collective-permute-start.3 = (f32[256,256]{1,0:T(8,128)S(1)}, f32[256,256]{1,0:T(8,128)S(1)}, u32[]{:S(2)}, u32[]{:S(2)}) collective-permute-start(f32[256,256]{1,0:T(8,128)S(1)} %collective-permute-done.1.left), channel_id=1, source_target_pairs={{0,16},{16,32},{32,48},{48,0},{1,17},{17,33},{33,49},{49,1},{2,18}... | collective-permute-start | bytes 786440 | tf_op jit(solution)/shard_map/ppermute | solution.py:213
  15.8 2.6 %collective-permute-start.4 = (f32[256,256]{1,0:T(8,128)S(1)}, f32[256,256]{1,0:T(8,128)S(1)}, u32[]{:S(2)}, u32[]{:S(2)}) collective-permute-start(f32[256,256]{1,0:T(8,128)S(1)} %collective-permute-done.1.left), channel_id=1, source_target_pairs={{0,64},{64,0},{1,65},{65,1},{2,66},{66,2},{3,67},{67,3},{4,68},{68... | collective-permute-start | bytes 786440 | tf_op jit(solution)/shard_map/ppermute | solution.py:216
  18.4 2.6 %collective-permute-start.5 = (f32[256,256]{1,0:T(8,128)S(1)}, f32[256,256]{1,0:T(8,128)S(1)}, u32[]{:S(2)}, u32[]{:S(2)}) collective-permute-start(f32[256,256]{1,0:T(8,128)S(1)} %collective-permute-done.across), channel_id=1, source_target_pairs={{0,48},{16,0},{32,16},{48,32},{1,49},{17,1},{33,17},{49,33},{2,50}... | collective-permute-start | bytes 786440 | tf_op jit(solution)/shard_map/ppermute | solution.py:213
  21.0 0.0 collective-permute-done.2.right
  21.0 5.7 %shard_map.66 = (f32[8,2,128,1024]{3,2,1,0:T(8,128)S(1)}, f32[2,8,128,256]{3,2,1,0:T(8,128)S(1)}) custom-call(s32[16]{0:T(128)S(1)} %compare_select_fusion.28.places, f32[8,2,128,1024]{3,2,1,0:T(8,128)S(1)} %get-tuple-element.321.here, f32[256,256]{1,0:T(8,128)S(1)} %collective-permute-done.1.left, ...), custom_call_target="tpu_custom_call", output_to_operand_aliasing={{1}: (5, {})} | custom-call | flops 2415919104 | bytes 1048576 | tf_op jit(solution)/shard_map/pallas_call | solution.py:118
  26.8 0.0 collective-permute-done.6.across_far
  26.8 0.0 collective-permute-done.3.far
  26.8 0.0 collective-permute-done.4.across_left
  26.8 2.4 %shard_map.68 = f32[8,128,256]{2,1,0:T(8,128)S(1)} custom-call(s32[16]{0:T(128)S(1)} %compare_select_fusion.28.places, f32[8,2,128,1024]{3,2,1,0:T(8,128)S(1)} %get-tuple-element.321.here, f32[8,2,128,1024]{3,2,1,0:T(8,128)S(1)} %get-tuple-element.326.there, f32[256,256]{1,0:T(8,128)S(1)} %collective-permute-done.3.far, ...), custom_call_target="tpu_custom_call" | custom-call | flops 1610612736 | bytes 1048576 | tf_op jit(solution)/shard_map/pallas_call | solution.py:118
  29.2 0.0 copy-start.1
  29.2 0.0 copy-start
  29.2 0.0 copy-start.2
  29.3 0.1 collective-permute-start.7
  29.3 2.4 %shard_map.67.left = f32[8,128,256]{2,1,0:T(8,128)S(1)} custom-call(s32[16]{0:T(128)S(1)} %compare_select_fusion.28.places, f32[8,2,128,1024]{3,2,1,0:T(8,128)S(1)} %get-tuple-element.321.here, f32[8,2,128,1024]{3,2,1,0:T(8,128)S(1)} %get-tuple-element.326.there, f32[256,256]{1,0:T(8,128)S(1)} %collective-permute-done.3.far, ...), custom_call_target="tpu_custom_call" | custom-call | flops 1610612736 | bytes 1048576 | tf_op jit(solution)/shard_map/pallas_call | solution.py:118
  31.8 0.2 collective-permute-done.7.right
  32.0 0.7 shard_map.69
  32.7 0.3 collective-permute-start.8
  33.0 3.7 %collective-permute-start.9 = (f32[128,256]{1,0:T(8,128)S(1)}, f32[128,256]{1,0:T(8,128)S(1)}, u32[]{:S(2)}, u32[]{:S(2)}) collective-permute-start(f32[128,256]{1,0:T(8,128)S(1)} %get-tuple-element.338), channel_id=1, source_target_pairs={{0,10},{2,8},{4,14},{6,12},{8,2},{10,0},{12,6},{14,4},{1,11},{3,9}... | collective-permute-start | bytes 393224 | tf_op jit(solution)/shard_map/ppermute | solution.py:293
  36.7 0.3 collective-permute-start.10
  37.0 2.1 %collective-permute-start.11 = (f32[128,256]{1,0:T(8,128)S(1)}, f32[128,256]{1,0:T(8,128)S(1)}, u32[]{:S(2)}, u32[]{:S(2)}) collective-permute-start(f32[128,256]{1,0:T(8,128)S(1)} %get-tuple-element.340), channel_id=1, source_target_pairs={{0,6},{2,4},{4,10},{6,8},{8,14},{10,12},{12,2},{14,0},{1,7},{3,5},... | collective-permute-start | bytes 393224 | tf_op jit(solution)/shard_map/ppermute | solution.py:293
  39.1 2.1 %collective-permute-start.12 = (f32[128,256]{1,0:T(8,128)S(1)}, f32[128,256]{1,0:T(8,128)S(1)}, u32[]{:S(2)}, u32[]{:S(2)}) collective-permute-start(f32[128,256]{1,0:T(8,128)S(1)} %get-tuple-element.341), channel_id=1, source_target_pairs={{0,14},{2,12},{4,2},{6,0},{8,6},{10,4},{12,10},{14,8},{1,15},{3,13... | collective-permute-start | bytes 393224 | tf_op jit(solution)/shard_map/ppermute | solution.py:293
  41.2 0.4 collective-permute-start.13
  41.6 3.2 %collective-permute-start.14 = (f32[128,256]{1,0:T(8,128)S(1)}, f32[128,256]{1,0:T(8,128)S(1)}, u32[]{:S(2)}, u32[]{:S(2)}) collective-permute-start(f32[128,256]{1,0:T(8,128)S(1)} %get-tuple-element.343), channel_id=1, source_target_pairs={{0,12},{2,14},{4,0},{6,2},{8,4},{10,6},{12,8},{14,10},{1,13},{3,15... | collective-permute-start | bytes 393224 | tf_op jit(solution)/shard_map/ppermute | solution.py:293
  44.8 1.0 %collective-permute-start.15 = (f32[128,256]{1,0:T(8,128)S(1)}, f32[128,256]{1,0:T(8,128)S(1)}, u32[]{:S(2)}, u32[]{:S(2)}) collective-permute-start(f32[128,256]{1,0:T(8,128)S(1)} %get-tuple-element.344), channel_id=1, source_target_pairs={{0,2},{2,0},{4,6},{6,4},{8,10},{10,8},{12,14},{14,12},{1,3},{3,1},... | collective-permute-start | bytes 393224 | tf_op jit(solution)/shard_map/ppermute | solution.py:293
  45.8 0.2 add_reduce_fusion
  46.0 2.4 %collective-permute-done.11.refs_2_ = f32[128,256]{1,0:T(8,128)S(1)} collective-permute-done((f32[128,256]{1,0:T(8,128)S(1)}, f32[128,256]{1,0:T(8,128)S(1)}, u32[]{:S(2)}, u32[]{:S(2)}) %collective-permute-start.11) | collective-permute-done | bytes 131104 | tf_op jit(solution)/shard_map/ppermute | solution.py:293
  48.3 0.6 collective-permute-done.12.refs_3_
  49.0 0.2 collective-permute-done.13.refs_4_
  49.1 0.8 collective-permute-done.14.refs_5_
  50.0 1.7 %collective-permute-done.15.refs_6_ = f32[128,256]{1,0:T(8,128)S(1)} collective-permute-done((f32[128,256]{1,0:T(8,128)S(1)}, f32[128,256]{1,0:T(8,128)S(1)}, u32[]{:S(2)}, u32[]{:S(2)}) %collective-permute-start.15) | collective-permute-done | bytes 131104 | tf_op jit(solution)/shard_map/ppermute | solution.py:293
  51.7 0.1 shard_map.70.own
  51.7 0.1 collective-permute-start.16
  51.8 0.6 fusion.6
  53.7 1.7 %shard_map.71 = f32[832,2,128]{2,1,0:T(2,128)} custom-call(s32[128]{0:T(128)S(1)} %get-tuple-element.461.own_place, s32[128]{0:T(128)S(1)} %get-tuple-element.448.other_place, s32[1]{0:T(128)} %bitcast.1.most, f32[128,256]{1,0:T(8,128)S(1)} %shard_map.70.own, f32[128,256]{1,0:T(8,128)S(1)} %collective-permute-done.16.other), custom_call_target="tpu_custom_call" | custom-call | tf_op jit(solution)/shard_map/pallas_call | solution.py:332
  55.4 8.1 %all-to-all-start.1 = ((f32[832,2,128]{2,1,0:T(2,128)}), f32[832,2,128]{2,1,0:T(2,128)S(1)}, u32[]{:S(2)}, u32[]{:S(2)}) async-start(f32[832,2,128]{2,1,0:T(2,128)} %shard_map.71), calls=%async_computation.1 | async-start | bytes 1703936 | tf_op jit(solution)/shard_map/all_to_all | solution.py:339
  63.5 0.1 broadcast_subtract_fusion.1.scale
  63.6 0.2 convert_reduce_fusion
  63.8 15.7 %all-to-all-done.1.got = f32[832,2,128]{2,1,0:T(2,128)S(1)} async-done(((f32[832,2,128]{2,1,0:T(2,128)}), f32[832,2,128]{2,1,0:T(2,128)S(1)}, u32[]{:S(2)}, u32[]{:S(2)}) %all-to-all-start.1) | async-done | bytes 852000 | tf_op jit(solution)/shard_map/all_to_all | solution.py:339
  79.5 0.7 shard_map.72
  80.3 0.7 copy.16
  (13 shorter events, 0.1 us)
Async XLA Ops:
  1.0 13.2 %collective-permute-start = (f32[256,256]{1,0:T(8,128)S(1)}, f32[256,256]{1,0:T(8,128)S(1)}, u32[]{:S(2)}, u32[]{:S(2)}) collective-permute-start(f32[256,256]{1,0:T(8,128)S(1)} %shard_map.64.block), channel_id=1, source_target_pairs={{0,64},{64,0},{1,65},{65,1},{2,66},{66,2},{3,67},{67,3},{4,68},{68... | collective-permute-start | bytes 786440 | tf_op jit(solution)/shard_map/ppermute | solution.py:216
  5.0 9.5 %collective-permute-start.1 = (f32[256,256]{1,0:T(8,128)S(1)}, f32[256,256]{1,0:T(8,128)S(1)}, u32[]{:S(2)}, u32[]{:S(2)}) collective-permute-start(f32[256,256]{1,0:T(8,128)S(1)} %shard_map.64.block), channel_id=1, source_target_pairs={{0,16},{16,32},{32,48},{48,0},{1,17},{17,33},{33,49},{49,1},{2,18}... | collective-permute-start | bytes 786440 | tf_op jit(solution)/shard_map/ppermute | solution.py:213
  6.5 14.5 %collective-permute-start.2 = (f32[256,256]{1,0:T(8,128)S(1)}, f32[256,256]{1,0:T(8,128)S(1)}, u32[]{:S(2)}, u32[]{:S(2)}) collective-permute-start(f32[256,256]{1,0:T(8,128)S(1)} %shard_map.64.block), channel_id=1, source_target_pairs={{0,48},{16,0},{32,16},{48,32},{1,49},{17,1},{33,17},{49,33},{2,50}... | collective-permute-start | bytes 786440 | tf_op jit(solution)/shard_map/ppermute | solution.py:213
  8.3 18.5 %collective-permute-start.6 = (f32[256,256]{1,0:T(8,128)S(1)}, f32[256,256]{1,0:T(8,128)S(1)}, u32[]{:S(2)}, u32[]{:S(2)}) collective-permute-start(f32[256,256]{1,0:T(8,128)S(1)} %shard_map.64.block), channel_id=1, source_target_pairs={{0,96},{16,112},{32,64},{48,80},{64,32},{80,48},{96,0},{112,16},{1... | collective-permute-start | bytes 786440 | tf_op jit(solution)/shard_map/ppermute | solution.py:242
  14.5 12.3 %collective-permute-start.3 = (f32[256,256]{1,0:T(8,128)S(1)}, f32[256,256]{1,0:T(8,128)S(1)}, u32[]{:S(2)}, u32[]{:S(2)}) collective-permute-start(f32[256,256]{1,0:T(8,128)S(1)} %collective-permute-done.1.left), channel_id=1, source_target_pairs={{0,16},{16,32},{32,48},{48,0},{1,17},{17,33},{33,49},{49,1},{2,18}... | collective-permute-start | bytes 786440 | tf_op jit(solution)/shard_map/ppermute | solution.py:213
  15.8 11.0 %collective-permute-start.4 = (f32[256,256]{1,0:T(8,128)S(1)}, f32[256,256]{1,0:T(8,128)S(1)}, u32[]{:S(2)}, u32[]{:S(2)}) collective-permute-start(f32[256,256]{1,0:T(8,128)S(1)} %collective-permute-done.1.left), channel_id=1, source_target_pairs={{0,64},{64,0},{1,65},{65,1},{2,66},{66,2},{3,67},{67,3},{4,68},{68... | collective-permute-start | bytes 786440 | tf_op jit(solution)/shard_map/ppermute | solution.py:216
  18.4 8.4 %collective-permute-start.5 = (f32[256,256]{1,0:T(8,128)S(1)}, f32[256,256]{1,0:T(8,128)S(1)}, u32[]{:S(2)}, u32[]{:S(2)}) collective-permute-start(f32[256,256]{1,0:T(8,128)S(1)} %collective-permute-done.across), channel_id=1, source_target_pairs={{0,48},{16,0},{32,16},{48,32},{1,49},{17,1},{33,17},{49,33},{2,50}... | collective-permute-start | bytes 786440 | tf_op jit(solution)/shard_map/ppermute | solution.py:213
  29.2 3.4 %copy-start.1 = (s32[128]{0:T(128)S(1)}, s32[128]{0:T(128)}, u32[]{:S(2)}) copy-start(s32[128]{0:T(128)} %param.11) | copy-start | bytes 1540
  29.2 34.3 %copy-start = (f32[256]{0:T(256)S(1)}, f32[256]{0:T(256)}, u32[]{:S(2)}) copy-start(f32[256]{0:T(256)} %param.13) | copy-start | bytes 3076
  29.2 34.3 %copy-start.2 = (f32[128]{0:T(128)S(1)}, f32[128]{0:T(128)}, u32[]{:S(2)}) copy-start(f32[128]{0:T(128)} %param.12) | copy-start | bytes 1540
  29.3 2.7 %collective-permute-start.7 = (f32[8,128,256]{2,1,0:T(8,128)S(1)}, f32[8,128,256]{2,1,0:T(8,128)S(1)}, u32[]{:S(2)}, u32[]{:S(2)}) collective-permute-start(f32[8,128,256]{2,1,0:T(8,128)S(1)} %shard_map.68), channel_id=1, source_target_pairs={{0,1},{1,0},{2,3},{3,2},{4,5},{5,4},{6,7},{7,6},{8,9},{9,8},{10,11... | collective-permute-start | bytes 3145736 | tf_op jit(solution)/shard_map/ppermute | solution.py:219
  32.7 8.6 %collective-permute-start.8 = (s32[128]{0:T(128)S(1)}, s32[128]{0:T(128)S(1)}, u32[]{:S(2)}, u32[]{:S(2)}) collective-permute-start(s32[128]{0:T(128)S(1)} %copy-done.1), channel_id=1, source_target_pairs={{0,1},{1,0},{2,3},{3,2},{4,5},{5,4},{6,7},{7,6},{8,9},{9,8},{10,11... | collective-permute-start | bytes 1544 | tf_op jit(solution)/shard_map/ppermute | solution.py:219
  33.0 8.6 %collective-permute-start.9 = (f32[128,256]{1,0:T(8,128)S(1)}, f32[128,256]{1,0:T(8,128)S(1)}, u32[]{:S(2)}, u32[]{:S(2)}) collective-permute-start(f32[128,256]{1,0:T(8,128)S(1)} %get-tuple-element.338), channel_id=1, source_target_pairs={{0,10},{2,8},{4,14},{6,12},{8,2},{10,0},{12,6},{14,4},{1,11},{3,9}... | collective-permute-start | bytes 393224 | tf_op jit(solution)/shard_map/ppermute | solution.py:293
  36.7 8.1 %collective-permute-start.10 = (f32[128,256]{1,0:T(8,128)S(1)}, f32[128,256]{1,0:T(8,128)S(1)}, u32[]{:S(2)}, u32[]{:S(2)}) collective-permute-start(f32[128,256]{1,0:T(8,128)S(1)} %get-tuple-element.339), channel_id=1, source_target_pairs={{0,8},{2,10},{4,12},{6,14},{8,0},{10,2},{12,4},{14,6},{1,9},{3,11}... | collective-permute-start | bytes 393224 | tf_op jit(solution)/shard_map/ppermute | solution.py:293
  37.0 11.3 %collective-permute-start.11 = (f32[128,256]{1,0:T(8,128)S(1)}, f32[128,256]{1,0:T(8,128)S(1)}, u32[]{:S(2)}, u32[]{:S(2)}) collective-permute-start(f32[128,256]{1,0:T(8,128)S(1)} %get-tuple-element.340), channel_id=1, source_target_pairs={{0,6},{2,4},{4,10},{6,8},{8,14},{10,12},{12,2},{14,0},{1,7},{3,5},... | collective-permute-start | bytes 393224 | tf_op jit(solution)/shard_map/ppermute | solution.py:293
  39.1 9.9 %collective-permute-start.12 = (f32[128,256]{1,0:T(8,128)S(1)}, f32[128,256]{1,0:T(8,128)S(1)}, u32[]{:S(2)}, u32[]{:S(2)}) collective-permute-start(f32[128,256]{1,0:T(8,128)S(1)} %get-tuple-element.341), channel_id=1, source_target_pairs={{0,14},{2,12},{4,2},{6,0},{8,6},{10,4},{12,10},{14,8},{1,15},{3,13... | collective-permute-start | bytes 393224 | tf_op jit(solution)/shard_map/ppermute | solution.py:293
  41.2 7.9 %collective-permute-start.13 = (f32[128,256]{1,0:T(8,128)S(1)}, f32[128,256]{1,0:T(8,128)S(1)}, u32[]{:S(2)}, u32[]{:S(2)}) collective-permute-start(f32[128,256]{1,0:T(8,128)S(1)} %get-tuple-element.342), channel_id=1, source_target_pairs={{0,4},{2,6},{4,8},{6,10},{8,12},{10,14},{12,0},{14,2},{1,5},{3,7},... | collective-permute-start | bytes 393224 | tf_op jit(solution)/shard_map/ppermute | solution.py:293
  41.6 8.4 %collective-permute-start.14 = (f32[128,256]{1,0:T(8,128)S(1)}, f32[128,256]{1,0:T(8,128)S(1)}, u32[]{:S(2)}, u32[]{:S(2)}) collective-permute-start(f32[128,256]{1,0:T(8,128)S(1)} %get-tuple-element.343), channel_id=1, source_target_pairs={{0,12},{2,14},{4,0},{6,2},{8,4},{10,6},{12,8},{14,10},{1,13},{3,15... | collective-permute-start | bytes 393224 | tf_op jit(solution)/shard_map/ppermute | solution.py:293
  44.8 6.9 %collective-permute-start.15 = (f32[128,256]{1,0:T(8,128)S(1)}, f32[128,256]{1,0:T(8,128)S(1)}, u32[]{:S(2)}, u32[]{:S(2)}) collective-permute-start(f32[128,256]{1,0:T(8,128)S(1)} %get-tuple-element.344), channel_id=1, source_target_pairs={{0,2},{2,0},{4,6},{6,4},{8,10},{10,8},{12,14},{14,12},{1,3},{3,1},... | collective-permute-start | bytes 393224 | tf_op jit(solution)/shard_map/ppermute | solution.py:293
  51.7 1.9 %collective-permute-start.16 = (f32[128,256]{1,0:T(8,128)S(1)}, f32[128,256]{1,0:T(8,128)S(1)}, u32[]{:S(2)}, u32[]{:S(2)}) collective-permute-start(f32[128,256]{1,0:T(8,128)S(1)} %shard_map.70.own), channel_id=1, source_target_pairs={{0,1},{1,0},{2,3},{3,2},{4,5},{5,4},{6,7},{7,6},{8,9},{9,8},{10,11... | collective-permute-start | bytes 393224 | tf_op jit(solution)/shard_map/ppermute | solution.py:219
  55.4 24.2 %all-to-all-start.1 = ((f32[832,2,128]{2,1,0:T(2,128)}), f32[832,2,128]{2,1,0:T(2,128)S(1)}, u32[]{:S(2)}, u32[]{:S(2)}) async-start(f32[832,2,128]{2,1,0:T(2,128)} %shard_map.71), calls=%async_computation.1 | async-start | bytes 1703936 | tf_op jit(solution)/shard_map/all_to_all | solution.py:339

commit v5 on v4

--- a/solution.py
+++ b/solution.py
@@ -223,7 +223,7 @@
     left, right, opposite = (x + x_size - 1) % x_size, (x + 1) % x_size, (x + 2) % x_size
     where = [1 - core, core, zh, 1 - zh, x, left, right, opposite]
     y, zl = lax.axis_index("y"), lax.axis_index("zl")
-    moves = [(2, 1), (2, 0), (1, 1), (3, 1), (1, 0), (3, 0), (0, 1), (0, 0)]
+    moves = [(1, 1), (3, 1), (2, 1), (2, 0), (0, 1), (1, 0), (3, 0), (0, 0)]
     where += [(y + up) % y_size * zl_size + (zl + over) % zl_size for up, over in moves]
     slot = jnp.arange(len(where), dtype=jnp.int32)
     places = jnp.zeros((len(where),), jnp.int32)
@@ -281,8 +281,6 @@
         [sums[2:]] * len(moves),
     )
 
-    *parts, partner, core = lax.optimization_barrier((*parts, partner, core))
-
     def send(part, move):
         up, over = move
         pairs = [
@@ -293,6 +291,7 @@
         return in_vmem(lax.ppermute(part, ("y", "zl"), pairs))
 
     partials = [send(part, move) for part, move in zip(parts[:-1], moves)] + [parts[-1]]
+    partials[0], partner, core = lax.optimization_barrier((partials[0], partner, core))
 
     rows = pltpu.VMEM((row_count, width), jnp.float32)
     own = pl.pallas_call(
@@ -342,7 +341,7 @@
         unpack_kernel,
         in_specs=[SMEM, VMEM, VMEM, VMEM],
         out_specs=[VMEM, SMEM],
-        out_shape=[rows, pltpu.SMEM((1,), jnp.int32)],
+        out_shape=[jax.ShapeDtypeStruct((row_count, width), jnp.float32), pltpu.SMEM((1,), jnp.int32)],
         scratch_shapes=[pltpu.VMEM((row_count, width), jnp.float32)],
         compiler_params=SMALL,
     )(chip * STRIDE + take_rank % SLOTS, exchange(0), own, scale)
@@ -357,7 +356,7 @@
             mend_kernel,
             in_specs=[SMEM, VMEM, VMEM, VMEM, VMEM],
             out_specs=VMEM,
-            out_shape=rows,
+            out_shape=jax.ShapeDtypeStruct((row_count, width), jnp.float32),
             compiler_params=SMALL,
         )(place, exchange(turn), own, scale, so_far)
         return turn + 1, after

time: 81.2 us -> 80.8 us (level)
  starting transfers between devices: 36.5 us -> 34.2 us
  waiting for transfers between devices: 21.9 us -> 23.7 us
    ppermute x7, starting transfers between devices: 12.7 us -> 10.3 us  [send(): return in_vmem(lax.ppermute(part, ('y', 'zl'), pairs))]
    ppermute x7, waiting for transfers between devices: 5.68 us -> 7.47 us  [send(): return in_vmem(lax.ppermute(part, ('y', 'zl'), pairs))]
  transfers between devices with their start and end apart: 18 -> 18, of which waited for: 8 -> 10; matrix products, arithmetic and copies ran while one was open for 1% -> 1% of each run, Pallas kernels for 16% -> 16%
where the time goes in v5:
time: 80.8 us; the launch traced here: 80.6 us
  starting transfers between devices  34.2 us (42%)
  waiting for transfers between devices  23.7 us (29%)
  Pallas kernels  19.3 us (24%)
  between operations  1.52 us (2%)
  other arithmetic  1.14 us (1%)
    pallas_call x5, Pallas kernels, call(): pl.pallas_call(kernel, in_specs=specs, out_specs=[VMEM] * len(results), o...  15.8 us
    all_to_all x1, waiting for transfers between devices, exchange(): return in_vmem(lax.all_to_all(outbox, chips, 0, 0, tiled=True))  15.7 us
    ppermute x7, starting transfers between devices, send(): return in_vmem(lax.ppermute(part, ('y', 'zl'), pairs))  10.3 us
    all_to_all x1, starting transfers between devices, exchange(): return in_vmem(lax.all_to_all(outbox, chips, 0, 0, tiled=True))  8.64 us
    ppermute x7, waiting for transfers between devices, send(): return in_vmem(lax.ppermute(part, ('y', 'zl'), pairs))  7.47 us
    ppermute x4, starting transfers between devices, shift(): lax.ppermute(block, 'x', [(n, (n + by) % x_size) for n in range(x_size)])  7.15 us
    ppermute x2, starting transfers between devices, cross(): return lax.ppermute(block, 'zh', [(0, 1), (1, 0)])  6.64 us
    pallas_call x1, Pallas kernels, exchange(): pl.pallas_call(pack_kernel, in_specs=[SMEM, SMEM, SMEM, VMEM, VMEM], out_...  1.69 us
  transfers between devices with their start and end apart: 18, of which 10 were waited for; matrix products, arithmetic and copies ran while one was open for 1% of the time, Pallas kernels for 16%

profile of v5, /device:TPU:0, one launch (start us, length us, event | category | flops | bytes accessed | tf_op | source)
XLA Modules:
  0.0 80.6 jit_solution(5514066350549337993)
XLA Ops:
  0.0 1.0 %shard_map.64.block = f32[256,256]{1,0:T(8,128)S(1)} custom-call(s32[2,2]{1,0:T(2,128)} %mask.1, f32[2,128,256]{2,1,0:T(8,128)} %block.1), custom_call_target="tpu_custom_call" | custom-call | tf_op jit(solution)/shard_map/pallas_call | solution.py:199
  1.0 4.0 %collective-permute-start = (f32[256,256]{1,0:T(8,128)S(1)}, f32[256,256]{1,0:T(8,128)S(1)}, u32[]{:S(2)}, u32[]{:S(2)}) collective-permute-start(f32[256,256]{1,0:T(8,128)S(1)} %shard_map.64.block), channel_id=1, source_target_pairs={{0,64},{64,0},{1,65},{65,1},{2,66},{66,2},{3,67},{67,3},{4,68},{68... | collective-permute-start | bytes 786440 | tf_op jit(solution)/shard_map/ppermute | solution.py:216
  5.0 1.5 %collective-permute-start.1 = (f32[256,256]{1,0:T(8,128)S(1)}, f32[256,256]{1,0:T(8,128)S(1)}, u32[]{:S(2)}, u32[]{:S(2)}) collective-permute-start(f32[256,256]{1,0:T(8,128)S(1)} %shard_map.64.block), channel_id=1, source_target_pairs={{0,16},{16,32},{32,48},{48,0},{1,17},{17,33},{33,49},{49,1},{2,18}... | collective-permute-start | bytes 786440 | tf_op jit(solution)/shard_map/ppermute | solution.py:213
  6.5 1.7 %collective-permute-start.2 = (f32[256,256]{1,0:T(8,128)S(1)}, f32[256,256]{1,0:T(8,128)S(1)}, u32[]{:S(2)}, u32[]{:S(2)}) collective-permute-start(f32[256,256]{1,0:T(8,128)S(1)} %shard_map.64.block), channel_id=1, source_target_pairs={{0,48},{16,0},{32,16},{48,32},{1,49},{17,1},{33,17},{49,33},{2,50}... | collective-permute-start | bytes 786440 | tf_op jit(solution)/shard_map/ppermute | solution.py:213
  8.3 1.3 %collective-permute-start.6 = (f32[256,256]{1,0:T(8,128)S(1)}, f32[256,256]{1,0:T(8,128)S(1)}, u32[]{:S(2)}, u32[]{:S(2)}) collective-permute-start(f32[256,256]{1,0:T(8,128)S(1)} %shard_map.64.block), channel_id=1, source_target_pairs={{0,96},{16,112},{32,64},{48,80},{64,32},{80,48},{96,0},{112,16},{1... | collective-permute-start | bytes 786440 | tf_op jit(solution)/shard_map/ppermute | solution.py:242
  9.6 4.6 %shard_map.65 = (f32[8,2,128,1024]{3,2,1,0:T(8,128)S(1)}, f32[2,8,128,256]{3,2,1,0:T(8,128)S(1)}) custom-call(s32[16]{0:T(128)S(1)} %compare_select_fusion.28.places, f32[256,256]{1,0:T(8,128)S(1)} %shard_map.64.block, f32[8,2,128,2048]{3,2,1,0:T(8,128)} %bitcast.4), custom_call_target="tpu_custom_call" | custom-call | flops 805306368 | bytes 1048576 | tf_op jit(solution)/shard_map/pallas_call | solution.py:118
  14.2 0.2 collective-permute-done.1.left
  14.5 1.3 %collective-permute-start.3 = (f32[256,256]{1,0:T(8,128)S(1)}, f32[256,256]{1,0:T(8,128)S(1)}, u32[]{:S(2)}, u32[]{:S(2)}) collective-permute-start(f32[256,256]{1,0:T(8,128)S(1)} %collective-permute-done.1.left), channel_id=1, source_target_pairs={{0,16},{16,32},{32,48},{48,0},{1,17},{17,33},{33,49},{49,1},{2,18}... | collective-permute-start | bytes 786440 | tf_op jit(solution)/shard_map/ppermute | solution.py:213
  15.8 2.6 %collective-permute-start.4 = (f32[256,256]{1,0:T(8,128)S(1)}, f32[256,256]{1,0:T(8,128)S(1)}, u32[]{:S(2)}, u32[]{:S(2)}) collective-permute-start(f32[256,256]{1,0:T(8,128)S(1)} %collective-permute-done.1.left), channel_id=1, source_target_pairs={{0,64},{64,0},{1,65},{65,1},{2,66},{66,2},{3,67},{67,3},{4,68},{68... | collective-permute-start | bytes 786440 | tf_op jit(solution)/shard_map/ppermute | solution.py:216
  18.4 2.6 %collective-permute-start.5 = (f32[256,256]{1,0:T(8,128)S(1)}, f32[256,256]{1,0:T(8,128)S(1)}, u32[]{:S(2)}, u32[]{:S(2)}) collective-permute-start(f32[256,256]{1,0:T(8,128)S(1)} %collective-permute-done.across), channel_id=1, source_target_pairs={{0,48},{16,0},{32,16},{48,32},{1,49},{17,1},{33,17},{49,33},{2,50}... | collective-permute-start | bytes 786440 | tf_op jit(solution)/shard_map/ppermute | solution.py:213
  21.0 0.0 collective-permute-done.2.right
  21.0 5.7 %shard_map.66 = (f32[8,2,128,1024]{3,2,1,0:T(8,128)S(1)}, f32[2,8,128,256]{3,2,1,0:T(8,128)S(1)}) custom-call(s32[16]{0:T(128)S(1)} %compare_select_fusion.28.places, f32[8,2,128,1024]{3,2,1,0:T(8,128)S(1)} %get-tuple-element.314.here, f32[256,256]{1,0:T(8,128)S(1)} %collective-permute-done.1.left, ...), custom_call_target="tpu_custom_call", output_to_operand_aliasing={{1}: (5, {})} | custom-call | flops 2415919104 | bytes 1048576 | tf_op jit(solution)/shard_map/pallas_call | solution.py:118
  26.8 0.0 collective-permute-done.3.far
  26.8 0.0 collective-permute-done.4.across_left
  26.8 2.4 %shard_map.68 = f32[8,128,256]{2,1,0:T(8,128)S(1)} custom-call(s32[16]{0:T(128)S(1)} %compare_select_fusion.28.places, f32[8,2,128,1024]{3,2,1,0:T(8,128)S(1)} %get-tuple-element.314.here, f32[8,2,128,1024]{3,2,1,0:T(8,128)S(1)} %get-tuple-element.319.there, f32[256,256]{1,0:T(8,128)S(1)} %collective-permute-done.3.far, ...), custom_call_target="tpu_custom_call" | custom-call | flops 1610612736 | bytes 1048576 | tf_op jit(solution)/shard_map/pallas_call | solution.py:118
  29.2 0.0 copy-start.2
  29.2 0.0 copy-start.1
  29.2 0.0 copy-start.3
  29.3 0.1 collective-permute-start.7
  29.3 2.4 %shard_map.67.left = f32[8,128,256]{2,1,0:T(8,128)S(1)} custom-call(s32[16]{0:T(128)S(1)} %compare_select_fusion.28.places, f32[8,2,128,1024]{3,2,1,0:T(8,128)S(1)} %get-tuple-element.314.here, f32[8,2,128,1024]{3,2,1,0:T(8,128)S(1)} %get-tuple-element.319.there, f32[256,256]{1,0:T(8,128)S(1)} %collective-permute-done.3.far, ...), custom_call_target="tpu_custom_call" | custom-call | flops 1610612736 | bytes 1048576 | tf_op jit(solution)/shard_map/pallas_call | solution.py:118
  31.8 0.2 collective-permute-done.7.right
  32.0 0.7 shard_map.69
  32.7 2.1 %collective-permute-start.8 = (f32[128,256]{1,0:T(8,128)S(1)}, f32[128,256]{1,0:T(8,128)S(1)}, u32[]{:S(2)}, u32[]{:S(2)}) collective-permute-start(f32[128,256]{1,0:T(8,128)S(1)} %get-tuple-element.321), channel_id=1, source_target_pairs={{0,6},{2,4},{4,10},{6,8},{8,14},{10,12},{12,2},{14,0},{1,7},{3,5},... | collective-permute-start | bytes 393224 | tf_op jit(solution)/shard_map/ppermute | solution.py:291
  34.8 2.1 %collective-permute-start.10 = (f32[128,256]{1,0:T(8,128)S(1)}, f32[128,256]{1,0:T(8,128)S(1)}, u32[]{:S(2)}, u32[]{:S(2)}) collective-permute-start(f32[128,256]{1,0:T(8,128)S(1)} %get-tuple-element.325), channel_id=1, source_target_pairs={{0,14},{2,12},{4,2},{6,0},{8,6},{10,4},{12,10},{14,8},{1,15},{3,13... | collective-permute-start | bytes 393224 | tf_op jit(solution)/shard_map/ppermute | solution.py:291
  36.9 2.4 %collective-permute-start.11 = (f32[128,256]{1,0:T(8,128)S(1)}, f32[128,256]{1,0:T(8,128)S(1)}, u32[]{:S(2)}, u32[]{:S(2)}) collective-permute-start(f32[128,256]{1,0:T(8,128)S(1)} %get-tuple-element.326), channel_id=1, source_target_pairs={{0,10},{2,8},{4,14},{6,12},{8,2},{10,0},{12,6},{14,4},{1,11},{3,9}... | collective-permute-start | bytes 393224 | tf_op jit(solution)/shard_map/ppermute | solution.py:291
  39.3 1.5 %collective-permute-start.12 = (f32[128,256]{1,0:T(8,128)S(1)}, f32[128,256]{1,0:T(8,128)S(1)}, u32[]{:S(2)}, u32[]{:S(2)}) collective-permute-start(f32[128,256]{1,0:T(8,128)S(1)} %get-tuple-element.327), channel_id=1, source_target_pairs={{0,8},{2,10},{4,12},{6,14},{8,0},{10,2},{12,4},{14,6},{1,9},{3,11}... | collective-permute-start | bytes 393224 | tf_op jit(solution)/shard_map/ppermute | solution.py:291
  40.8 1.0 %collective-permute-start.13 = (f32[128,256]{1,0:T(8,128)S(1)}, f32[128,256]{1,0:T(8,128)S(1)}, u32[]{:S(2)}, u32[]{:S(2)}) collective-permute-start(f32[128,256]{1,0:T(8,128)S(1)} %get-tuple-element.328), channel_id=1, source_target_pairs={{0,2},{2,0},{4,6},{6,4},{8,10},{10,8},{12,14},{14,12},{1,3},{3,1},... | collective-permute-start | bytes 393224 | tf_op jit(solution)/shard_map/ppermute | solution.py:291
  41.9 0.3 collective-permute-done.8.refs_0_
  42.2 0.1 collective-permute-start.14
  42.2 2.8 %collective-permute-done.10.refs_1_ = f32[128,256]{1,0:T(8,128)S(1)} collective-permute-done((f32[128,256]{1,0:T(8,128)S(1)}, f32[128,256]{1,0:T(8,128)S(1)}, u32[]{:S(2)}, u32[]{:S(2)}) %collective-permute-start.10) | collective-permute-done | bytes 131104 | tf_op jit(solution)/shard_map/ppermute | solution.py:291
  45.0 1.0 %collective-permute-start.15 = (f32[128,256]{1,0:T(8,128)S(1)}, f32[128,256]{1,0:T(8,128)S(1)}, u32[]{:S(2)}, u32[]{:S(2)}) collective-permute-start(f32[128,256]{1,0:T(8,128)S(1)} %get-tuple-element.330), channel_id=1, source_target_pairs={{0,12},{2,14},{4,0},{6,2},{8,4},{10,6},{12,8},{14,10},{1,13},{3,15... | collective-permute-start | bytes 393224 | tf_op jit(solution)/shard_map/ppermute | solution.py:291
  46.1 0.1 collective-permute-done.11.refs_2_
  46.2 2.2 %collective-permute-done.12.refs_3_ = f32[128,256]{1,0:T(8,128)S(1)} collective-permute-done((f32[128,256]{1,0:T(8,128)S(1)}, f32[128,256]{1,0:T(8,128)S(1)}, u32[]{:S(2)}, u32[]{:S(2)}) %collective-permute-start.12) | collective-permute-done | bytes 131104 | tf_op jit(solution)/shard_map/ppermute | solution.py:291
  48.4 0.5 collective-permute-done.13.refs_4_
  48.9 1.3 %collective-permute-done.14.refs_5_ = f32[128,256]{1,0:T(8,128)S(1)} collective-permute-done((f32[128,256]{1,0:T(8,128)S(1)}, f32[128,256]{1,0:T(8,128)S(1)}, u32[]{:S(2)}, u32[]{:S(2)}) %collective-permute-start.14) | collective-permute-done | bytes 131104 | tf_op jit(solution)/shard_map/ppermute | solution.py:291
  50.2 0.3 collective-permute-done.15.refs_6_
  50.5 0.1 shard_map.70.own
  50.5 0.1 collective-permute-start.16
  50.6 0.2 add_reduce_fusion
  50.8 0.7 fusion.6
  52.8 1.7 %shard_map.71 = f32[832,2,128]{2,1,0:T(2,128)} custom-call(s32[128]{0:T(128)S(1)} %get-tuple-element.447.own_place, s32[128]{0:T(128)S(1)} %get-tuple-element.434.other_place, s32[1]{0:T(128)} %bitcast.1.most, f32[128,256]{1,0:T(8,128)S(1)} %shard_map.70.own, f32[128,256]{1,0:T(8,128)S(1)} %collective-permute-done.16.other), custom_call_target="tpu_custom_call" | custom-call | tf_op jit(solution)/shard_map/pallas_call | solution.py:331
  54.5 8.6 %all-to-all-start.1 = ((f32[832,2,128]{2,1,0:T(2,128)}), f32[832,2,128]{2,1,0:T(2,128)S(1)}, u32[]{:S(2)}, u32[]{:S(2)}) async-start(f32[832,2,128]{2,1,0:T(2,128)} %shard_map.71), calls=%async_computation.1 | async-start | bytes 1703936 | tf_op jit(solution)/shard_map/all_to_all | solution.py:338
  63.1 0.1 broadcast_subtract_fusion.1.scale
  63.2 0.2 convert_reduce_fusion
  63.4 15.7 %all-to-all-done.1.got = f32[832,2,128]{2,1,0:T(2,128)S(1)} async-done(((f32[832,2,128]{2,1,0:T(2,128)}), f32[832,2,128]{2,1,0:T(2,128)S(1)}, u32[]{:S(2)}, u32[]{:S(2)}) %all-to-all-start.1) | async-done | bytes 852000 | tf_op jit(solution)/shard_map/all_to_all | solution.py:338
  79.1 0.7 shard_map.72
  79.9 0.0 copy-start
  79.9 0.6 copy-done
  (14 shorter events, 0.1 us)
Async XLA Ops:
  1.0 13.2 %collective-permute-start = (f32[256,256]{1,0:T(8,128)S(1)}, f32[256,256]{1,0:T(8,128)S(1)}, u32[]{:S(2)}, u32[]{:S(2)}) collective-permute-start(f32[256,256]{1,0:T(8,128)S(1)} %shard_map.64.block), channel_id=1, source_target_pairs={{0,64},{64,0},{1,65},{65,1},{2,66},{66,2},{3,67},{67,3},{4,68},{68... | collective-permute-start | bytes 786440 | tf_op jit(solution)/shard_map/ppermute | solution.py:216
  5.0 9.5 %collective-permute-start.1 = (f32[256,256]{1,0:T(8,128)S(1)}, f32[256,256]{1,0:T(8,128)S(1)}, u32[]{:S(2)}, u32[]{:S(2)}) collective-permute-start(f32[256,256]{1,0:T(8,128)S(1)} %shard_map.64.block), channel_id=1, source_target_pairs={{0,16},{16,32},{32,48},{48,0},{1,17},{17,33},{33,49},{49,1},{2,18}... | collective-permute-start | bytes 786440 | tf_op jit(solution)/shard_map/ppermute | solution.py:213
  6.5 14.5 %collective-permute-start.2 = (f32[256,256]{1,0:T(8,128)S(1)}, f32[256,256]{1,0:T(8,128)S(1)}, u32[]{:S(2)}, u32[]{:S(2)}) collective-permute-start(f32[256,256]{1,0:T(8,128)S(1)} %shard_map.64.block), channel_id=1, source_target_pairs={{0,48},{16,0},{32,16},{48,32},{1,49},{17,1},{33,17},{49,33},{2,50}... | collective-permute-start | bytes 786440 | tf_op jit(solution)/shard_map/ppermute | solution.py:213
  8.3 18.5 %collective-permute-start.6 = (f32[256,256]{1,0:T(8,128)S(1)}, f32[256,256]{1,0:T(8,128)S(1)}, u32[]{:S(2)}, u32[]{:S(2)}) collective-permute-start(f32[256,256]{1,0:T(8,128)S(1)} %shard_map.64.block), channel_id=1, source_target_pairs={{0,96},{16,112},{32,64},{48,80},{64,32},{80,48},{96,0},{112,16},{1... | collective-permute-start | bytes 786440 | tf_op jit(solution)/shard_map/ppermute | solution.py:242
  14.5 12.3 %collective-permute-start.3 = (f32[256,256]{1,0:T(8,128)S(1)}, f32[256,256]{1,0:T(8,128)S(1)}, u32[]{:S(2)}, u32[]{:S(2)}) collective-permute-start(f32[256,256]{1,0:T(8,128)S(1)} %collective-permute-done.1.left), channel_id=1, source_target_pairs={{0,16},{16,32},{32,48},{48,0},{1,17},{17,33},{33,49},{49,1},{2,18}... | collective-permute-start | bytes 786440 | tf_op jit(solution)/shard_map/ppermute | solution.py:213
  15.8 11.0 %collective-permute-start.4 = (f32[256,256]{1,0:T(8,128)S(1)}, f32[256,256]{1,0:T(8,128)S(1)}, u32[]{:S(2)}, u32[]{:S(2)}) collective-permute-start(f32[256,256]{1,0:T(8,128)S(1)} %collective-permute-done.1.left), channel_id=1, source_target_pairs={{0,64},{64,0},{1,65},{65,1},{2,66},{66,2},{3,67},{67,3},{4,68},{68... | collective-permute-start | bytes 786440 | tf_op jit(solution)/shard_map/ppermute | solution.py:216
  18.4 8.4 %collective-permute-start.5 = (f32[256,256]{1,0:T(8,128)S(1)}, f32[256,256]{1,0:T(8,128)S(1)}, u32[]{:S(2)}, u32[]{:S(2)}) collective-permute-start(f32[256,256]{1,0:T(8,128)S(1)} %collective-permute-done.across), channel_id=1, source_target_pairs={{0,48},{16,0},{32,16},{48,32},{1,49},{17,1},{33,17},{49,33},{2,50}... | collective-permute-start | bytes 786440 | tf_op jit(solution)/shard_map/ppermute | solution.py:213
  29.2 16.9 %copy-start.2 = (s32[128]{0:T(128)S(1)}, s32[128]{0:T(128)}, u32[]{:S(2)}) copy-start(s32[128]{0:T(128)} %param.11) | copy-start | bytes 1540
  29.2 33.9 %copy-start.1 = (f32[256]{0:T(256)S(1)}, f32[256]{0:T(256)}, u32[]{:S(2)}) copy-start(f32[256]{0:T(256)} %param.13) | copy-start | bytes 3076
  29.2 33.9 %copy-start.3 = (f32[128]{0:T(128)S(1)}, f32[128]{0:T(128)}, u32[]{:S(2)}) copy-start(f32[128]{0:T(128)} %param.12) | copy-start | bytes 1540
  29.3 2.7 %collective-permute-start.7 = (f32[8,128,256]{2,1,0:T(8,128)S(1)}, f32[8,128,256]{2,1,0:T(8,128)S(1)}, u32[]{:S(2)}, u32[]{:S(2)}) collective-permute-start(f32[8,128,256]{2,1,0:T(8,128)S(1)} %shard_map.68), channel_id=1, source_target_pairs={{0,1},{1,0},{2,3},{3,2},{4,5},{5,4},{6,7},{7,6},{8,9},{9,8},{10,11... | collective-permute-start | bytes 3145736 | tf_op jit(solution)/shard_map/ppermute | solution.py:219
  32.7 9.5 %collective-permute-start.8 = (f32[128,256]{1,0:T(8,128)S(1)}, f32[128,256]{1,0:T(8,128)S(1)}, u32[]{:S(2)}, u32[]{:S(2)}) collective-permute-start(f32[128,256]{1,0:T(8,128)S(1)} %get-tuple-element.321), channel_id=1, source_target_pairs={{0,6},{2,4},{4,10},{6,8},{8,14},{10,12},{12,2},{14,0},{1,7},{3,5},... | collective-permute-start | bytes 393224 | tf_op jit(solution)/shard_map/ppermute | solution.py:291
  34.8 10.3 %collective-permute-start.10 = (f32[128,256]{1,0:T(8,128)S(1)}, f32[128,256]{1,0:T(8,128)S(1)}, u32[]{:S(2)}, u32[]{:S(2)}) collective-permute-start(f32[128,256]{1,0:T(8,128)S(1)} %get-tuple-element.325), channel_id=1, source_target_pairs={{0,14},{2,12},{4,2},{6,0},{8,6},{10,4},{12,10},{14,8},{1,15},{3,13... | collective-permute-start | bytes 393224 | tf_op jit(solution)/shard_map/ppermute | solution.py:291
  36.9 9.4 %collective-permute-start.11 = (f32[128,256]{1,0:T(8,128)S(1)}, f32[128,256]{1,0:T(8,128)S(1)}, u32[]{:S(2)}, u32[]{:S(2)}) collective-permute-start(f32[128,256]{1,0:T(8,128)S(1)} %get-tuple-element.326), channel_id=1, source_target_pairs={{0,10},{2,8},{4,14},{6,12},{8,2},{10,0},{12,6},{14,4},{1,11},{3,9}... | collective-permute-start | bytes 393224 | tf_op jit(solution)/shard_map/ppermute | solution.py:291
  39.3 9.1 %collective-permute-start.12 = (f32[128,256]{1,0:T(8,128)S(1)}, f32[128,256]{1,0:T(8,128)S(1)}, u32[]{:S(2)}, u32[]{:S(2)}) collective-permute-start(f32[128,256]{1,0:T(8,128)S(1)} %get-tuple-element.327), channel_id=1, source_target_pairs={{0,8},{2,10},{4,12},{6,14},{8,0},{10,2},{12,4},{14,6},{1,9},{3,11}... | collective-permute-start | bytes 393224 | tf_op jit(solution)/shard_map/ppermute | solution.py:291
  40.8 8.1 %collective-permute-start.13 = (f32[128,256]{1,0:T(8,128)S(1)}, f32[128,256]{1,0:T(8,128)S(1)}, u32[]{:S(2)}, u32[]{:S(2)}) collective-permute-start(f32[128,256]{1,0:T(8,128)S(1)} %get-tuple-element.328), channel_id=1, source_target_pairs={{0,2},{2,0},{4,6},{6,4},{8,10},{10,8},{12,14},{14,12},{1,3},{3,1},... | collective-permute-start | bytes 393224 | tf_op jit(solution)/shard_map/ppermute | solution.py:291
  42.2 8.0 %collective-permute-start.14 = (f32[128,256]{1,0:T(8,128)S(1)}, f32[128,256]{1,0:T(8,128)S(1)}, u32[]{:S(2)}, u32[]{:S(2)}) collective-permute-start(f32[128,256]{1,0:T(8,128)S(1)} %get-tuple-element.329), channel_id=1, source_target_pairs={{0,4},{2,6},{4,8},{6,10},{8,12},{10,14},{12,0},{14,2},{1,5},{3,7},... | collective-permute-start | bytes 393224 | tf_op jit(solution)/shard_map/ppermute | solution.py:291
  45.0 5.4 %collective-permute-start.15 = (f32[128,256]{1,0:T(8,128)S(1)}, f32[128,256]{1,0:T(8,128)S(1)}, u32[]{:S(2)}, u32[]{:S(2)}) collective-permute-start(f32[128,256]{1,0:T(8,128)S(1)} %get-tuple-element.330), channel_id=1, source_target_pairs={{0,12},{2,14},{4,0},{6,2},{8,4},{10,6},{12,8},{14,10},{1,13},{3,15... | collective-permute-start | bytes 393224 | tf_op jit(solution)/shard_map/ppermute | solution.py:291
  46.2 4.4 %collective-permute-start.9 = (s32[128]{0:T(128)S(1)}, s32[128]{0:T(128)S(1)}, u32[]{:S(2)}, u32[]{:S(2)}) collective-permute-start(s32[128]{0:T(128)S(1)} %copy-done.2), channel_id=1, source_target_pairs={{0,1},{1,0},{2,3},{3,2},{4,5},{5,4},{6,7},{7,6},{8,9},{9,8},{10,11... | collective-permute-start | bytes 1544 | tf_op jit(solution)/shard_map/ppermute | solution.py:219
  50.5 2.2 %collective-permute-start.16 = (f32[128,256]{1,0:T(8,128)S(1)}, f32[128,256]{1,0:T(8,128)S(1)}, u32[]{:S(2)}, u32[]{:S(2)}) collective-permute-start(f32[128,256]{1,0:T(8,128)S(1)} %shard_map.70.own), channel_id=1, source_target_pairs={{0,1},{1,0},{2,3},{3,2},{4,5},{5,4},{6,7},{7,6},{8,9},{9,8},{10,11... | collective-permute-start | bytes 393224 | tf_op jit(solution)/shard_map/ppermute | solution.py:219
  54.5 24.7 %all-to-all-start.1 = ((f32[832,2,128]{2,1,0:T(2,128)}), f32[832,2,128]{2,1,0:T(2,128)S(1)}, u32[]{:S(2)}, u32[]{:S(2)}) async-start(f32[832,2,128]{2,1,0:T(2,128)} %shard_map.71), calls=%async_computation.1 | async-start | bytes 1703936 | tf_op jit(solution)/shard_map/all_to_all | solution.py:338
  79.9 0.7 copy-start

commit v6 on v5

--- a/solution.py
+++ b/solution.py
@@ -293,6 +293,32 @@
     partials = [send(part, move) for part, move in zip(parts[:-1], moves)] + [parts[-1]]
     partials[0], partner, core = lax.optimization_barrier((partials[0], partner, core))
 
+    sibling = swap(partner)
+    row = jnp.arange(row_count, dtype=jnp.int32)
+
+    def rank(wanted, others, others_first):
+        to, beside = wanted // row_count, others // row_count
+        earlier = (to[:, None] == to[None, :]) & (row[None, :] < row[:, None])
+        also = (to[:, None] == beside[None, :]) & others_first
+        return jnp.sum(earlier.astype(jnp.int32) + also.astype(jnp.int32), axis=1)
+
+    ranks = (rank(partner, sibling, core == 1), rank(sibling, partner, core == 0))
+    most = (jnp.maximum(jnp.max(ranks[0]), jnp.max(ranks[1])) + 1).reshape(1)
+    chip = partner // (row_count * core_size)
+    before = (chip[:, None] == chip[None, :]) & (partner[None, :] < partner[:, None])
+    take_rank = jnp.sum(before, axis=1, dtype=jnp.int32)
+    scale = vir_pair[None, :] - occ_pair[:, None]
+
+    def send_place(wanted, rank, turn):
+        to = wanted // row_count
+        inside = (rank // SLOTS == turn) & (to % core_size == core)
+        return to // core_size * STRIDE + jnp.where(inside, rank % SLOTS, SLOTS)
+
+    first = (send_place(partner, ranks[0], 0), send_place(sibling, ranks[1], 0), most)
+    take_first = chip * STRIDE + take_rank % SLOTS
+    partials[1], first, take_first, scale = lax.optimization_barrier(
+        (partials[1], first, take_first, scale)
+    )
     rows = pltpu.VMEM((row_count, width), jnp.float32)
     own = pl.pallas_call(
         sum_kernel,
@@ -303,38 +329,17 @@
     )(*partials)
     other = swap(own)
 
-    sibling = swap(partner)
-    row = jnp.arange(row_count, dtype=jnp.int32)
-
-    def rank(wanted, others, others_first):
-        to, beside = wanted // row_count, others // row_count
-        earlier = (to[:, None] == to[None, :]) & (row[None, :] < row[:, None])
-        also = (to[:, None] == beside[None, :]) & others_first
-        return jnp.sum(earlier.astype(jnp.int32) + also.astype(jnp.int32), axis=1)
-
-    ranks = (rank(partner, sibling, core == 1), rank(sibling, partner, core == 0))
-    most = (jnp.maximum(jnp.max(ranks[0]), jnp.max(ranks[1])) + 1).reshape(1)
-    chip = partner // (row_count * core_size)
-    before = (chip[:, None] == chip[None, :]) & (partner[None, :] < partner[:, None])
-    take_rank = jnp.sum(before, axis=1, dtype=jnp.int32)
-    scale = vir_pair[None, :] - occ_pair[:, None]
-
-    def send_place(wanted, rank, turn):
-        to = wanted // row_count
-        inside = (rank // SLOTS == turn) & (to % core_size == core)
-        return to // core_size * STRIDE + jnp.where(inside, rank % SLOTS, SLOTS)
-
     packed = pltpu.VMEM((device_count // core_size * STRIDE, 2, width // 2), jnp.float32)
     chips = ("zh", "x", "y", "zl")
 
-    def exchange(turn):
+    def exchange(places):
         outbox = pl.pallas_call(
             pack_kernel,
             in_specs=[SMEM, SMEM, SMEM, VMEM, VMEM],
             out_specs=VMEM,
             out_shape=packed,
             compiler_params=SMALL,
-        )(send_place(partner, ranks[0], turn), send_place(sibling, ranks[1], turn), most, own, other)
+        )(*places, own, other)
         return in_vmem(lax.all_to_all(outbox, chips, 0, 0, tiled=True))
 
     update, turns = pl.pallas_call(
@@ -344,13 +349,14 @@
         out_shape=[jax.ShapeDtypeStruct((row_count, width), jnp.float32), pltpu.SMEM((1,), jnp.int32)],
         scratch_shapes=[pltpu.VMEM((row_count, width), jnp.float32)],
         compiler_params=SMALL,
-    )(chip * STRIDE + take_rank % SLOTS, exchange(0), own, scale)
+    )(take_first, exchange(first), own, scale)
 
     def more(state):
         return state[0] < turns[0]
 
     def again(state):
         turn, so_far = state
+        to_places = (send_place(partner, ranks[0], turn), send_place(sibling, ranks[1], turn), most)
         place = jnp.where(take_rank // SLOTS == turn, chip * STRIDE + take_rank % SLOTS, -1)
         after = pl.pallas_call(
             mend_kernel,
@@ -358,7 +364,7 @@
             out_specs=VMEM,
             out_shape=jax.ShapeDtypeStruct((row_count, width), jnp.float32),
             compiler_params=SMALL,
-        )(place, exchange(turn), own, scale, so_far)
+        )(place, exchange(to_places), own, scale, so_far)
         return turn + 1, after
 
     return lax.while_loop(more, again, (jnp.int32(1), update))[1]

time: 80.8 us -> 79.9 us (0.989)
  waiting for transfers between devices: 23.7 us -> 21.9 us
  starting transfers between devices: 34.2 us -> 35.2 us
    ppermute x7, waiting for transfers between devices: 7.47 us -> 3.38 us  [send(): return in_vmem(lax.ppermute(part, ('y', 'zl'), pairs))]
    ppermute x3, waiting for transfers between devices: 0.24 us -> 2.47 us  [swap(): return lax.ppermute(array, 'c', [(0, 1), (1, 0)])]
    ppermute x7, starting transfers between devices: 10.3 us -> 11.2 us  [send(): return in_vmem(lax.ppermute(part, ('y', 'zl'), pairs))]
  transfers between devices with their start and end apart: 18 -> 18, of which waited for: 10 -> 9; matrix products, arithmetic and copies ran while one was open for 1% -> 1% of each run, Pallas kernels for 16% -> 16%
where the time goes in v6:
time: 79.9 us; the launch traced here: 79.7 us
  starting transfers between devices  35.2 us (44%)
  waiting for transfers between devices  21.9 us (27%)
  Pallas kernels  19.3 us (24%)
  between operations  1.5 us (2%)
  other arithmetic  1.13 us (1%)
    all_to_all x1, waiting for transfers between devices, exchange(): return in_vmem(lax.all_to_all(outbox, chips, 0, 0, tiled=True))  15.8 us
    pallas_call x5, Pallas kernels, call(): pl.pallas_call(kernel, in_specs=specs, out_specs=[VMEM] * len(results), o...  15.8 us
    ppermute x7, starting transfers between devices, send(): return in_vmem(lax.ppermute(part, ('y', 'zl'), pairs))  11.2 us
    all_to_all x1, starting transfers between devices, exchange(): return in_vmem(lax.all_to_all(outbox, chips, 0, 0, tiled=True))  8.7 us
    ppermute x4, starting transfers between devices, shift(): lax.ppermute(block, 'x', [(n, (n + by) % x_size) for n in range(x_size)])  7.15 us
    ppermute x2, starting transfers between devices, cross(): return lax.ppermute(block, 'zh', [(0, 1), (1, 0)])  6.64 us
    ppermute x7, waiting for transfers between devices, send(): return in_vmem(lax.ppermute(part, ('y', 'zl'), pairs))  3.38 us
    ppermute x3, waiting for transfers between devices, swap(): return lax.ppermute(array, 'c', [(0, 1), (1, 0)])  2.47 us
  transfers between devices with their start and end apart: 18, of which 9 were waited for; matrix products, arithmetic and copies ran while one was open for 1% of the time, Pallas kernels for 16%

profile of v6, /device:TPU:0, one launch (start us, length us, event | category | flops | bytes accessed | tf_op | source)
XLA Modules:
  0.0 79.7 jit_solution(7850371165781827470)
XLA Ops:
  0.0 1.0 %shard_map.64.block = f32[256,256]{1,0:T(8,128)S(1)} custom-call(s32[2,2]{1,0:T(2,128)} %mask.1, f32[2,128,256]{2,1,0:T(8,128)} %block.1), custom_call_target="tpu_custom_call" | custom-call | tf_op jit(solution)/shard_map/pallas_call | solution.py:199
  1.0 4.0 %collective-permute-start = (f32[256,256]{1,0:T(8,128)S(1)}, f32[256,256]{1,0:T(8,128)S(1)}, u32[]{:S(2)}, u32[]{:S(2)}) collective-permute-start(f32[256,256]{1,0:T(8,128)S(1)} %shard_map.64.block), channel_id=1, source_target_pairs={{0,64},{64,0},{1,65},{65,1},{2,66},{66,2},{3,67},{67,3},{4,68},{68... | collective-permute-start | bytes 786440 | tf_op jit(solution)/shard_map/ppermute | solution.py:216
  5.0 1.5 %collective-permute-start.1 = (f32[256,256]{1,0:T(8,128)S(1)}, f32[256,256]{1,0:T(8,128)S(1)}, u32[]{:S(2)}, u32[]{:S(2)}) collective-permute-start(f32[256,256]{1,0:T(8,128)S(1)} %shard_map.64.block), channel_id=1, source_target_pairs={{0,16},{16,32},{32,48},{48,0},{1,17},{17,33},{33,49},{49,1},{2,18}... | collective-permute-start | bytes 786440 | tf_op jit(solution)/shard_map/ppermute | solution.py:213
  6.5 1.7 %collective-permute-start.2 = (f32[256,256]{1,0:T(8,128)S(1)}, f32[256,256]{1,0:T(8,128)S(1)}, u32[]{:S(2)}, u32[]{:S(2)}) collective-permute-start(f32[256,256]{1,0:T(8,128)S(1)} %shard_map.64.block), channel_id=1, source_target_pairs={{0,48},{16,0},{32,16},{48,32},{1,49},{17,1},{33,17},{49,33},{2,50}... | collective-permute-start | bytes 786440 | tf_op jit(solution)/shard_map/ppermute | solution.py:213
  8.3 1.3 %collective-permute-start.6 = (f32[256,256]{1,0:T(8,128)S(1)}, f32[256,256]{1,0:T(8,128)S(1)}, u32[]{:S(2)}, u32[]{:S(2)}) collective-permute-start(f32[256,256]{1,0:T(8,128)S(1)} %shard_map.64.block), channel_id=1, source_target_pairs={{0,96},{16,112},{32,64},{48,80},{64,32},{80,48},{96,0},{112,16},{1... | collective-permute-start | bytes 786440 | tf_op jit(solution)/shard_map/ppermute | solution.py:242
  9.6 4.6 %shard_map.65 = (f32[8,2,128,1024]{3,2,1,0:T(8,128)S(1)}, f32[2,8,128,256]{3,2,1,0:T(8,128)S(1)}) custom-call(s32[16]{0:T(128)S(1)} %compare_select_fusion.28.places, f32[256,256]{1,0:T(8,128)S(1)} %shard_map.64.block, f32[8,2,128,2048]{3,2,1,0:T(8,128)} %bitcast.4), custom_call_target="tpu_custom_call" | custom-call | flops 805306368 | bytes 1048576 | tf_op jit(solution)/shard_map/pallas_call | solution.py:118
  14.2 0.0 collective-permute-done.across
  14.2 0.2 collective-permute-done.1.left
  14.5 1.3 %collective-permute-start.3 = (f32[256,256]{1,0:T(8,128)S(1)}, f32[256,256]{1,0:T(8,128)S(1)}, u32[]{:S(2)}, u32[]{:S(2)}) collective-permute-start(f32[256,256]{1,0:T(8,128)S(1)} %collective-permute-done.1.left), channel_id=1, source_target_pairs={{0,16},{16,32},{32,48},{48,0},{1,17},{17,33},{33,49},{49,1},{2,18}... | collective-permute-start | bytes 786440 | tf_op jit(solution)/shard_map/ppermute | solution.py:213
  15.8 2.6 %collective-permute-start.4 = (f32[256,256]{1,0:T(8,128)S(1)}, f32[256,256]{1,0:T(8,128)S(1)}, u32[]{:S(2)}, u32[]{:S(2)}) collective-permute-start(f32[256,256]{1,0:T(8,128)S(1)} %collective-permute-done.1.left), channel_id=1, source_target_pairs={{0,64},{64,0},{1,65},{65,1},{2,66},{66,2},{3,67},{67,3},{4,68},{68... | collective-permute-start | bytes 786440 | tf_op jit(solution)/shard_map/ppermute | solution.py:216
  18.4 2.6 %collective-permute-start.5 = (f32[256,256]{1,0:T(8,128)S(1)}, f32[256,256]{1,0:T(8,128)S(1)}, u32[]{:S(2)}, u32[]{:S(2)}) collective-permute-start(f32[256,256]{1,0:T(8,128)S(1)} %collective-permute-done.across), channel_id=1, source_target_pairs={{0,48},{16,0},{32,16},{48,32},{1,49},{17,1},{33,17},{49,33},{2,50}... | collective-permute-start | bytes 786440 | tf_op jit(solution)/shard_map/ppermute | solution.py:213
  21.0 5.7 %shard_map.66 = (f32[8,2,128,1024]{3,2,1,0:T(8,128)S(1)}, f32[2,8,128,256]{3,2,1,0:T(8,128)S(1)}) custom-call(s32[16]{0:T(128)S(1)} %compare_select_fusion.28.places, f32[8,2,128,1024]{3,2,1,0:T(8,128)S(1)} %get-tuple-element.320.here, f32[256,256]{1,0:T(8,128)S(1)} %collective-permute-done.1.left, ...), custom_call_target="tpu_custom_call", output_to_operand_aliasing={{1}: (5, {})} | custom-call | flops 2415919104 | bytes 1048576 | tf_op jit(solution)/shard_map/pallas_call | solution.py:118
  26.8 0.0 collective-permute-done.4.across_left
  26.8 2.4 %shard_map.68 = f32[8,128,256]{2,1,0:T(8,128)S(1)} custom-call(s32[16]{0:T(128)S(1)} %compare_select_fusion.28.places, f32[8,2,128,1024]{3,2,1,0:T(8,128)S(1)} %get-tuple-element.320.here, f32[8,2,128,1024]{3,2,1,0:T(8,128)S(1)} %get-tuple-element.325.there, f32[256,256]{1,0:T(8,128)S(1)} %collective-permute-done.3.far, ...), custom_call_target="tpu_custom_call" | custom-call | flops 1610612736 | bytes 1048576 | tf_op jit(solution)/shard_map/pallas_call | solution.py:118
  29.2 0.0 copy-start.2
  29.2 0.0 copy-start.3
  29.2 0.0 copy-start.1
  29.3 0.1 collective-permute-start.7
  29.3 2.4 %shard_map.67.left = f32[8,128,256]{2,1,0:T(8,128)S(1)} custom-call(s32[16]{0:T(128)S(1)} %compare_select_fusion.28.places, f32[8,2,128,1024]{3,2,1,0:T(8,128)S(1)} %get-tuple-element.320.here, f32[8,2,128,1024]{3,2,1,0:T(8,128)S(1)} %get-tuple-element.325.there, f32[256,256]{1,0:T(8,128)S(1)} %collective-permute-done.3.far, ...), custom_call_target="tpu_custom_call" | custom-call | flops 1610612736 | bytes 1048576 | tf_op jit(solution)/shard_map/pallas_call | solution.py:118
  31.8 0.2 collective-permute-done.7.right
  32.0 0.7 shard_map.69
  32.7 2.1 %collective-permute-start.9 = (f32[128,256]{1,0:T(8,128)S(1)}, f32[128,256]{1,0:T(8,128)S(1)}, u32[]{:S(2)}, u32[]{:S(2)}) collective-permute-start(f32[128,256]{1,0:T(8,128)S(1)} %get-tuple-element.328), channel_id=1, source_target_pairs={{0,6},{2,4},{4,10},{6,8},{8,14},{10,12},{12,2},{14,0},{1,7},{3,5},... | collective-permute-start | bytes 393224 | tf_op jit(solution)/shard_map/ppermute | solution.py:291
  34.8 0.1 broadcast_subtract_fusion.scale
  34.8 2.2 %collective-permute-start.8 = (f32[128,256]{1,0:T(8,128)S(1)}, f32[128,256]{1,0:T(8,128)S(1)}, u32[]{:S(2)}, u32[]{:S(2)}) collective-permute-start(f32[128,256]{1,0:T(8,128)S(1)} %get-tuple-element.327), channel_id=1, source_target_pairs={{0,14},{2,12},{4,2},{6,0},{8,6},{10,4},{12,10},{14,8},{1,15},{3,13... | collective-permute-start | bytes 393224 | tf_op jit(solution)/shard_map/ppermute | solution.py:291
  37.0 2.4 %collective-permute-start.11 = (f32[128,256]{1,0:T(8,128)S(1)}, f32[128,256]{1,0:T(8,128)S(1)}, u32[]{:S(2)}, u32[]{:S(2)}) collective-permute-start(f32[128,256]{1,0:T(8,128)S(1)} %get-tuple-element.337), channel_id=1, source_target_pairs={{0,10},{2,8},{4,14},{6,12},{8,2},{10,0},{12,6},{14,4},{1,11},{3,9}... | collective-permute-start | bytes 393224 | tf_op jit(solution)/shard_map/ppermute | solution.py:291
  39.5 1.5 %collective-permute-start.12 = (f32[128,256]{1,0:T(8,128)S(1)}, f32[128,256]{1,0:T(8,128)S(1)}, u32[]{:S(2)}, u32[]{:S(2)}) collective-permute-start(f32[128,256]{1,0:T(8,128)S(1)} %get-tuple-element.338), channel_id=1, source_target_pairs={{0,8},{2,10},{4,12},{6,14},{8,0},{10,2},{12,4},{14,6},{1,9},{3,11}... | collective-permute-start | bytes 393224 | tf_op jit(solution)/shard_map/ppermute | solution.py:291
  41.0 1.0 %collective-permute-start.13 = (f32[128,256]{1,0:T(8,128)S(1)}, f32[128,256]{1,0:T(8,128)S(1)}, u32[]{:S(2)}, u32[]{:S(2)}) collective-permute-start(f32[128,256]{1,0:T(8,128)S(1)} %get-tuple-element.339), channel_id=1, source_target_pairs={{0,2},{2,0},{4,6},{6,4},{8,10},{10,8},{12,14},{14,12},{1,3},{3,1},... | collective-permute-start | bytes 393224 | tf_op jit(solution)/shard_map/ppermute | solution.py:291
  42.0 0.0 collective-permute-done.9.refs_0_
  42.1 0.2 convert_reduce_fusion
  42.3 0.9 %collective-permute-done.10 = s32[128]{0:T(128)S(1)} collective-permute-done((s32[128]{0:T(128)S(1)}, s32[128]{0:T(128)S(1)}, u32[]{:S(2)}, u32[]{:S(2)}) %collective-permute-start.10) | collective-permute-done | bytes 544 | tf_op jit(solution)/shard_map/ppermute | solution.py:219
  43.2 0.3 collective-permute-start.14
  43.5 0.2 add_reduce_fusion
  43.7 1.4 %collective-permute-done.8.refs_1_ = f32[128,256]{1,0:T(8,128)S(1)} collective-permute-done((f32[128,256]{1,0:T(8,128)S(1)}, f32[128,256]{1,0:T(8,128)S(1)}, u32[]{:S(2)}, u32[]{:S(2)}) %collective-permute-start.8) | collective-permute-done | bytes 131104 | tf_op jit(solution)/shard_map/ppermute | solution.py:291
  45.1 1.6 %collective-permute-start.15 = (f32[128,256]{1,0:T(8,128)S(1)}, f32[128,256]{1,0:T(8,128)S(1)}, u32[]{:S(2)}, u32[]{:S(2)}) collective-permute-start(f32[128,256]{1,0:T(8,128)S(1)} %get-tuple-element.341), channel_id=1, source_target_pairs={{0,12},{2,14},{4,0},{6,2},{8,4},{10,6},{12,8},{14,10},{1,13},{3,15... | collective-permute-start | bytes 393224 | tf_op jit(solution)/shard_map/ppermute | solution.py:291
  46.7 0.6 fusion.4
  48.6 0.0 collective-permute-done.11.refs_2_
  48.7 0.3 collective-permute-done.13.refs_4_
  48.9 1.1 %collective-permute-done.14.refs_5_ = f32[128,256]{1,0:T(8,128)S(1)} collective-permute-done((f32[128,256]{1,0:T(8,128)S(1)}, f32[128,256]{1,0:T(8,128)S(1)}, u32[]{:S(2)}, u32[]{:S(2)}) %collective-permute-start.14) | collective-permute-done | bytes 131104 | tf_op jit(solution)/shard_map/ppermute | solution.py:291
  50.0 0.5 collective-permute-done.15.refs_6_
  50.6 0.1 shard_map.70.own
  50.6 0.1 collective-permute-start.16
  50.7 1.3 %collective-permute-done.16.other = f32[128,256]{1,0:T(8,128)S(1)} collective-permute-done((f32[128,256]{1,0:T(8,128)S(1)}, f32[128,256]{1,0:T(8,128)S(1)}, u32[]{:S(2)}, u32[]{:S(2)}) %collective-permute-start.16) | collective-permute-done | bytes 131104 | tf_op jit(solution)/shard_map/ppermute | solution.py:219
  52.0 1.7 %shard_map.71 = f32[832,2,128]{2,1,0:T(2,128)} custom-call(s32[128]{0:T(128)S(1)} %get-tuple-element.332.own_place, s32[128]{0:T(128)S(1)} %get-tuple-element.333.other_place, s32[1]{0:T(128)} %bitcast.2.most, f32[128,256]{1,0:T(8,128)S(1)} %shard_map.70.own, f32[128,256]{1,0:T(8,128)S(1)} %collective-permute-done.16.other), custom_call_target="tpu_custom_call" | custom-call | tf_op jit(solution)/shard_map/pallas_call | solution.py:336
  53.7 8.7 %all-to-all-start.1 = ((f32[832,2,128]{2,1,0:T(2,128)}), f32[832,2,128]{2,1,0:T(2,128)S(1)}, u32[]{:S(2)}, u32[]{:S(2)}) async-start(f32[832,2,128]{2,1,0:T(2,128)} %shard_map.71), calls=%async_computation.1 | async-start | bytes 1703936 | tf_op jit(solution)/shard_map/all_to_all | solution.py:343
  62.4 15.8 %all-to-all-done.1.got = f32[832,2,128]{2,1,0:T(2,128)S(1)} async-done(((f32[832,2,128]{2,1,0:T(2,128)}), f32[832,2,128]{2,1,0:T(2,128)S(1)}, u32[]{:S(2)}, u32[]{:S(2)}) %all-to-all-start.1) | async-done | bytes 852000 | tf_op jit(solution)/shard_map/all_to_all | solution.py:343
  78.3 0.7 shard_map.72
  79.0 0.0 copy-start
  79.0 0.6 copy-done
  (14 shorter events, 0.1 us)
Async XLA Ops:
  1.0 13.2 %collective-permute-start = (f32[256,256]{1,0:T(8,128)S(1)}, f32[256,256]{1,0:T(8,128)S(1)}, u32[]{:S(2)}, u32[]{:S(2)}) collective-permute-start(f32[256,256]{1,0:T(8,128)S(1)} %shard_map.64.block), channel_id=1, source_target_pairs={{0,64},{64,0},{1,65},{65,1},{2,66},{66,2},{3,67},{67,3},{4,68},{68... | collective-permute-start | bytes 786440 | tf_op jit(solution)/shard_map/ppermute | solution.py:216
  5.0 9.5 %collective-permute-start.1 = (f32[256,256]{1,0:T(8,128)S(1)}, f32[256,256]{1,0:T(8,128)S(1)}, u32[]{:S(2)}, u32[]{:S(2)}) collective-permute-start(f32[256,256]{1,0:T(8,128)S(1)} %shard_map.64.block), channel_id=1, source_target_pairs={{0,16},{16,32},{32,48},{48,0},{1,17},{17,33},{33,49},{49,1},{2,18}... | collective-permute-start | bytes 786440 | tf_op jit(solution)/shard_map/ppermute | solution.py:213
  6.5 14.5 %collective-permute-start.2 = (f32[256,256]{1,0:T(8,128)S(1)}, f32[256,256]{1,0:T(8,128)S(1)}, u32[]{:S(2)}, u32[]{:S(2)}) collective-permute-start(f32[256,256]{1,0:T(8,128)S(1)} %shard_map.64.block), channel_id=1, source_target_pairs={{0,48},{16,0},{32,16},{48,32},{1,49},{17,1},{33,17},{49,33},{2,50}... | collective-permute-start | bytes 786440 | tf_op jit(solution)/shard_map/ppermute | solution.py:213
  8.3 18.5 %collective-permute-start.6 = (f32[256,256]{1,0:T(8,128)S(1)}, f32[256,256]{1,0:T(8,128)S(1)}, u32[]{:S(2)}, u32[]{:S(2)}) collective-permute-start(f32[256,256]{1,0:T(8,128)S(1)} %shard_map.64.block), channel_id=1, source_target_pairs={{0,96},{16,112},{32,64},{48,80},{64,32},{80,48},{96,0},{112,16},{1... | collective-permute-start | bytes 786440 | tf_op jit(solution)/shard_map/ppermute | solution.py:242
  14.5 12.3 %collective-permute-start.3 = (f32[256,256]{1,0:T(8,128)S(1)}, f32[256,256]{1,0:T(8,128)S(1)}, u32[]{:S(2)}, u32[]{:S(2)}) collective-permute-start(f32[256,256]{1,0:T(8,128)S(1)} %collective-permute-done.1.left), channel_id=1, source_target_pairs={{0,16},{16,32},{32,48},{48,0},{1,17},{17,33},{33,49},{49,1},{2,18}... | collective-permute-start | bytes 786440 | tf_op jit(solution)/shard_map/ppermute | solution.py:213
  15.8 11.0 %collective-permute-start.4 = (f32[256,256]{1,0:T(8,128)S(1)}, f32[256,256]{1,0:T(8,128)S(1)}, u32[]{:S(2)}, u32[]{:S(2)}) collective-permute-start(f32[256,256]{1,0:T(8,128)S(1)} %collective-permute-done.1.left), channel_id=1, source_target_pairs={{0,64},{64,0},{1,65},{65,1},{2,66},{66,2},{3,67},{67,3},{4,68},{68... | collective-permute-start | bytes 786440 | tf_op jit(solution)/shard_map/ppermute | solution.py:216
  18.4 8.4 %collective-permute-start.5 = (f32[256,256]{1,0:T(8,128)S(1)}, f32[256,256]{1,0:T(8,128)S(1)}, u32[]{:S(2)}, u32[]{:S(2)}) collective-permute-start(f32[256,256]{1,0:T(8,128)S(1)} %collective-permute-done.across), channel_id=1, source_target_pairs={{0,48},{16,0},{32,16},{48,32},{1,49},{17,1},{33,17},{49,33},{2,50}... | collective-permute-start | bytes 786440 | tf_op jit(solution)/shard_map/ppermute | solution.py:213
  29.2 5.5 %copy-start.2 = (f32[256]{0:T(256)S(1)}, f32[256]{0:T(256)}, u32[]{:S(2)}) copy-start(f32[256]{0:T(256)} %param.13) | copy-start | bytes 3076
  29.2 5.5 %copy-start.3 = (f32[128]{0:T(128)S(1)}, f32[128]{0:T(128)}, u32[]{:S(2)}) copy-start(f32[128]{0:T(128)} %param.12) | copy-start | bytes 1540
  29.2 12.8 %copy-start.1 = (s32[128]{0:T(128)S(1)}, s32[128]{0:T(128)}, u32[]{:S(2)}) copy-start(s32[128]{0:T(128)} %param.11) | copy-start | bytes 1540
  29.3 2.7 %collective-permute-start.7 = (f32[8,128,256]{2,1,0:T(8,128)S(1)}, f32[8,128,256]{2,1,0:T(8,128)S(1)}, u32[]{:S(2)}, u32[]{:S(2)}) collective-permute-start(f32[8,128,256]{2,1,0:T(8,128)S(1)} %shard_map.68), channel_id=1, source_target_pairs={{0,1},{1,0},{2,3},{3,2},{4,5},{5,4},{6,7},{7,6},{8,9},{9,8},{10,11... | collective-permute-start | bytes 3145736 | tf_op jit(solution)/shard_map/ppermute | solution.py:219
  32.7 9.4 %collective-permute-start.9 = (f32[128,256]{1,0:T(8,128)S(1)}, f32[128,256]{1,0:T(8,128)S(1)}, u32[]{:S(2)}, u32[]{:S(2)}) collective-permute-start(f32[128,256]{1,0:T(8,128)S(1)} %get-tuple-element.328), channel_id=1, source_target_pairs={{0,6},{2,4},{4,10},{6,8},{8,14},{10,12},{12,2},{14,0},{1,7},{3,5},... | collective-permute-start | bytes 393224 | tf_op jit(solution)/shard_map/ppermute | solution.py:291
  34.8 10.3 %collective-permute-start.8 = (f32[128,256]{1,0:T(8,128)S(1)}, f32[128,256]{1,0:T(8,128)S(1)}, u32[]{:S(2)}, u32[]{:S(2)}) collective-permute-start(f32[128,256]{1,0:T(8,128)S(1)} %get-tuple-element.327), channel_id=1, source_target_pairs={{0,14},{2,12},{4,2},{6,0},{8,6},{10,4},{12,10},{14,8},{1,15},{3,13... | collective-permute-start | bytes 393224 | tf_op jit(solution)/shard_map/ppermute | solution.py:291
  37.0 11.6 %collective-permute-start.11 = (f32[128,256]{1,0:T(8,128)S(1)}, f32[128,256]{1,0:T(8,128)S(1)}, u32[]{:S(2)}, u32[]{:S(2)}) collective-permute-start(f32[128,256]{1,0:T(8,128)S(1)} %get-tuple-element.337), channel_id=1, source_target_pairs={{0,10},{2,8},{4,14},{6,12},{8,2},{10,0},{12,6},{14,4},{1,11},{3,9}... | collective-permute-start | bytes 393224 | tf_op jit(solution)/shard_map/ppermute | solution.py:291
  39.5 9.2 %collective-permute-start.12 = (f32[128,256]{1,0:T(8,128)S(1)}, f32[128,256]{1,0:T(8,128)S(1)}, u32[]{:S(2)}, u32[]{:S(2)}) collective-permute-start(f32[128,256]{1,0:T(8,128)S(1)} %get-tuple-element.338), channel_id=1, source_target_pairs={{0,8},{2,10},{4,12},{6,14},{8,0},{10,2},{12,4},{14,6},{1,9},{3,11}... | collective-permute-start | bytes 393224 | tf_op jit(solution)/shard_map/ppermute | solution.py:291
  41.0 7.9 %collective-permute-start.13 = (f32[128,256]{1,0:T(8,128)S(1)}, f32[128,256]{1,0:T(8,128)S(1)}, u32[]{:S(2)}, u32[]{:S(2)}) collective-permute-start(f32[128,256]{1,0:T(8,128)S(1)} %get-tuple-element.339), channel_id=1, source_target_pairs={{0,2},{2,0},{4,6},{6,4},{8,10},{10,8},{12,14},{14,12},{1,3},{3,1},... | collective-permute-start | bytes 393224 | tf_op jit(solution)/shard_map/ppermute | solution.py:291
  42.1 1.1 %collective-permute-start.10 = (s32[128]{0:T(128)S(1)}, s32[128]{0:T(128)S(1)}, u32[]{:S(2)}, u32[]{:S(2)}) collective-permute-start(s32[128]{0:T(128)S(1)} %copy-done.1), channel_id=1, source_target_pairs={{0,1},{1,0},{2,3},{3,2},{4,5},{5,4},{6,7},{7,6},{8,9},{9,8},{10,11... | collective-permute-start | bytes 1544 | tf_op jit(solution)/shard_map/ppermute | solution.py:219
  43.2 6.8 %collective-permute-start.14 = (f32[128,256]{1,0:T(8,128)S(1)}, f32[128,256]{1,0:T(8,128)S(1)}, u32[]{:S(2)}, u32[]{:S(2)}) collective-permute-start(f32[128,256]{1,0:T(8,128)S(1)} %get-tuple-element.340), channel_id=1, source_target_pairs={{0,4},{2,6},{4,8},{6,10},{8,12},{10,14},{12,0},{14,2},{1,5},{3,7},... | collective-permute-start | bytes 393224 | tf_op jit(solution)/shard_map/ppermute | solution.py:291
  45.1 5.4 %collective-permute-start.15 = (f32[128,256]{1,0:T(8,128)S(1)}, f32[128,256]{1,0:T(8,128)S(1)}, u32[]{:S(2)}, u32[]{:S(2)}) collective-permute-start(f32[128,256]{1,0:T(8,128)S(1)} %get-tuple-element.341), channel_id=1, source_target_pairs={{0,12},{2,14},{4,0},{6,2},{8,4},{10,6},{12,8},{14,10},{1,13},{3,15... | collective-permute-start | bytes 393224 | tf_op jit(solution)/shard_map/ppermute | solution.py:291
  50.6 1.4 %collective-permute-start.16 = (f32[128,256]{1,0:T(8,128)S(1)}, f32[128,256]{1,0:T(8,128)S(1)}, u32[]{:S(2)}, u32[]{:S(2)}) collective-permute-start(f32[128,256]{1,0:T(8,128)S(1)} %shard_map.70.own), channel_id=1, source_target_pairs={{0,1},{1,0},{2,3},{3,2},{4,5},{5,4},{6,7},{7,6},{8,9},{9,8},{10,11... | collective-permute-start | bytes 393224 | tf_op jit(solution)/shard_map/ppermute | solution.py:219
  53.7 24.5 %all-to-all-start.1 = ((f32[832,2,128]{2,1,0:T(2,128)}), f32[832,2,128]{2,1,0:T(2,128)S(1)}, u32[]{:S(2)}, u32[]{:S(2)}) async-start(f32[832,2,128]{2,1,0:T(2,128)} %shard_map.71), calls=%async_computation.1 | async-start | bytes 1703936 | tf_op jit(solution)/shard_map/all_to_all | solution.py:343
  79.0 0.7 copy-start

commit v7 on v6

--- a/solution.py
+++ b/solution.py
@@ -223,7 +223,7 @@
     left, right, opposite = (x + x_size - 1) % x_size, (x + 1) % x_size, (x + 2) % x_size
     where = [1 - core, core, zh, 1 - zh, x, left, right, opposite]
     y, zl = lax.axis_index("y"), lax.axis_index("zl")
-    moves = [(1, 1), (3, 1), (2, 1), (2, 0), (0, 1), (1, 0), (3, 0), (0, 0)]
+    moves = [(1, 1), (3, 1), (1, 0), (3, 0), (2, 1), (2, 0), (0, 1), (0, 0)]
     where += [(y + up) % y_size * zl_size + (zl + over) % zl_size for up, over in moves]
     slot = jnp.arange(len(where), dtype=jnp.int32)
     places = jnp.zeros((len(where),), jnp.int32)
@@ -234,7 +234,7 @@
     wide = amplitudes.shape[1] // z_size
     side = (chunks, core_size, row_count, wide)
     sums = (core_size, chunks, row_count, width)
-    loads = [pltpu.SemaphoreType.DMA((4,))]
+    loads = [pltpu.SemaphoreType.DMA((8,))]
     work = 6 * core_size * chunks * row_count * width * tiles * tile
 
     across, up1, down1 = cross(mine), shift(mine, 1), shift(mine, -1)

time: 79.9 us -> 80.1 us (level)
    all_to_all x1, starting transfers between devices: 8.7 us -> 7.82 us  [exchange(): return in_vmem(lax.all_to_all(outbox, chips, 0, 0, tiled=True))]
    ppermute x7, starting transfers between devices: 11.2 us -> 12 us  [send(): return in_vmem(lax.ppermute(part, ('y', 'zl'), pairs))]
  transfers between devices with their start and end apart: 18 -> 18, of which waited for: 9 -> 8; matrix products, arithmetic and copies ran while one was open for 1% -> 1% of each run, Pallas kernels for 16% -> 17%
where the time goes in v7:
time: 80.1 us; the launch traced here: 79.8 us
  starting transfers between devices  35.2 us (44%)
  waiting for transfers between devices  21.4 us (27%)
  Pallas kernels  19.9 us (25%)
  between operations  1.52 us (2%)
  other arithmetic  1.13 us (1%)
    pallas_call x5, Pallas kernels, call(): pl.pallas_call(kernel, in_specs=specs, out_specs=[VMEM] * len(results), o...  16.4 us
    all_to_all x1, waiting for transfers between devices, exchange(): return in_vmem(lax.all_to_all(outbox, chips, 0, 0, tiled=True))  15.8 us
    ppermute x7, starting transfers between devices, send(): return in_vmem(lax.ppermute(part, ('y', 'zl'), pairs))  12 us
    all_to_all x1, starting transfers between devices, exchange(): return in_vmem(lax.all_to_all(outbox, chips, 0, 0, tiled=True))  7.82 us
    ppermute x4, starting transfers between devices, shift(): lax.ppermute(block, 'x', [(n, (n + by) % x_size) for n in range(x_size)])  7.16 us
    ppermute x2, starting transfers between devices, cross(): return lax.ppermute(block, 'zh', [(0, 1), (1, 0)])  6.69 us
    ppermute x7, waiting for transfers between devices, send(): return in_vmem(lax.ppermute(part, ('y', 'zl'), pairs))  2.95 us
    ppermute x3, waiting for transfers between devices, swap(): return lax.ppermute(array, 'c', [(0, 1), (1, 0)])  2.48 us
  transfers between devices with their start and end apart: 18, of which 8 were waited for; matrix products, arithmetic and copies ran while one was open for 1% of the time, Pallas kernels for 17%

profile of v7, /device:TPU:0, one launch (start us, length us, event | category | flops | bytes accessed | tf_op | source)
XLA Modules:
  0.0 79.8 jit_solution(10292756005570410126)
XLA Ops:
  0.0 1.0 %shard_map.64.block = f32[256,256]{1,0:T(8,128)S(1)} custom-call(s32[2,2]{1,0:T(2,128)} %mask.1, f32[2,128,256]{2,1,0:T(8,128)} %block.1), custom_call_target="tpu_custom_call" | custom-call | tf_op jit(solution)/shard_map/pallas_call | solution.py:199
  1.0 4.0 %collective-permute-start = (f32[256,256]{1,0:T(8,128)S(1)}, f32[256,256]{1,0:T(8,128)S(1)}, u32[]{:S(2)}, u32[]{:S(2)}) collective-permute-start(f32[256,256]{1,0:T(8,128)S(1)} %shard_map.64.block), channel_id=1, source_target_pairs={{0,64},{64,0},{1,65},{65,1},{2,66},{66,2},{3,67},{67,3},{4,68},{68... | collective-permute-start | bytes 786440 | tf_op jit(solution)/shard_map/ppermute | solution.py:216
  5.0 1.5 %collective-permute-start.1 = (f32[256,256]{1,0:T(8,128)S(1)}, f32[256,256]{1,0:T(8,128)S(1)}, u32[]{:S(2)}, u32[]{:S(2)}) collective-permute-start(f32[256,256]{1,0:T(8,128)S(1)} %shard_map.64.block), channel_id=1, source_target_pairs={{0,16},{16,32},{32,48},{48,0},{1,17},{17,33},{33,49},{49,1},{2,18}... | collective-permute-start | bytes 786440 | tf_op jit(solution)/shard_map/ppermute | solution.py:213
  6.5 1.7 %collective-permute-start.2 = (f32[256,256]{1,0:T(8,128)S(1)}, f32[256,256]{1,0:T(8,128)S(1)}, u32[]{:S(2)}, u32[]{:S(2)}) collective-permute-start(f32[256,256]{1,0:T(8,128)S(1)} %shard_map.64.block), channel_id=1, source_target_pairs={{0,48},{16,0},{32,16},{48,32},{1,49},{17,1},{33,17},{49,33},{2,50}... | collective-permute-start | bytes 786440 | tf_op jit(solution)/shard_map/ppermute | solution.py:213
  8.3 1.3 %collective-permute-start.6 = (f32[256,256]{1,0:T(8,128)S(1)}, f32[256,256]{1,0:T(8,128)S(1)}, u32[]{:S(2)}, u32[]{:S(2)}) collective-permute-start(f32[256,256]{1,0:T(8,128)S(1)} %shard_map.64.block), channel_id=1, source_target_pairs={{0,96},{16,112},{32,64},{48,80},{64,32},{80,48},{96,0},{112,16},{1... | collective-permute-start | bytes 786440 | tf_op jit(solution)/shard_map/ppermute | solution.py:242
  9.6 4.7 %shard_map.65 = (f32[8,2,128,1024]{3,2,1,0:T(8,128)S(1)}, f32[2,8,128,256]{3,2,1,0:T(8,128)S(1)}) custom-call(s32[16]{0:T(128)S(1)} %compare_select_fusion.28.places, f32[256,256]{1,0:T(8,128)S(1)} %shard_map.64.block, f32[8,2,128,2048]{3,2,1,0:T(8,128)} %bitcast.4), custom_call_target="tpu_custom_call" | custom-call | flops 805306368 | bytes 1048576 | tf_op jit(solution)/shard_map/pallas_call | solution.py:118
  14.3 0.2 collective-permute-done.1.left
  14.5 1.3 %collective-permute-start.3 = (f32[256,256]{1,0:T(8,128)S(1)}, f32[256,256]{1,0:T(8,128)S(1)}, u32[]{:S(2)}, u32[]{:S(2)}) collective-permute-start(f32[256,256]{1,0:T(8,128)S(1)} %collective-permute-done.1.left), channel_id=1, source_target_pairs={{0,16},{16,32},{32,48},{48,0},{1,17},{17,33},{33,49},{49,1},{2,18}... | collective-permute-start | bytes 786440 | tf_op jit(solution)/shard_map/ppermute | solution.py:213
  15.8 2.7 %collective-permute-start.4 = (f32[256,256]{1,0:T(8,128)S(1)}, f32[256,256]{1,0:T(8,128)S(1)}, u32[]{:S(2)}, u32[]{:S(2)}) collective-permute-start(f32[256,256]{1,0:T(8,128)S(1)} %collective-permute-done.1.left), channel_id=1, source_target_pairs={{0,64},{64,0},{1,65},{65,1},{2,66},{66,2},{3,67},{67,3},{4,68},{68... | collective-permute-start | bytes 786440 | tf_op jit(solution)/shard_map/ppermute | solution.py:216
  18.4 2.7 %collective-permute-start.5 = (f32[256,256]{1,0:T(8,128)S(1)}, f32[256,256]{1,0:T(8,128)S(1)}, u32[]{:S(2)}, u32[]{:S(2)}) collective-permute-start(f32[256,256]{1,0:T(8,128)S(1)} %collective-permute-done.across), channel_id=1, source_target_pairs={{0,48},{16,0},{32,16},{48,32},{1,49},{17,1},{33,17},{49,33},{2,50}... | collective-permute-start | bytes 786440 | tf_op jit(solution)/shard_map/ppermute | solution.py:213
  21.1 0.0 collective-permute-done.2.right
  21.1 6.3 %shard_map.66 = (f32[8,2,128,1024]{3,2,1,0:T(8,128)S(1)}, f32[2,8,128,256]{3,2,1,0:T(8,128)S(1)}) custom-call(s32[16]{0:T(128)S(1)} %compare_select_fusion.28.places, f32[8,2,128,1024]{3,2,1,0:T(8,128)S(1)} %get-tuple-element.320.here, f32[256,256]{1,0:T(8,128)S(1)} %collective-permute-done.1.left, ...), custom_call_target="tpu_custom_call", output_to_operand_aliasing={{1}: (5, {})} | custom-call | flops 2415919104 | bytes 1048576 | tf_op jit(solution)/shard_map/pallas_call | solution.py:118
  27.3 0.0 collective-permute-done.6.across_far
  27.4 0.0 collective-permute-done.3.far
  27.4 0.0 collective-permute-done.5.across_right
  27.4 2.4 %shard_map.68 = f32[8,128,256]{2,1,0:T(8,128)S(1)} custom-call(s32[16]{0:T(128)S(1)} %compare_select_fusion.28.places, f32[8,2,128,1024]{3,2,1,0:T(8,128)S(1)} %get-tuple-element.320.here, f32[8,2,128,1024]{3,2,1,0:T(8,128)S(1)} %get-tuple-element.325.there, f32[256,256]{1,0:T(8,128)S(1)} %collective-permute-done.3.far, ...), custom_call_target="tpu_custom_call" | custom-call | flops 1610612736 | bytes 1048576 | tf_op jit(solution)/shard_map/pallas_call | solution.py:118
  29.8 0.0 copy-start.2
  29.8 0.0 copy-start.3
  29.8 0.0 copy-start.1
  29.8 0.1 collective-permute-start.7
  29.9 2.4 %shard_map.67.left = f32[8,128,256]{2,1,0:T(8,128)S(1)} custom-call(s32[16]{0:T(128)S(1)} %compare_select_fusion.28.places, f32[8,2,128,1024]{3,2,1,0:T(8,128)S(1)} %get-tuple-element.320.here, f32[8,2,128,1024]{3,2,1,0:T(8,128)S(1)} %get-tuple-element.325.there, f32[256,256]{1,0:T(8,128)S(1)} %collective-permute-done.3.far, ...), custom_call_target="tpu_custom_call" | custom-call | flops 1610612736 | bytes 1048576 | tf_op jit(solution)/shard_map/pallas_call | solution.py:118
  32.3 0.2 collective-permute-done.7.right
  32.6 0.7 shard_map.69
  33.2 2.1 %collective-permute-start.9 = (f32[128,256]{1,0:T(8,128)S(1)}, f32[128,256]{1,0:T(8,128)S(1)}, u32[]{:S(2)}, u32[]{:S(2)}) collective-permute-start(f32[128,256]{1,0:T(8,128)S(1)} %get-tuple-element.328), channel_id=1, source_target_pairs={{0,6},{2,4},{4,10},{6,8},{8,14},{10,12},{12,2},{14,0},{1,7},{3,5},... | collective-permute-start | bytes 393224 | tf_op jit(solution)/shard_map/ppermute | solution.py:291
  35.3 0.1 broadcast_subtract_fusion.scale
  35.4 2.2 %collective-permute-start.8 = (f32[128,256]{1,0:T(8,128)S(1)}, f32[128,256]{1,0:T(8,128)S(1)}, u32[]{:S(2)}, u32[]{:S(2)}) collective-permute-start(f32[128,256]{1,0:T(8,128)S(1)} %get-tuple-element.327), channel_id=1, source_target_pairs={{0,14},{2,12},{4,2},{6,0},{8,6},{10,4},{12,10},{14,8},{1,15},{3,13... | collective-permute-start | bytes 393224 | tf_op jit(solution)/shard_map/ppermute | solution.py:291
  37.6 0.4 collective-permute-start.11
  38.0 2.9 %collective-permute-start.12 = (f32[128,256]{1,0:T(8,128)S(1)}, f32[128,256]{1,0:T(8,128)S(1)}, u32[]{:S(2)}, u32[]{:S(2)}) collective-permute-start(f32[128,256]{1,0:T(8,128)S(1)} %get-tuple-element.338), channel_id=1, source_target_pairs={{0,12},{2,14},{4,0},{6,2},{8,4},{10,6},{12,8},{14,10},{1,13},{3,15... | collective-permute-start | bytes 393224 | tf_op jit(solution)/shard_map/ppermute | solution.py:291
  40.8 1.2 %collective-permute-start.13 = (f32[128,256]{1,0:T(8,128)S(1)}, f32[128,256]{1,0:T(8,128)S(1)}, u32[]{:S(2)}, u32[]{:S(2)}) collective-permute-start(f32[128,256]{1,0:T(8,128)S(1)} %get-tuple-element.339), channel_id=1, source_target_pairs={{0,10},{2,8},{4,14},{6,12},{8,2},{10,0},{12,6},{14,4},{1,11},{3,9}... | collective-permute-start | bytes 393224 | tf_op jit(solution)/shard_map/ppermute | solution.py:291
  42.1 0.6 collective-permute-done.9.refs_0_
  42.6 0.0 collective-permute-start.10
  42.6 0.2 convert_reduce_fusion
  42.9 0.9 %collective-permute-done.10 = s32[128]{0:T(128)S(1)} collective-permute-done((s32[128]{0:T(128)S(1)}, s32[128]{0:T(128)S(1)}, u32[]{:S(2)}, u32[]{:S(2)}) %collective-permute-start.10) | collective-permute-done | bytes 544 | tf_op jit(solution)/shard_map/ppermute | solution.py:219
  43.8 2.2 %collective-permute-start.14 = (f32[128,256]{1,0:T(8,128)S(1)}, f32[128,256]{1,0:T(8,128)S(1)}, u32[]{:S(2)}, u32[]{:S(2)}) collective-permute-start(f32[128,256]{1,0:T(8,128)S(1)} %get-tuple-element.340), channel_id=1, source_target_pairs={{0,8},{2,10},{4,12},{6,14},{8,0},{10,2},{12,4},{14,6},{1,9},{3,11}... | collective-permute-start | bytes 393224 | tf_op jit(solution)/shard_map/ppermute | solution.py:291
  46.0 0.2 add_reduce_fusion
  46.2 1.1 %collective-permute-start.15 = (f32[128,256]{1,0:T(8,128)S(1)}, f32[128,256]{1,0:T(8,128)S(1)}, u32[]{:S(2)}, u32[]{:S(2)}) collective-permute-start(f32[128,256]{1,0:T(8,128)S(1)} %get-tuple-element.341), channel_id=1, source_target_pairs={{0,2},{2,0},{4,6},{6,4},{8,10},{10,8},{12,14},{14,12},{1,3},{3,1},... | collective-permute-start | bytes 393224 | tf_op jit(solution)/shard_map/ppermute | solution.py:291
  47.2 0.6 fusion.4
  49.2 1.7 %collective-permute-done.14.refs_5_ = f32[128,256]{1,0:T(8,128)S(1)} collective-permute-done((f32[128,256]{1,0:T(8,128)S(1)}, f32[128,256]{1,0:T(8,128)S(1)}, u32[]{:S(2)}, u32[]{:S(2)}) %collective-permute-start.14) | collective-permute-done | bytes 131104 | tf_op jit(solution)/shard_map/ppermute | solution.py:291
  50.9 0.7 collective-permute-done.15.refs_6_
  51.6 0.1 shard_map.70.own
  51.6 0.1 collective-permute-start.16
  51.7 1.3 %collective-permute-done.16.other = f32[128,256]{1,0:T(8,128)S(1)} collective-permute-done((f32[128,256]{1,0:T(8,128)S(1)}, f32[128,256]{1,0:T(8,128)S(1)}, u32[]{:S(2)}, u32[]{:S(2)}) %collective-permute-start.16) | collective-permute-done | bytes 131104 | tf_op jit(solution)/shard_map/ppermute | solution.py:219
  53.0 1.7 %shard_map.71 = f32[832,2,128]{2,1,0:T(2,128)} custom-call(s32[128]{0:T(128)S(1)} %get-tuple-element.332.own_place, s32[128]{0:T(128)S(1)} %get-tuple-element.333.other_place, s32[1]{0:T(128)} %bitcast.2.most, f32[128,256]{1,0:T(8,128)S(1)} %shard_map.70.own, f32[128,256]{1,0:T(8,128)S(1)} %collective-permute-done.16.other), custom_call_target="tpu_custom_call" | custom-call | tf_op jit(solution)/shard_map/pallas_call | solution.py:336
  54.7 7.8 %all-to-all-start.1 = ((f32[832,2,128]{2,1,0:T(2,128)}), f32[832,2,128]{2,1,0:T(2,128)S(1)}, u32[]{:S(2)}, u32[]{:S(2)}) async-start(f32[832,2,128]{2,1,0:T(2,128)} %shard_map.71), calls=%async_computation.1 | async-start | bytes 1703936 | tf_op jit(solution)/shard_map/all_to_all | solution.py:343
  62.6 15.8 %all-to-all-done.1.got = f32[832,2,128]{2,1,0:T(2,128)S(1)} async-done(((f32[832,2,128]{2,1,0:T(2,128)}), f32[832,2,128]{2,1,0:T(2,128)S(1)}, u32[]{:S(2)}, u32[]{:S(2)}) %all-to-all-start.1) | async-done | bytes 852000 | tf_op jit(solution)/shard_map/all_to_all | solution.py:343
  78.4 0.7 shard_map.72
  79.2 0.0 copy-start
  79.2 0.6 copy-done
  (14 shorter events, 0.1 us)
Async XLA Ops:
  1.0 13.3 %collective-permute-start = (f32[256,256]{1,0:T(8,128)S(1)}, f32[256,256]{1,0:T(8,128)S(1)}, u32[]{:S(2)}, u32[]{:S(2)}) collective-permute-start(f32[256,256]{1,0:T(8,128)S(1)} %shard_map.64.block), channel_id=1, source_target_pairs={{0,64},{64,0},{1,65},{65,1},{2,66},{66,2},{3,67},{67,3},{4,68},{68... | collective-permute-start | bytes 786440 | tf_op jit(solution)/shard_map/ppermute | solution.py:216
  5.0 9.5 %collective-permute-start.1 = (f32[256,256]{1,0:T(8,128)S(1)}, f32[256,256]{1,0:T(8,128)S(1)}, u32[]{:S(2)}, u32[]{:S(2)}) collective-permute-start(f32[256,256]{1,0:T(8,128)S(1)} %shard_map.64.block), channel_id=1, source_target_pairs={{0,16},{16,32},{32,48},{48,0},{1,17},{17,33},{33,49},{49,1},{2,18}... | collective-permute-start | bytes 786440 | tf_op jit(solution)/shard_map/ppermute | solution.py:213
  6.5 14.5 %collective-permute-start.2 = (f32[256,256]{1,0:T(8,128)S(1)}, f32[256,256]{1,0:T(8,128)S(1)}, u32[]{:S(2)}, u32[]{:S(2)}) collective-permute-start(f32[256,256]{1,0:T(8,128)S(1)} %shard_map.64.block), channel_id=1, source_target_pairs={{0,48},{16,0},{32,16},{48,32},{1,49},{17,1},{33,17},{49,33},{2,50}... | collective-permute-start | bytes 786440 | tf_op jit(solution)/shard_map/ppermute | solution.py:213
  8.3 19.1 %collective-permute-start.6 = (f32[256,256]{1,0:T(8,128)S(1)}, f32[256,256]{1,0:T(8,128)S(1)}, u32[]{:S(2)}, u32[]{:S(2)}) collective-permute-start(f32[256,256]{1,0:T(8,128)S(1)} %shard_map.64.block), channel_id=1, source_target_pairs={{0,96},{16,112},{32,64},{48,80},{64,32},{80,48},{96,0},{112,16},{1... | collective-permute-start | bytes 786440 | tf_op jit(solution)/shard_map/ppermute | solution.py:242
  14.5 12.9 %collective-permute-start.3 = (f32[256,256]{1,0:T(8,128)S(1)}, f32[256,256]{1,0:T(8,128)S(1)}, u32[]{:S(2)}, u32[]{:S(2)}) collective-permute-start(f32[256,256]{1,0:T(8,128)S(1)} %collective-permute-done.1.left), channel_id=1, source_target_pairs={{0,16},{16,32},{32,48},{48,0},{1,17},{17,33},{33,49},{49,1},{2,18}... | collective-permute-start | bytes 786440 | tf_op jit(solution)/shard_map/ppermute | solution.py:213
  15.8 11.6 %collective-permute-start.4 = (f32[256,256]{1,0:T(8,128)S(1)}, f32[256,256]{1,0:T(8,128)S(1)}, u32[]{:S(2)}, u32[]{:S(2)}) collective-permute-start(f32[256,256]{1,0:T(8,128)S(1)} %collective-permute-done.1.left), channel_id=1, source_target_pairs={{0,64},{64,0},{1,65},{65,1},{2,66},{66,2},{3,67},{67,3},{4,68},{68... | collective-permute-start | bytes 786440 | tf_op jit(solution)/shard_map/ppermute | solution.py:216
  18.4 9.0 %collective-permute-start.5 = (f32[256,256]{1,0:T(8,128)S(1)}, f32[256,256]{1,0:T(8,128)S(1)}, u32[]{:S(2)}, u32[]{:S(2)}) collective-permute-start(f32[256,256]{1,0:T(8,128)S(1)} %collective-permute-done.across), channel_id=1, source_target_pairs={{0,48},{16,0},{32,16},{48,32},{1,49},{17,1},{33,17},{49,33},{2,50}... | collective-permute-start | bytes 786440 | tf_op jit(solution)/shard_map/ppermute | solution.py:213
  29.8 5.5 %copy-start.2 = (f32[256]{0:T(256)S(1)}, f32[256]{0:T(256)}, u32[]{:S(2)}) copy-start(f32[256]{0:T(256)} %param.13) | copy-start | bytes 3076
  29.8 5.5 %copy-start.3 = (f32[128]{0:T(128)S(1)}, f32[128]{0:T(128)}, u32[]{:S(2)}) copy-start(f32[128]{0:T(128)} %param.12) | copy-start | bytes 1540
  29.8 12.8 %copy-start.1 = (s32[128]{0:T(128)S(1)}, s32[128]{0:T(128)}, u32[]{:S(2)}) copy-start(s32[128]{0:T(128)} %param.11) | copy-start | bytes 1540
  29.8 2.7 %collective-permute-start.7 = (f32[8,128,256]{2,1,0:T(8,128)S(1)}, f32[8,128,256]{2,1,0:T(8,128)S(1)}, u32[]{:S(2)}, u32[]{:S(2)}) collective-permute-start(f32[8,128,256]{2,1,0:T(8,128)S(1)} %shard_map.68), channel_id=1, source_target_pairs={{0,1},{1,0},{2,3},{3,2},{4,5},{5,4},{6,7},{7,6},{8,9},{9,8},{10,11... | collective-permute-start | bytes 3145736 | tf_op jit(solution)/shard_map/ppermute | solution.py:219
  33.2 9.4 %collective-permute-start.9 = (f32[128,256]{1,0:T(8,128)S(1)}, f32[128,256]{1,0:T(8,128)S(1)}, u32[]{:S(2)}, u32[]{:S(2)}) collective-permute-start(f32[128,256]{1,0:T(8,128)S(1)} %get-tuple-element.328), channel_id=1, source_target_pairs={{0,6},{2,4},{4,10},{6,8},{8,14},{10,12},{12,2},{14,0},{1,7},{3,5},... | collective-permute-start | bytes 393224 | tf_op jit(solution)/shard_map/ppermute | solution.py:291
  35.4 10.7 %collective-permute-start.8 = (f32[128,256]{1,0:T(8,128)S(1)}, f32[128,256]{1,0:T(8,128)S(1)}, u32[]{:S(2)}, u32[]{:S(2)}) collective-permute-start(f32[128,256]{1,0:T(8,128)S(1)} %get-tuple-element.327), channel_id=1, source_target_pairs={{0,14},{2,12},{4,2},{6,0},{8,6},{10,4},{12,10},{14,8},{1,15},{3,13... | collective-permute-start | bytes 393224 | tf_op jit(solution)/shard_map/ppermute | solution.py:291
  37.6 11.6 %collective-permute-start.11 = (f32[128,256]{1,0:T(8,128)S(1)}, f32[128,256]{1,0:T(8,128)S(1)}, u32[]{:S(2)}, u32[]{:S(2)}) collective-permute-start(f32[128,256]{1,0:T(8,128)S(1)} %get-tuple-element.337), channel_id=1, source_target_pairs={{0,4},{2,6},{4,8},{6,10},{8,12},{10,14},{12,0},{14,2},{1,5},{3,7},... | collective-permute-start | bytes 393224 | tf_op jit(solution)/shard_map/ppermute | solution.py:291
  38.0 11.2 %collective-permute-start.12 = (f32[128,256]{1,0:T(8,128)S(1)}, f32[128,256]{1,0:T(8,128)S(1)}, u32[]{:S(2)}, u32[]{:S(2)}) collective-permute-start(f32[128,256]{1,0:T(8,128)S(1)} %get-tuple-element.338), channel_id=1, source_target_pairs={{0,12},{2,14},{4,0},{6,2},{8,4},{10,6},{12,8},{14,10},{1,13},{3,15... | collective-permute-start | bytes 393224 | tf_op jit(solution)/shard_map/ppermute | solution.py:291
  40.8 8.4 %collective-permute-start.13 = (f32[128,256]{1,0:T(8,128)S(1)}, f32[128,256]{1,0:T(8,128)S(1)}, u32[]{:S(2)}, u32[]{:S(2)}) collective-permute-start(f32[128,256]{1,0:T(8,128)S(1)} %get-tuple-element.339), channel_id=1, source_target_pairs={{0,10},{2,8},{4,14},{6,12},{8,2},{10,0},{12,6},{14,4},{1,11},{3,9}... | collective-permute-start | bytes 393224 | tf_op jit(solution)/shard_map/ppermute | solution.py:291
  42.6 1.1 %collective-permute-start.10 = (s32[128]{0:T(128)S(1)}, s32[128]{0:T(128)S(1)}, u32[]{:S(2)}, u32[]{:S(2)}) collective-permute-start(s32[128]{0:T(128)S(1)} %copy-done.1), channel_id=1, source_target_pairs={{0,1},{1,0},{2,3},{3,2},{4,5},{5,4},{6,7},{7,6},{8,9},{9,8},{10,11... | collective-permute-start | bytes 1544 | tf_op jit(solution)/shard_map/ppermute | solution.py:219
  43.8 7.1 %collective-permute-start.14 = (f32[128,256]{1,0:T(8,128)S(1)}, f32[128,256]{1,0:T(8,128)S(1)}, u32[]{:S(2)}, u32[]{:S(2)}) collective-permute-start(f32[128,256]{1,0:T(8,128)S(1)} %get-tuple-element.340), channel_id=1, source_target_pairs={{0,8},{2,10},{4,12},{6,14},{8,0},{10,2},{12,4},{14,6},{1,9},{3,11}... | collective-permute-start | bytes 393224 | tf_op jit(solution)/shard_map/ppermute | solution.py:291
  46.2 5.4 %collective-permute-start.15 = (f32[128,256]{1,0:T(8,128)S(1)}, f32[128,256]{1,0:T(8,128)S(1)}, u32[]{:S(2)}, u32[]{:S(2)}) collective-permute-start(f32[128,256]{1,0:T(8,128)S(1)} %get-tuple-element.341), channel_id=1, source_target_pairs={{0,2},{2,0},{4,6},{6,4},{8,10},{10,8},{12,14},{14,12},{1,3},{3,1},... | collective-permute-start | bytes 393224 | tf_op jit(solution)/shard_map/ppermute | solution.py:291
  51.6 1.4 %collective-permute-start.16 = (f32[128,256]{1,0:T(8,128)S(1)}, f32[128,256]{1,0:T(8,128)S(1)}, u32[]{:S(2)}, u32[]{:S(2)}) collective-permute-start(f32[128,256]{1,0:T(8,128)S(1)} %shard_map.70.own), channel_id=1, source_target_pairs={{0,1},{1,0},{2,3},{3,2},{4,5},{5,4},{6,7},{7,6},{8,9},{9,8},{10,11... | collective-permute-start | bytes 393224 | tf_op jit(solution)/shard_map/ppermute | solution.py:219
  54.7 23.6 %all-to-all-start.1 = ((f32[832,2,128]{2,1,0:T(2,128)}), f32[832,2,128]{2,1,0:T(2,128)S(1)}, u32[]{:S(2)}, u32[]{:S(2)}) async-start(f32[832,2,128]{2,1,0:T(2,128)} %shard_map.71), calls=%async_computation.1 | async-start | bytes 1703936 | tf_op jit(solution)/shard_map/all_to_all | solution.py:343
  79.2 0.7 copy-start
